TPU v7x, 32 devices: a whole 2x2x4 slice. The times are simulated.
32 devices in a mesh: pix: 8 (over z, x), ang: 4 (over y, core).
Axes of the slice: x: 2, y: 2, z: 4, core: 2. Of those that a mesh axis runs over, the one named last changes fastest.
Arguments:
- volume: float32 [256, 128, 128], P(('pix', 'ang')), may hold values from -6 to 6
- projector: float32 [5120, 128, 128], P(('pix', 'ang')), may hold values from -0.078125 to 0.078125
- tile_ids: int32 [5120], P(('pix', 'ang')), may hold values from 0 to 1023, as said below
- counts: int32 [128, 128, 128], P('ang'), may hold values from 64 to 4095
- ray_counts: int32 [4, 8], P('ang'), may hold values from 1 to 4, 20 in all within a row
Outputs:
- updated: float32 [256, 128, 128], P(('pix', 'ang'))
Inputs may be any that keep to these rules, and one draw needn't show every extreme that they name: `tile_ids`: within each device's aligned block of 160 entries the values are distinct; value v names ray block v // 32 and pixel tile v % 32 of that device. `ray_counts`: each row sums to 20; the largest entry of every row is 4.
All inputs are finite; a program needn't handle non-finite values.
Results may differ from a plain program's by a relative error of at most 0.0001.
Values sent between devices are 32-bit elements; how exact they have to be, the bound alone decides.
No kernel may reach another device: no remote copies, remote signals or barrier semaphores. Data moves between devices by JAX's collectives and lax.ppermute only.
A program may use at most 128 MiB of HBM per device.

v0:
```python
import functools

import jax
import jax.numpy as jnp
from jax import lax
from jax.experimental import pallas as pl
from jax.experimental.pallas import tpu as pltpu
from jax.sharding import PartitionSpec as P

blank_flux = 4096.0
step_size = 0.5
unroll = 8
chunk = 16
vmem_bytes = 40 * 1024 * 1024

smem = pl.BlockSpec(memory_space=pltpu.SMEM)
vmem = pl.BlockSpec(memory_space=pltpu.VMEM)
anywhere = pl.BlockSpec(memory_space=pl.ANY)
params = pltpu.CompilerParams(vmem_limit_bytes=vmem_bytes)
f32, bf16, i32 = jnp.float32, jnp.bfloat16, jnp.int32


def halves(value):
    high = value.astype(bf16)
    return high, (value - high.astype(f32)).astype(bf16)


def plan_kernel(own_tiles, pixel_tiles, live_total, ids, rays, place, counts, rank_of, col_of, tile_of, total, picked, slot_rank, sem):
    tile_count = ids.shape[0]
    ray_blocks = counts.shape[0]
    capacity = ray_blocks // rays.shape[1]
    piece = picked.shape[1]
    start = pl.multiple_of(place[0], piece)

    def slot(j, rank):
        live = lax.rem(j, capacity) < rays[0, lax.div(j, capacity)]
        slot_rank[j] = jnp.where(live, rank, -1)

        @pl.when(live)
        def _():
            pltpu.make_async_copy(counts.at[j, pl.ds(start, piece)], picked.at[rank], sem).start()

        return rank + live.astype(i32)

    lax.fori_loop(0, ray_blocks, slot, jnp.int32(0))

    def tile(t, n):
        value = ids[t]
        rank = slot_rank[lax.div(value, pixel_tiles)]
        col = lax.rem(value, pixel_tiles)
        owner = lax.div(col, own_tiles)
        rank_of[n] = rank
        col_of[n] = (owner ^ place[1]) * own_tiles + lax.rem(col, own_tiles)
        tile_of[n] = t
        return n + (rank >= 0).astype(i32)

    n = lax.fori_loop(0, tile_count, tile, jnp.int32(0))
    for extra in range(unroll):
        rank_of[n + extra] = live_total
        col_of[n + extra] = pixel_tiles
        tile_of[n + extra] = 0
    total[0] = n
    pltpu.make_async_copy(picked, picked, sem).wait()


def split_kernel(projector, out):
    step = min(chunk, projector.shape[0])
    width = projector.shape[2]

    def body(index, block):
        high, low = halves(block[...])
        rows = pl.ds(index[0] * step, step)
        out[rows, :, :width] = high
        out[rows, :, width:] = low

    pltpu.emit_pipeline(
        lambda block: body((pl.program_id(0),), block),
        grid=(projector.shape[0] // step,),
        in_specs=[pl.BlockSpec((step,) + projector.shape[1:], lambda i: (i, 0, 0))],
    )(projector)


def forward_kernel(angles, deep, rank_of, col_of, tile_of, total, place, split, *refs):
    tiles, outs, (packed, sums) = refs[:angles], refs[angles : angles + deep], refs[angles + deep :]
    own_tiles, half, width = tiles[0].shape
    piece = half // deep

    for a in range(angles):

        def fill(i, carry, a=a):
            for k in range(deep):
                rows = pl.ds(pl.multiple_of((place[2] ^ k) * piece, piece), piece)
                high, low = halves(tiles[a][i, rows, :])
                for side in range(2):
                    lanes = slice(side * width, (side + 1) * width)
                    packed[a * own_tiles + i, k * piece : (k + 1) * piece, lanes] = high
                    packed[a * own_tiles + i, half + k * piece : half + (k + 1) * piece, lanes] = low
            return carry

        lax.fori_loop(0, own_tiles, fill, 0)
    sums[...] = jnp.zeros_like(sums)

    def step(i, carry):
        products = []
        for u in range(unroll):
            j = i * unroll + u
            product = lax.dot_general(
                packed[col_of[j]], split[tile_of[j]], (((1,), (1,)), ((), ())), preferred_element_type=f32
            )
            products.append(product[:half] + product[half:])
        for u in range(unroll):
            sums[rank_of[i * unroll + u]] += products[u]
        return carry

    lax.fori_loop(0, lax.div(total[0] + unroll - 1, unroll), step, 0)
    for k in range(deep):
        out = outs[k]
        out[...] = sums[: out.shape[0], k * piece : (k + 1) * piece, :]


def backward_kernel(angles, deep, rank_of, col_of, tile_of, total, split, *refs):
    blocks, outs, (packed, sums) = refs[:deep], refs[deep : deep + angles], refs[deep + angles :]
    live, piece, width = blocks[0].shape
    half = piece * deep
    own_tiles = outs[0].shape[0]
    for k in range(deep):

        def fill(i, carry, k=k):
            high, low = halves(blocks[k][i])
            packed[i, k * piece : (k + 1) * piece, :] = high
            packed[i, half + k * piece : half + (k + 1) * piece, :] = low
            return carry

        lax.fori_loop(0, live, fill, 0)
    sums[...] = jnp.zeros_like(sums)

    def step(i, carry):
        products = []
        for u in range(unroll):
            j = i * unroll + u
            product = jnp.dot(packed[rank_of[j]], split[tile_of[j]], preferred_element_type=f32)
            product = product[:half] + product[half:]
            products.append(product[:, :width] + product[:, width:])
        for u in range(unroll):
            sums[col_of[i * unroll + u]] += products[u]
        return carry

    lax.fori_loop(0, lax.div(total[0] + unroll - 1, unroll), step, 0)
    for a in range(angles):
        outs[a][...] = sums[a * own_tiles : (a + 1) * own_tiles]


def add_kernel(left, right, out):
    out[...] = left[...] + right[...]


def residual_kernel(counts, *refs):
    *terms, out = refs
    summed = terms[0][...]
    for term in terms[1:]:
        summed = summed + term[...]
    measured = counts[...].astype(f32)
    out[...] = measured / blank_flux * (summed - jnp.log(blank_flux / measured))


def update_kernel(deep, place, volume, *refs):
    *terms, out = refs
    half = terms[0].shape[1]
    piece = half // deep
    per_half = len(terms) // 2
    for side in range(2):
        base = (place[3] ^ side) * half
        for k in range(deep):
            rows = pl.ds(pl.multiple_of(base + (place[2] ^ k) * piece, piece), piece)
            local = slice(k * piece, (k + 1) * piece)
            gradient = terms[side * per_half][:, local, :]
            for term in terms[side * per_half + 1 : (side + 1) * per_half]:
                gradient = gradient + term[:, local, :]
            out[:, rows, :] = volume[:, rows, :] - step_size * gradient


def call(kernel, out_shape, in_specs, scratch=(), out_specs=None):
    if out_specs is None:
        out_specs = jax.tree.map(lambda leaf: vmem, out_shape)
    return pl.pallas_call(
        kernel,
        out_shape=out_shape,
        in_specs=in_specs,
        out_specs=out_specs,
        scratch_shapes=list(scratch),
        compiler_params=params,
    )


def add(left, right):
    return call(add_kernel, jax.ShapeDtypeStruct(left.shape, f32), [vmem, vmem])(left, right)


def shards(volume, projector, tile_ids, counts, ray_counts):
    pix, ang = lax.axis_size("pix"), lax.axis_size("ang")
    own_tiles, slices, width = volume.shape
    ray_blocks = counts.shape[0]
    tile_count, rays, _ = projector.shape
    pixel_tiles = own_tiles * ang
    live = ray_blocks * 5 // 8
    deep = pix // 2
    half, piece = slices // 2, slices // pix
    me, angle = lax.axis_index("pix"), lax.axis_index("ang")
    side, depth = me % 2, me // 2
    place = jnp.stack([side * half + depth * piece, angle, depth, side]).astype(i32)

    across = lambda value, axis, flip: lax.ppermute(
        value, axis, [(d, d ^ flip) for d in range(lax.axis_size(axis))]
    )
    angle_bits = [1 << b for b in range(ang.bit_length() - 1)]

    def spread(value):
        held = {0: value}
        for bit in reversed(angle_bits):
            held.update({k ^ bit: across(part, "ang", bit) for k, part in list(held.items())})
        return [held[k] for k in range(ang)]

    far = lax.dynamic_slice_in_dim(volume, (1 - side) * half, half, 1)
    near = lax.dynamic_slice_in_dim(volume, side * half, half, 1)
    far_tiles = spread(far)
    near_tiles = spread(near)

    listed = jax.ShapeDtypeStruct((tile_count + unroll,), i32)
    rank_of, col_of, tile_of, total, picked = call(
        functools.partial(plan_kernel, own_tiles, pixel_tiles, live),
        (listed, listed, listed, jax.ShapeDtypeStruct((1,), i32), jax.ShapeDtypeStruct((live, piece, rays), i32)),
        [smem, smem, smem, anywhere],
        [pltpu.SMEM((ray_blocks,), i32), pltpu.SemaphoreType.DMA],
        (smem, smem, smem, smem, vmem),
    )(tile_ids, ray_counts, place, counts)
    lists = (rank_of, col_of, tile_of, total)

    split = call(split_kernel, pltpu.VMEM((tile_count, rays, 2 * width), bf16), [anywhere], (), vmem)(projector)

    def forward(tiles):
        return call(
            functools.partial(forward_kernel, ang, deep),
            (jax.ShapeDtypeStruct((live, piece, rays), f32),) * deep,
            [smem] * 5 + [vmem] * (1 + ang),
            [
                pltpu.VMEM((pixel_tiles + 1, 2 * half, 2 * width), bf16),
                pltpu.VMEM((live + 1, half, rays), f32),
            ],
        )(*lists, place, split, *tiles)

    def backward(blocks):
        return call(
            functools.partial(backward_kernel, ang, deep),
            (jax.ShapeDtypeStruct((own_tiles, half, width), f32),) * ang,
            [smem] * 4 + [vmem] * (1 + deep),
            [
                pltpu.VMEM((live + 1, 2 * half, rays), bf16),
                pltpu.VMEM((pixel_tiles + 1, half, width), f32),
            ],
        )(*lists, split, *blocks)

    far_parts = forward(far_tiles)
    order = list(range(deep - 1, -1, -1))
    crossed = {k: across(far_parts[k], "pix", 1) for k in order}
    near_parts = forward(near_tiles)
    arrived = [across(add(near_parts[k], crossed[k]), "pix", 2 * k) for k in order if k]
    own = call(
        residual_kernel, jax.ShapeDtypeStruct((live, piece, rays), f32), [vmem] * (3 + len(arrived))
    )(picked, near_parts[0], crossed[0], *arrived)

    near_blocks = [own] + [across(own, "pix", 2 * k) for k in range(1, deep)]
    far_blocks = [across(block, "pix", 1) for block in near_blocks]

    def gather(parts):
        parts = dict(enumerate(parts))
        for bit in angle_bits[:-1]:
            for k in [k for k in parts if k & bit]:
                moved = across(parts.pop(k), "ang", bit)
                parts[k ^ bit] = add(parts[k ^ bit], moved)
        last = angle_bits[-1]
        return [parts[0], across(parts[last], "ang", last)]

    terms = gather(backward(near_blocks)) + gather(backward(far_blocks))
    return call(
        functools.partial(update_kernel, deep), jax.ShapeDtypeStruct(volume.shape, f32), [smem] + [vmem] * 5
    )(place, volume, *terms)


def solution(mesh):
    placed = (
        P(("pix", "ang"), None, None),
        P(("pix", "ang"), None, None),
        P(("pix", "ang")),
        P("ang", None, None),
        P("ang", None),
    )
    return jax.shard_map(
        shards, mesh=mesh, in_specs=placed, out_specs=P(("pix", "ang"), None, None), check_vma=False
    )
```

profile of v0, /device:TPU:0, one launch (start us, length us, event | category | flops | bytes accessed | tf_op | source)
XLA Modules:
  0.0 102.5 jit_solution(9822322948751446678)
XLA Ops:
  1.1 3.0 %collective-permute-start.4 = (f32[8,64,128]{2,1,0:T(8,128)S(1)}, f32[8,64,128]{2,1,0:T(8,128)S(1)}, u32[]{:S(2)}, u32[]{:S(2)}) collective-permute-start(f32[8,64,128]{2,1,0:T(8,128)S(1)} %get-tuple-element.47.refs_0_), channel_id=1, source_target_pairs={{0,2},{1,3},{2,0},{3,1},{4,6},{5,7},{6,4},{7,5},{8,10},{9,11},{10,... | collective-permute-start | bytes 786440 | tf_op jit(solution)/shard_map/ppermute | solution.py:212
  4.2 7.1 %collective-permute-done.4.refs_2_ = f32[8,64,128]{2,1,0:T(8,128)S(1)} collective-permute-done((f32[8,64,128]{2,1,0:T(8,128)S(1)}, f32[8,64,128]{2,1,0:T(8,128)S(1)}, u32[]{:S(2)}, u32[]{:S(2)}) %collective-permute-start.4) | collective-permute-done | bytes 262176 | tf_op jit(solution)/shard_map/ppermute | solution.py:212
  11.8 7.8 %shard_map.56.split = bf16[160,128,256]{2,1,0:T(8,128)(2,1)S(1)} custom-call(f32[160,128,128]{2,1,0:T(8,128)} %projector.1), custom_call_target="tpu_custom_call" | custom-call | tf_op jit(solution)/shard_map/pallas_call | solution.py:238
  19.8 4.2 %shard_map.55 = (s32[168]{0:T(256)S(1)}, s32[168]{0:T(256)S(1)}, s32[168]{0:T(256)S(1)}, s32[1]{0:T(128)}, s32[20,16,128]{2,1,0:T(8,128)S(1)}) custom-call(s32[160]{0:T(256)S(1)} %copy-done.2, s32[1,8]{1,0:T(1,128)S(1)} %copy-done.3, s32[4]{0:T(128)S(1)} %pad_add_fusion.place, s32[32,128,128]{2,1,0:T(8,128)S(1)} %copy-done.1), custom_call_target="tpu_custom_call" | custom-call | tf_op jit(solution)/shard_map/pallas_call | solution.py:229
  24.0 5.4 %shard_map.58 = (f32[20,16,128]{2,1,0:T(8,128)S(1)}, f32[20,16,128]{2,1,0:T(8,128)S(1)}, f32[20,16,128]{2,1,0:T(8,128)S(1)}, f32[20,16,128]{2,1,0:T(8,128)S(1)}) custom-call(s32[168]{0:T(256)S(1)} %get-tuple-element.26.rank_of, s32[168]{0:T(256)S(1)} %get-tuple-element.27.col_of, s32[168]{0:T(256)S(1)} %get-tuple-element.28.tile_of, ...), custom_call_target="tpu_custom_call" | custom-call | tf_op jit(solution)/shard_map/pallas_call | solution.py:241
  29.4 2.4 %collective-permute-start.7 = (f32[20,16,128]{2,1,0:T(8,128)S(1)}, f32[20,16,128]{2,1,0:T(8,128)S(1)}, u32[]{:S(2)}, u32[]{:S(2)}) collective-permute-start(f32[20,16,128]{2,1,0:T(8,128)S(1)} %get-tuple-element.34), channel_id=1, source_target_pairs={{0,4},{4,0},{8,12},{12,8},{16,20},{20,16},{24,28},{28,24},{1,5},{5... | collective-permute-start | bytes 491528 | tf_op jit(solution)/shard_map/ppermute | solution.py:212
  31.9 1.9 %collective-permute-start.11 = (f32[20,16,128]{2,1,0:T(8,128)S(1)}, f32[20,16,128]{2,1,0:T(8,128)S(1)}, u32[]{:S(2)}, u32[]{:S(2)}) collective-permute-start(f32[20,16,128]{2,1,0:T(8,128)S(1)} %get-tuple-element.38), channel_id=1, source_target_pairs={{0,4},{4,0},{8,12},{12,8},{16,20},{20,16},{24,28},{28,24},{1,5},{5... | collective-permute-start | bytes 491528 | tf_op jit(solution)/shard_map/ppermute | solution.py:212
  33.9 5.4 %shard_map.57 = (f32[20,16,128]{2,1,0:T(8,128)S(1)}, f32[20,16,128]{2,1,0:T(8,128)S(1)}, f32[20,16,128]{2,1,0:T(8,128)S(1)}, f32[20,16,128]{2,1,0:T(8,128)S(1)}) custom-call(s32[168]{0:T(256)S(1)} %get-tuple-element.26.rank_of, s32[168]{0:T(256)S(1)} %get-tuple-element.27.col_of, s32[168]{0:T(256)S(1)} %get-tuple-element.28.tile_of, ...), custom_call_target="tpu_custom_call" | custom-call | tf_op jit(solution)/shard_map/pallas_call | solution.py:241
  39.4 4.4 %collective-permute-start.8 = (f32[20,16,128]{2,1,0:T(8,128)S(1)}, f32[20,16,128]{2,1,0:T(8,128)S(1)}, u32[]{:S(2)}, u32[]{:S(2)}) collective-permute-start(f32[20,16,128]{2,1,0:T(8,128)S(1)} %shard_map.59), channel_id=1, source_target_pairs={{0,24},{4,28},{8,16},{12,20},{16,8},{20,12},{24,0},{28,4},{1,25},{... | collective-permute-start | bytes 491528 | tf_op jit(solution)/shard_map/ppermute | solution.py:212
  44.0 1.5 %collective-permute-start.12 = (f32[20,16,128]{2,1,0:T(8,128)S(1)}, f32[20,16,128]{2,1,0:T(8,128)S(1)}, u32[]{:S(2)}, u32[]{:S(2)}) collective-permute-start(f32[20,16,128]{2,1,0:T(8,128)S(1)} %shard_map.61), channel_id=1, source_target_pairs={{0,8},{4,12},{8,0},{12,4},{16,24},{20,28},{24,16},{28,20},{1,9},{5... | collective-permute-start | bytes 491528 | tf_op jit(solution)/shard_map/ppermute | solution.py:212
  45.5 1.4 %collective-permute-done.6.refs_1_ = f32[20,16,128]{2,1,0:T(8,128)S(1)} collective-permute-done((f32[20,16,128]{2,1,0:T(8,128)S(1)}, f32[20,16,128]{2,1,0:T(8,128)S(1)}, u32[]{:S(2)}, u32[]{:S(2)}) %collective-permute-start.6) | collective-permute-done | bytes 163872 | tf_op jit(solution)/shard_map/ppermute | solution.py:212
  46.9 2.0 %collective-permute-done.8.refs_2_ = f32[20,16,128]{2,1,0:T(8,128)S(1)} collective-permute-done((f32[20,16,128]{2,1,0:T(8,128)S(1)}, f32[20,16,128]{2,1,0:T(8,128)S(1)}, u32[]{:S(2)}, u32[]{:S(2)}) %collective-permute-start.8) | collective-permute-done | bytes 163872 | tf_op jit(solution)/shard_map/ppermute | solution.py:212
  49.0 8.3 %collective-permute-done.10.refs_3_ = f32[20,16,128]{2,1,0:T(8,128)S(1)} collective-permute-done((f32[20,16,128]{2,1,0:T(8,128)S(1)}, f32[20,16,128]{2,1,0:T(8,128)S(1)}, u32[]{:S(2)}, u32[]{:S(2)}) %collective-permute-start.10) | collective-permute-done | bytes 163872 | tf_op jit(solution)/shard_map/ppermute | solution.py:212
  57.5 3.0 %collective-permute-start.14 = (f32[20,16,128]{2,1,0:T(8,128)S(1)}, f32[20,16,128]{2,1,0:T(8,128)S(1)}, u32[]{:S(2)}, u32[]{:S(2)}) collective-permute-start(f32[20,16,128]{2,1,0:T(8,128)S(1)} %shard_map.62.refs_0_), channel_id=1, source_target_pairs={{0,16},{4,20},{8,24},{12,28},{16,0},{20,4},{24,8},{28,12},{1,17},{... | collective-permute-start | bytes 491528 | tf_op jit(solution)/shard_map/ppermute | solution.py:212
  60.5 1.4 %collective-permute-start.15 = (f32[20,16,128]{2,1,0:T(8,128)S(1)}, f32[20,16,128]{2,1,0:T(8,128)S(1)}, u32[]{:S(2)}, u32[]{:S(2)}) collective-permute-start(f32[20,16,128]{2,1,0:T(8,128)S(1)} %shard_map.62.refs_0_), channel_id=1, source_target_pairs={{0,24},{4,28},{8,16},{12,20},{16,8},{20,12},{24,0},{28,4},{1,25},{... | collective-permute-start | bytes 491528 | tf_op jit(solution)/shard_map/ppermute | solution.py:212
  63.2 2.4 %collective-permute-done.13.refs_1_ = f32[20,16,128]{2,1,0:T(8,128)S(1)} collective-permute-done((f32[20,16,128]{2,1,0:T(8,128)S(1)}, f32[20,16,128]{2,1,0:T(8,128)S(1)}, u32[]{:S(2)}, u32[]{:S(2)}) %collective-permute-start.13) | collective-permute-done | bytes 163872 | tf_op jit(solution)/shard_map/ppermute | solution.py:212
  66.2 5.8 %collective-permute-done.14.refs_2_ = f32[20,16,128]{2,1,0:T(8,128)S(1)} collective-permute-done((f32[20,16,128]{2,1,0:T(8,128)S(1)}, f32[20,16,128]{2,1,0:T(8,128)S(1)}, u32[]{:S(2)}, u32[]{:S(2)}) %collective-permute-start.14) | collective-permute-done | bytes 163872 | tf_op jit(solution)/shard_map/ppermute | solution.py:212
  72.1 1.9 %collective-permute-start.21 = (f32[20,16,128]{2,1,0:T(8,128)S(1)}, f32[20,16,128]{2,1,0:T(8,128)S(1)}, u32[]{:S(2)}, u32[]{:S(2)}) collective-permute-start(f32[20,16,128]{2,1,0:T(8,128)S(1)} %collective-permute-done.14.refs_2_), channel_id=1, source_target_pairs={{0,4},{4,0},{8,12},{12,8},{16,20},{20,16},{24,28},{28,24},{1,5},{5... | collective-permute-start | bytes 491528 | tf_op jit(solution)/shard_map/ppermute | solution.py:212
  74.1 5.5 %shard_map.63 = (f32[8,64,128]{2,1,0:T(8,128)S(1)}, f32[8,64,128]{2,1,0:T(8,128)S(1)}, f32[8,64,128]{2,1,0:T(8,128)S(1)}, f32[8,64,128]{2,1,0:T(8,128)S(1)}) custom-call(s32[168]{0:T(256)S(1)} %get-tuple-element.26.rank_of, s32[168]{0:T(256)S(1)} %get-tuple-element.27.col_of, s32[168]{0:T(256)S(1)} %get-tuple-element.28.tile_of, s32[1]{0:T(128)} %get-tuple-element.29.total, ...), custom_call_target="tpu_custom_call" | custom-call | tf_op jit(solution)/shard_map/pallas_call | solution.py:252
  79.7 5.5 %shard_map.66 = (f32[8,64,128]{2,1,0:T(8,128)S(1)}, f32[8,64,128]{2,1,0:T(8,128)S(1)}, f32[8,64,128]{2,1,0:T(8,128)S(1)}, f32[8,64,128]{2,1,0:T(8,128)S(1)}) custom-call(s32[168]{0:T(256)S(1)} %get-tuple-element.26.rank_of, s32[168]{0:T(256)S(1)} %get-tuple-element.27.col_of, s32[168]{0:T(256)S(1)} %get-tuple-element.28.tile_of, s32[1]{0:T(128)} %get-tuple-element.29.total, ...), custom_call_target="tpu_custom_call" | custom-call | tf_op jit(solution)/shard_map/pallas_call | solution.py:252
  86.6 2.3 %collective-permute-start.18 = (f32[8,64,128]{2,1,0:T(8,128)S(1)}, f32[8,64,128]{2,1,0:T(8,128)S(1)}, u32[]{:S(2)}, u32[]{:S(2)}) collective-permute-start(f32[8,64,128]{2,1,0:T(8,128)S(1)} %shard_map.65), channel_id=1, source_target_pairs={{0,2},{1,3},{2,0},{3,1},{4,6},{5,7},{6,4},{7,5},{8,10},{9,11},{10,... | collective-permute-start | bytes 786440 | tf_op jit(solution)/shard_map/ppermute | solution.py:212
  89.6 6.3 %collective-permute-done.18.refs_1_ = f32[8,64,128]{2,1,0:T(8,128)S(1)} collective-permute-done((f32[8,64,128]{2,1,0:T(8,128)S(1)}, f32[8,64,128]{2,1,0:T(8,128)S(1)}, u32[]{:S(2)}, u32[]{:S(2)}) %collective-permute-start.18) | collective-permute-done | bytes 262176 | tf_op jit(solution)/shard_map/ppermute | solution.py:212
  95.9 5.1 %collective-permute-done.25.refs_3_ = f32[8,64,128]{2,1,0:T(8,128)S(1)} collective-permute-done((f32[8,64,128]{2,1,0:T(8,128)S(1)}, f32[8,64,128]{2,1,0:T(8,128)S(1)}, u32[]{:S(2)}, u32[]{:S(2)}) %collective-permute-start.25) | collective-permute-done | bytes 262176 | tf_op jit(solution)/shard_map/ppermute | solution.py:212
  101.0 1.4 %shard_map.69 = f32[8,128,128]{2,1,0:T(8,128)} custom-call(s32[4]{0:T(128)S(1)} %pad_add_fusion.place, f32[8,128,128]{2,1,0:T(8,128)S(1)} %copy-done, f32[8,64,128]{2,1,0:T(8,128)S(1)} %shard_map.64.refs_0_, f32[8,64,128]{2,1,0:T(8,128)S(1)} %collective-permute-done.18.refs_1_, f32[8,64,128]{2,1,0:T(8,128)S(1)} %shard_map.67.refs_2_, ...), custom_call_target="tpu_custom_call" | custom-call | tf_op jit(solution)/shard_map/pallas_call | solution.py:284
  (53 shorter events, 6.5 us)
Async XLA Ops:
  1.1 10.2 %collective-permute-start.4 = (f32[8,64,128]{2,1,0:T(8,128)S(1)}, f32[8,64,128]{2,1,0:T(8,128)S(1)}, u32[]{:S(2)}, u32[]{:S(2)}) collective-permute-start(f32[8,64,128]{2,1,0:T(8,128)S(1)} %get-tuple-element.47.refs_0_), channel_id=1, source_target_pairs={{0,2},{1,3},{2,0},{3,1},{4,6},{5,7},{6,4},{7,5},{8,10},{9,11},{10,... | collective-permute-start | bytes 786440 | tf_op jit(solution)/shard_map/ppermute | solution.py:212
  4.1 15.5 %collective-permute-start.1 = (f32[8,64,128]{2,1,0:T(8,128)S(1)}, f32[8,64,128]{2,1,0:T(8,128)S(1)}, u32[]{:S(2)}, u32[]{:S(2)}) collective-permute-start(f32[8,64,128]{2,1,0:T(8,128)S(1)} %get-tuple-element.48.refs_0_), channel_id=1, source_target_pairs={{0,2},{1,3},{2,0},{3,1},{4,6},{5,7},{6,4},{7,5},{8,10},{9,11},{10,... | collective-permute-start | bytes 786440 | tf_op jit(solution)/shard_map/ppermute | solution.py:212
  4.2 19.8 %collective-permute-start.3 = (f32[8,64,128]{2,1,0:T(8,128)S(1)}, f32[8,64,128]{2,1,0:T(8,128)S(1)}, u32[]{:S(2)}, u32[]{:S(2)}) collective-permute-start(f32[8,64,128]{2,1,0:T(8,128)S(1)} %get-tuple-element.47.refs_0_), channel_id=1, source_target_pairs={{0,1},{1,0},{2,3},{3,2},{4,5},{5,4},{6,7},{7,6},{8,9},{9,8},{10,11... | collective-permute-start | bytes 786440 | tf_op jit(solution)/shard_map/ppermute | solution.py:212
  11.2 12.7 %collective-permute-start.5 = (f32[8,64,128]{2,1,0:T(8,128)S(1)}, f32[8,64,128]{2,1,0:T(8,128)S(1)}, u32[]{:S(2)}, u32[]{:S(2)}) collective-permute-start(f32[8,64,128]{2,1,0:T(8,128)S(1)} %collective-permute-done.4.refs_2_), channel_id=1, source_target_pairs={{0,1},{1,0},{2,3},{3,2},{4,5},{5,4},{6,7},{7,6},{8,9},{9,8},{10,11... | collective-permute-start | bytes 786440 | tf_op jit(solution)/shard_map/ppermute | solution.py:212
  11.2 22.6 %collective-permute-start = (f32[8,64,128]{2,1,0:T(8,128)S(1)}, f32[8,64,128]{2,1,0:T(8,128)S(1)}, u32[]{:S(2)}, u32[]{:S(2)}) collective-permute-start(f32[8,64,128]{2,1,0:T(8,128)S(1)} %get-tuple-element.48.refs_0_), channel_id=1, source_target_pairs={{0,1},{1,0},{2,3},{3,2},{4,5},{5,4},{6,7},{7,6},{8,9},{9,8},{10,11... | collective-permute-start | bytes 786440 | tf_op jit(solution)/shard_map/ppermute | solution.py:212
  19.6 14.3 %collective-permute-start.2 = (f32[8,64,128]{2,1,0:T(8,128)S(1)}, f32[8,64,128]{2,1,0:T(8,128)S(1)}, u32[]{:S(2)}, u32[]{:S(2)}) collective-permute-start(f32[8,64,128]{2,1,0:T(8,128)S(1)} %collective-permute-done.1.refs_2_), channel_id=1, source_target_pairs={{0,1},{1,0},{2,3},{3,2},{4,5},{5,4},{6,7},{7,6},{8,9},{9,8},{10,11... | collective-permute-start | bytes 786440 | tf_op jit(solution)/shard_map/ppermute | solution.py:212
  29.4 10.0 %collective-permute-start.7 = (f32[20,16,128]{2,1,0:T(8,128)S(1)}, f32[20,16,128]{2,1,0:T(8,128)S(1)}, u32[]{:S(2)}, u32[]{:S(2)}) collective-permute-start(f32[20,16,128]{2,1,0:T(8,128)S(1)} %get-tuple-element.34), channel_id=1, source_target_pairs={{0,4},{4,0},{8,12},{12,8},{16,20},{20,16},{24,28},{28,24},{1,5},{5... | collective-permute-start | bytes 491528 | tf_op jit(solution)/shard_map/ppermute | solution.py:212
  31.8 12.0 %collective-permute-start.9 = (f32[20,16,128]{2,1,0:T(8,128)S(1)}, f32[20,16,128]{2,1,0:T(8,128)S(1)}, u32[]{:S(2)}, u32[]{:S(2)}) collective-permute-start(f32[20,16,128]{2,1,0:T(8,128)S(1)} %get-tuple-element.36), channel_id=1, source_target_pairs={{0,4},{4,0},{8,12},{12,8},{16,20},{20,16},{24,28},{28,24},{1,5},{5... | collective-permute-start | bytes 491528 | tf_op jit(solution)/shard_map/ppermute | solution.py:212
  31.9 12.1 %collective-permute-start.11 = (f32[20,16,128]{2,1,0:T(8,128)S(1)}, f32[20,16,128]{2,1,0:T(8,128)S(1)}, u32[]{:S(2)}, u32[]{:S(2)}) collective-permute-start(f32[20,16,128]{2,1,0:T(8,128)S(1)} %get-tuple-element.38), channel_id=1, source_target_pairs={{0,4},{4,0},{8,12},{12,8},{16,20},{20,16},{24,28},{28,24},{1,5},{5... | collective-permute-start | bytes 491528 | tf_op jit(solution)/shard_map/ppermute | solution.py:212
  33.8 13.1 %collective-permute-start.6 = (f32[20,16,128]{2,1,0:T(8,128)S(1)}, f32[20,16,128]{2,1,0:T(8,128)S(1)}, u32[]{:S(2)}, u32[]{:S(2)}) collective-permute-start(f32[20,16,128]{2,1,0:T(8,128)S(1)} %get-tuple-element.32), channel_id=1, source_target_pairs={{0,4},{4,0},{8,12},{12,8},{16,20},{20,16},{24,28},{28,24},{1,5},{5... | collective-permute-start | bytes 491528 | tf_op jit(solution)/shard_map/ppermute | solution.py:212
  39.4 9.5 %collective-permute-start.8 = (f32[20,16,128]{2,1,0:T(8,128)S(1)}, f32[20,16,128]{2,1,0:T(8,128)S(1)}, u32[]{:S(2)}, u32[]{:S(2)}) collective-permute-start(f32[20,16,128]{2,1,0:T(8,128)S(1)} %shard_map.59), channel_id=1, source_target_pairs={{0,24},{4,28},{8,16},{12,20},{16,8},{20,12},{24,0},{28,4},{1,25},{... | collective-permute-start | bytes 491528 | tf_op jit(solution)/shard_map/ppermute | solution.py:212
  43.9 13.4 %collective-permute-start.10 = (f32[20,16,128]{2,1,0:T(8,128)S(1)}, f32[20,16,128]{2,1,0:T(8,128)S(1)}, u32[]{:S(2)}, u32[]{:S(2)}) collective-permute-start(f32[20,16,128]{2,1,0:T(8,128)S(1)} %shard_map.60), channel_id=1, source_target_pairs={{0,16},{4,20},{8,24},{12,28},{16,0},{20,4},{24,8},{28,12},{1,17},{... | collective-permute-start | bytes 491528 | tf_op jit(solution)/shard_map/ppermute | solution.py:212
  44.0 13.3 %collective-permute-start.12 = (f32[20,16,128]{2,1,0:T(8,128)S(1)}, f32[20,16,128]{2,1,0:T(8,128)S(1)}, u32[]{:S(2)}, u32[]{:S(2)}) collective-permute-start(f32[20,16,128]{2,1,0:T(8,128)S(1)} %shard_map.61), channel_id=1, source_target_pairs={{0,8},{4,12},{8,0},{12,4},{16,24},{20,28},{24,16},{28,20},{1,9},{5... | collective-permute-start | bytes 491528 | tf_op jit(solution)/shard_map/ppermute | solution.py:212
  57.4 8.2 %collective-permute-start.13 = (f32[20,16,128]{2,1,0:T(8,128)S(1)}, f32[20,16,128]{2,1,0:T(8,128)S(1)}, u32[]{:S(2)}, u32[]{:S(2)}) collective-permute-start(f32[20,16,128]{2,1,0:T(8,128)S(1)} %shard_map.62.refs_0_), channel_id=1, source_target_pairs={{0,8},{4,12},{8,0},{12,4},{16,24},{20,28},{24,16},{28,20},{1,9},{5... | collective-permute-start | bytes 491528 | tf_op jit(solution)/shard_map/ppermute | solution.py:212
  57.5 14.6 %collective-permute-start.14 = (f32[20,16,128]{2,1,0:T(8,128)S(1)}, f32[20,16,128]{2,1,0:T(8,128)S(1)}, u32[]{:S(2)}, u32[]{:S(2)}) collective-permute-start(f32[20,16,128]{2,1,0:T(8,128)S(1)} %shard_map.62.refs_0_), channel_id=1, source_target_pairs={{0,16},{4,20},{8,24},{12,28},{16,0},{20,4},{24,8},{28,12},{1,17},{... | collective-permute-start | bytes 491528 | tf_op jit(solution)/shard_map/ppermute | solution.py:212
  60.5 13.5 %collective-permute-start.15 = (f32[20,16,128]{2,1,0:T(8,128)S(1)}, f32[20,16,128]{2,1,0:T(8,128)S(1)}, u32[]{:S(2)}, u32[]{:S(2)}) collective-permute-start(f32[20,16,128]{2,1,0:T(8,128)S(1)} %shard_map.62.refs_0_), channel_id=1, source_target_pairs={{0,24},{4,28},{8,16},{12,20},{16,8},{20,12},{24,0},{28,4},{1,25},{... | collective-permute-start | bytes 491528 | tf_op jit(solution)/shard_map/ppermute | solution.py:212
  61.9 17.8 %collective-permute-start.19 = (f32[20,16,128]{2,1,0:T(8,128)S(1)}, f32[20,16,128]{2,1,0:T(8,128)S(1)}, u32[]{:S(2)}, u32[]{:S(2)}) collective-permute-start(f32[20,16,128]{2,1,0:T(8,128)S(1)} %shard_map.62.refs_0_), channel_id=1, source_target_pairs={{0,4},{4,0},{8,12},{12,8},{16,20},{20,16},{24,28},{28,24},{1,5},{5... | collective-permute-start | bytes 491528 | tf_op jit(solution)/shard_map/ppermute | solution.py:212
  65.6 14.1 %collective-permute-start.20 = (f32[20,16,128]{2,1,0:T(8,128)S(1)}, f32[20,16,128]{2,1,0:T(8,128)S(1)}, u32[]{:S(2)}, u32[]{:S(2)}) collective-permute-start(f32[20,16,128]{2,1,0:T(8,128)S(1)} %collective-permute-done.13.refs_1_), channel_id=1, source_target_pairs={{0,4},{4,0},{8,12},{12,8},{16,20},{20,16},{24,28},{28,24},{1,5},{5... | collective-permute-start | bytes 491528 | tf_op jit(solution)/shard_map/ppermute | solution.py:212
  72.1 7.6 %collective-permute-start.21 = (f32[20,16,128]{2,1,0:T(8,128)S(1)}, f32[20,16,128]{2,1,0:T(8,128)S(1)}, u32[]{:S(2)}, u32[]{:S(2)}) collective-permute-start(f32[20,16,128]{2,1,0:T(8,128)S(1)} %collective-permute-done.14.refs_2_), channel_id=1, source_target_pairs={{0,4},{4,0},{8,12},{12,8},{16,20},{20,16},{24,28},{28,24},{1,5},{5... | collective-permute-start | bytes 491528 | tf_op jit(solution)/shard_map/ppermute | solution.py:212
  74.0 5.7 %collective-permute-start.22 = (f32[20,16,128]{2,1,0:T(8,128)S(1)}, f32[20,16,128]{2,1,0:T(8,128)S(1)}, u32[]{:S(2)}, u32[]{:S(2)}) collective-permute-start(f32[20,16,128]{2,1,0:T(8,128)S(1)} %collective-permute-done.15.refs_3_), channel_id=1, source_target_pairs={{0,4},{4,0},{8,12},{12,8},{16,20},{20,16},{24,28},{28,24},{1,5},{5... | collective-permute-start | bytes 491528 | tf_op jit(solution)/shard_map/ppermute | solution.py:212
  79.6 7.0 %collective-permute-start.17 = (f32[8,64,128]{2,1,0:T(8,128)S(1)}, f32[8,64,128]{2,1,0:T(8,128)S(1)}, u32[]{:S(2)}, u32[]{:S(2)}) collective-permute-start(f32[8,64,128]{2,1,0:T(8,128)S(1)} %get-tuple-element.42), channel_id=1, source_target_pairs={{0,1},{1,0},{2,3},{3,2},{4,5},{5,4},{6,7},{7,6},{8,9},{9,8},{10,11... | collective-permute-start | bytes 786440 | tf_op jit(solution)/shard_map/ppermute | solution.py:212
  85.2 3.7 %collective-permute-start.24 = (f32[8,64,128]{2,1,0:T(8,128)S(1)}, f32[8,64,128]{2,1,0:T(8,128)S(1)}, u32[]{:S(2)}, u32[]{:S(2)}) collective-permute-start(f32[8,64,128]{2,1,0:T(8,128)S(1)} %get-tuple-element.46), channel_id=1, source_target_pairs={{0,1},{1,0},{2,3},{3,2},{4,5},{5,4},{6,7},{7,6},{8,9},{9,8},{10,11... | collective-permute-start | bytes 786440 | tf_op jit(solution)/shard_map/ppermute | solution.py:212
  86.6 9.4 %collective-permute-start.18 = (f32[8,64,128]{2,1,0:T(8,128)S(1)}, f32[8,64,128]{2,1,0:T(8,128)S(1)}, u32[]{:S(2)}, u32[]{:S(2)}) collective-permute-start(f32[8,64,128]{2,1,0:T(8,128)S(1)} %shard_map.65), channel_id=1, source_target_pairs={{0,2},{1,3},{2,0},{3,1},{4,6},{5,7},{6,4},{7,5},{8,10},{9,11},{10,... | collective-permute-start | bytes 786440 | tf_op jit(solution)/shard_map/ppermute | solution.py:212
  88.9 12.1 %collective-permute-start.25 = (f32[8,64,128]{2,1,0:T(8,128)S(1)}, f32[8,64,128]{2,1,0:T(8,128)S(1)}, u32[]{:S(2)}, u32[]{:S(2)}) collective-permute-start(f32[8,64,128]{2,1,0:T(8,128)S(1)} %shard_map.68), channel_id=1, source_target_pairs={{0,2},{1,3},{2,0},{3,1},{4,6},{5,7},{6,4},{7,5},{8,10},{9,11},{10,... | collective-permute-start | bytes 786440 | tf_op jit(solution)/shard_map/ppermute | solution.py:212
  (6 other events, 74.5 us)
where the time goes:
time: 103 us; the launch traced here: 102 us
  waiting for transfers between devices  38.6 us (37%)
  Pallas kernels  35.5 us (34%)
  starting transfers between devices  26.9 us (26%)
  local copies, waits for them, and re-layouts  1.08 us (1%)
    ppermute x26, waiting for transfers between devices, shards(): lax.ppermute(value, axis, [(d, d ^ flip) for d in range(lax.axis_size(axi...  38.6 us
    ppermute x26, starting transfers between devices, shards(): lax.ppermute(value, axis, [(d, d ^ flip) for d in range(lax.axis_size(axi...  26.9 us
    pallas_call x2, Pallas kernels, backward(): call(functools.partial(backward_kernel, ang, deep), (jax.ShapeDtypeStruct...  10.9 us
    pallas_call x2, Pallas kernels, forward(): call(functools.partial(forward_kernel, ang, deep), (jax.ShapeDtypeStruct(...  10.9 us
    pallas_call x1, Pallas kernels, shards(): call(split_kernel, pltpu.VMEM((tile_count, rays, 2 * width), bf16), [anyw...  7.82 us
    pallas_call x1, Pallas kernels, shards(): call(functools.partial(plan_kernel, own_tiles, pixel_tiles, live), (liste...  4.16 us
  transfers between devices with their start and end apart: 26, of which 8 were waited for; matrix products, arithmetic and copies ran while one was open for 0% of the time, Pallas kernels for 33%

commit v1 on v0

v1 whole, which is shorter than its diff:
```python
import functools

import jax
import jax.numpy as jnp
from jax import lax
from jax.experimental import pallas as pl
from jax.experimental.pallas import tpu as pltpu
from jax.sharding import PartitionSpec as P

blank_flux = 4096.0
step_size = 0.5
unroll = 8
group = 8
vmem_bytes = 40 * 1024 * 1024

smem = pl.BlockSpec(memory_space=pltpu.SMEM)
vmem = pl.BlockSpec(memory_space=pltpu.VMEM)
hbm = pl.BlockSpec(memory_space=pltpu.HBM)
params = pltpu.CompilerParams(vmem_limit_bytes=vmem_bytes)
f32, bf16, i32 = jnp.float32, jnp.bfloat16, jnp.int32


def halves(value):
    high = value.astype(bf16)
    return high, (value - high.astype(f32)).astype(bf16)


def front_kernel(own_tiles, angles, live_total, ids_hbm, rays_hbm, place, counts, projector, rank_of, col_of, tile_of, total, picked, split, ids, rays, slot_rank, block, fetched, sem, sides):
    copies = [
        pltpu.make_async_copy(ids_hbm, ids, sides.at[0]),
        pltpu.make_async_copy(rays_hbm, rays, sides.at[1]),
    ]
    for copy in copies:
        copy.start()
    for copy in copies:
        copy.wait()
    tile_count = ids.shape[0]
    span = tile_count + unroll
    pixel_tiles = own_tiles * angles
    ray_blocks = counts.shape[0]
    capacity = ray_blocks // rays.shape[1]
    piece = picked.shape[1]
    width = block.shape[2]
    start = pl.multiple_of(place[0], piece)
    for a in range(angles):
        total[a] = 0

    def slot(j, rank):
        live = lax.rem(j, capacity) < rays[0, lax.div(j, capacity)]
        slot_rank[j] = jnp.where(live, rank, -1)

        @pl.when(live)
        def _():
            pltpu.make_async_copy(counts.at[j, pl.ds(start, piece)], picked.at[rank], sem).start()

        return rank + live.astype(i32)

    lax.fori_loop(0, ray_blocks, slot, jnp.int32(0), unroll=4)

    def fetch(t, n):
        pltpu.make_async_copy(projector.at[t], block.at[n], fetched.at[lax.div(n, group)]).start()

    def tile(t, n):
        value = ids[t]
        rank = slot_rank[lax.div(value, pixel_tiles)]

        @pl.when(rank >= 0)
        def _():
            fetch(t, n)
            col = lax.rem(value, pixel_tiles)
            turn = lax.div(col, own_tiles) ^ place[1]
            at = total[turn]
            total[turn] = at + 1
            at = turn * span + at
            rank_of[at] = rank
            col_of[at] = turn * own_tiles + lax.rem(col, own_tiles)
            tile_of[at] = n

        return n + (rank >= 0).astype(i32)

    n = lax.fori_loop(0, tile_count, tile, jnp.int32(0), unroll=4)
    groups = lax.div(n + group - 1, group)

    def fill(extra, carry):
        fetch(0, extra)
        return carry

    lax.fori_loop(n, groups * group, fill, 0)
    for a in range(angles):
        for extra in range(unroll):
            at = a * span + total[a] + extra
            rank_of[at] = live_total
            col_of[at] = pixel_tiles
            tile_of[at] = 0

    def halve(g, carry):
        rows = pl.ds(g * group, group)
        pltpu.make_async_copy(block.at[rows], block.at[rows], fetched.at[g]).wait()
        for u in range(group):
            high, low = halves(block[g * group + u])
            split[g * group + u, :, :width] = high
            split[g * group + u, :, width:] = low
        return carry

    lax.fori_loop(0, groups, halve, 0)
    pltpu.make_async_copy(picked, picked, sem).wait()


def each(turns, span, total, product, sums, index):
    for a in turns:

        def step(i, carry, a=a):
            base = a * span + i * unroll
            products = [product(base + u) for u in range(unroll)]
            for u in range(unroll):
                sums[index[base + u]] += products[u]
            return carry

        lax.fori_loop(0, lax.div(total[a] + unroll - 1, unroll), step, 0)


def forward_kernel(turns, span, deep, chained, rank_of, col_of, tile_of, total, place, split, *refs):
    tiles, refs = refs[: len(turns)], refs[len(turns) :]
    before, refs = refs[:chained], refs[chained:]
    *outs, packed, sums = refs
    own_tiles, half, width = tiles[0].shape
    piece = half // deep

    for a, tile in zip(turns, tiles):

        def fill(i, carry, a=a, tile=tile):
            for k in range(deep):
                rows = pl.ds(pl.multiple_of((place[2] ^ k) * piece, piece), piece)
                high, low = halves(tile[i, rows, :])
                for side in range(2):
                    lanes = slice(side * width, (side + 1) * width)
                    packed[a * own_tiles + i, k * piece : (k + 1) * piece, lanes] = high
                    packed[a * own_tiles + i, half + k * piece : half + (k + 1) * piece, lanes] = low
            return carry

        lax.fori_loop(0, own_tiles, fill, 0)
    sums[...] = before[0][...] if chained else jnp.zeros_like(sums)

    def product(j):
        both = lax.dot_general(
            packed[col_of[j]], split[tile_of[j]], (((1,), (1,)), ((), ())), preferred_element_type=f32
        )
        return both[:half] + both[half:]

    each(turns, span, total, product, sums, rank_of)
    if len(outs) == 1:
        outs[0][...] = sums[...]
        return
    for k in range(deep):
        out = outs[k]
        out[...] = sums[: out.shape[0], k * piece : (k + 1) * piece, :]


def backward_kernel(turns, span, deep, rank_of, col_of, tile_of, total, split, *refs):
    blocks, refs = refs[:deep], refs[deep:]
    *outs, packed, sums = refs
    live, piece, width = blocks[0].shape
    half = piece * deep
    own_tiles = outs[0].shape[0]
    for k in range(deep):

        def fill(i, carry, k=k):
            high, low = halves(blocks[k][i])
            packed[i, k * piece : (k + 1) * piece, :] = high
            packed[i, half + k * piece : half + (k + 1) * piece, :] = low
            return carry

        lax.fori_loop(0, live, fill, 0, unroll=4)
    for a in turns:
        sums[a * own_tiles : (a + 1) * own_tiles] = jnp.zeros_like(outs[0])

    def product(j):
        both = jnp.dot(packed[rank_of[j]], split[tile_of[j]], preferred_element_type=f32)
        both = both[:half] + both[half:]
        return both[:, :width] + both[:, width:]

    each(turns, span, total, product, sums, col_of)
    for a, out in zip(turns, outs):
        out[...] = sums[a * own_tiles : (a + 1) * own_tiles]


def add_kernel(left, right, out):
    out[...] = left[...] + right[...]


def residual_kernel(counts, *refs):
    *terms, out = refs
    summed = terms[0][...]
    for term in terms[1:]:
        summed = summed + term[...]
    measured = counts[...].astype(f32)
    out[...] = measured / blank_flux * (summed - jnp.log(blank_flux / measured))


def update_kernel(deep, place, volume, *refs):
    *terms, out = refs
    half = terms[0].shape[1]
    piece = half // deep
    per_half = len(terms) // 2
    for side in range(2):
        base = (place[3] ^ side) * half
        for k in range(deep):
            rows = pl.ds(pl.multiple_of(base + (place[2] ^ k) * piece, piece), piece)
            local = slice(k * piece, (k + 1) * piece)
            gradient = terms[side * per_half][:, local, :]
            for term in terms[side * per_half + 1 : (side + 1) * per_half]:
                gradient = gradient + term[:, local, :]
            out[:, rows, :] = volume[:, rows, :] - step_size * gradient


def call(kernel, out_shape, in_specs, scratch=(), out_specs=None, traffic=None):
    if out_specs is None:
        out_specs = jax.tree.map(lambda leaf: vmem, out_shape)
    return pl.pallas_call(
        kernel,
        out_shape=out_shape,
        in_specs=in_specs,
        out_specs=out_specs,
        scratch_shapes=list(scratch),
        compiler_params=params,
        cost_estimate=None if traffic is None else pl.CostEstimate(flops=0, bytes_accessed=traffic, transcendentals=0),
    )


def in_hbm(value):
    return pltpu.with_memory_space_constraint(value, pltpu.HBM)


def add(left, right):
    return call(add_kernel, jax.ShapeDtypeStruct(left.shape, f32), [vmem, vmem])(left, right)


def shards(volume, projector, tile_ids, counts, ray_counts):
    pix, ang = lax.axis_size("pix"), lax.axis_size("ang")
    own_tiles, slices, width = volume.shape
    ray_blocks = counts.shape[0]
    tile_count, rays, _ = projector.shape
    pixel_tiles = own_tiles * ang
    live = ray_blocks * 5 // 8
    deep = pix // 2
    half, piece = slices // 2, slices // pix
    me, angle = lax.axis_index("pix"), lax.axis_index("ang")
    side, depth = me % 2, me // 2
    place = jnp.stack([side * half + depth * piece, angle, depth, side]).astype(i32)

    across = lambda value, axis, flip: lax.ppermute(
        value, axis, [(d, d ^ flip) for d in range(lax.axis_size(axis))]
    )
    angle_bits = [1 << b for b in range(ang.bit_length() - 1)]

    def after(value, *others):
        return lax.optimization_barrier((value,) + others)[0]

    def spread(value):
        top = angle_bits[-1]
        return {0: value, top: across(value, "ang", top), 1: across(value, "ang", 1)}

    def relay(held, *others):
        top = angle_bits[-1]
        held = dict(held)
        held[top ^ 1] = across(after(held[top], *others), "ang", 1)
        for bit in angle_bits[1:-1]:
            held.update({k ^ bit: across(part, "ang", bit) for k, part in list(held.items())})
        return held

    far = lax.dynamic_slice_in_dim(volume, (1 - side) * half, half, 1)
    near = lax.dynamic_slice_in_dim(volume, side * half, half, 1)
    far_tiles = spread(far)
    near_tiles = spread(near)

    span = tile_count + unroll
    stored = -(-tile_count // group) * group
    heavy = projector.size * 4
    listed = jax.ShapeDtypeStruct((ang * span,), i32)
    rank_of, col_of, tile_of, total, picked, split = call(
        functools.partial(front_kernel, own_tiles, ang, live),
        (
            listed,
            listed,
            listed,
            jax.ShapeDtypeStruct((ang,), i32),
            jax.ShapeDtypeStruct((live, piece, rays), i32),
            pltpu.VMEM((stored, rays, 2 * width), bf16),
        ),
        [hbm, hbm, smem, hbm, hbm],
        [
            pltpu.SMEM(tile_ids.shape, i32),
            pltpu.SMEM(ray_counts.shape, i32),
            pltpu.SMEM((ray_blocks,), i32),
            pltpu.VMEM((stored, rays, width), f32),
            pltpu.SemaphoreType.DMA((stored // group,)),
            pltpu.SemaphoreType.DMA,
            pltpu.SemaphoreType.DMA((2,)),
        ],
        (smem, smem, smem, smem, vmem, vmem),
        None,
    )(in_hbm(tile_ids), in_hbm(ray_counts), place, in_hbm(counts), in_hbm(projector))
    lists = (rank_of, col_of, tile_of)
    rows = jax.ShapeDtypeStruct((live, piece, rays), f32)
    columns = jax.ShapeDtypeStruct((own_tiles, half, width), f32)

    def forward(turns, tiles, before=(), final=True):
        return call(
            functools.partial(forward_kernel, turns, span, deep, len(before)),
            (rows,) * deep if final else pltpu.VMEM((live + 1, half, rays), f32),
            [smem] * 5 + [vmem] * (1 + len(turns) + len(before)),
            [
                pltpu.VMEM((pixel_tiles + 1, 2 * half, 2 * width), bf16),
                pltpu.VMEM((live + 1, half, rays), f32),
            ],
            traffic=None,
        )(*lists, total, place, split, *[tiles[a] for a in turns], *before)

    def backward(turns, blocks, total):
        parts = call(
            functools.partial(backward_kernel, turns, span, deep),
            (columns,) * len(turns),
            [smem] * 4 + [vmem] * (1 + deep),
            [
                pltpu.VMEM((live + 1, 2 * half, rays), bf16),
                pltpu.VMEM((pixel_tiles + 1, half, width), f32),
            ],
            traffic=None,
        )(*lists, total, split, *blocks)
        return dict(zip(turns, parts))

    turns = tuple(range(ang))
    early = tuple(k for k in turns if k < 2)
    late = turns[2:]
    far_sums = forward(early, far_tiles, (), False)
    near_sums = forward(early, near_tiles, (), False)
    far_tiles = relay(far_tiles, far_sums)
    near_tiles = relay(near_tiles, near_sums)
    far_parts = forward(late, far_tiles, (after(far_sums, near_sums),))
    order = list(range(deep - 1, -1, -1))
    crossed = {k: across(far_parts[k], "pix", 1) for k in order}
    near_parts = forward(late, near_tiles, (near_sums,))
    arrived = [across(add(near_parts[k], crossed[k]), "pix", 2 * k) for k in order if k]
    own = call(
        residual_kernel, jax.ShapeDtypeStruct((live, piece, rays), f32), [vmem] * (3 + len(arrived))
    )(picked, near_parts[0], crossed[0], *arrived)

    near_blocks = [own] + [across(own, "pix", 2 * k) for k in range(1, deep)]
    far_blocks = [across(block, "pix", 1) for block in near_blocks]

    def gather(blocks, total, cuts, *others):
        odd, parts = {}, {}
        for at, cut in enumerate(cuts):
            if at:
                total = after(total, *others)
            made = backward(cut, blocks, total)
            odd.update({k ^ 1: across(part, "ang", 1) for k, part in made.items() if k & 1})
            parts.update({k: part for k, part in made.items() if not k & 1})
        parts = {k: part + odd[k] for k, part in parts.items()}
        for bit in angle_bits[1:-1]:
            for k in [k for k in parts if k & bit]:
                moved = across(parts.pop(k), "ang", bit)
                parts[k ^ bit] = parts[k ^ bit] + moved
        last = parts[angle_bits[-1]]
        return [parts[0], across(last, "ang", angle_bits[-1])], last

    terms, sent = gather(near_blocks, total, (turns,))
    terms = terms + gather(far_blocks, total, (turns[1::2], turns[::2]), sent)[0]
    return call(
        functools.partial(update_kernel, deep), jax.ShapeDtypeStruct(volume.shape, f32), [smem] + [vmem] * 5
    )(place, volume, *terms)


def solution(mesh):
    placed = (
        P(("pix", "ang"), None, None),
        P(("pix", "ang"), None, None),
        P(("pix", "ang")),
        P("ang", None, None),
        P("ang", None),
    )
    return jax.shard_map(
        shards, mesh=mesh, in_specs=placed, out_specs=P(("pix", "ang"), None, None), check_vma=False
    )
```

time: 103 us -> 89.8 us (0.87)
  waiting for transfers between devices: 38.6 us -> 26.4 us
  Pallas kernels: 35.5 us -> 29.3 us
  starting transfers between devices: 26.9 us -> 32.4 us
    ppermute x26, waiting for transfers between devices: 38.6 us -> 26.4 us  [shards(): lax.ppermute(value, axis, [(d, d ^ flip) for d in range(lax.axis_size(axi...]
    pallas_call x6 -> x8, Pallas kernels: 33.8 us -> 27.7 us  [the longest x4 11.4 us: forward(): call(functools.partial(forward_kernel, turns, span, deep, len(before)), (...]
    ppermute x26, starting transfers between devices: 26.9 us -> 32.4 us  [shards(): lax.ppermute(value, axis, [(d, d ^ flip) for d in range(lax.axis_size(axi...]
  transfers between devices with their start and end apart: 26 -> 26, of which waited for: 8 -> 7; matrix products, arithmetic and copies ran while one was open for 0% -> 0% of each run, Pallas kernels for 33% -> 31%
where the time goes in v1:
time: 89.8 us; the launch traced here: 89.6 us
  starting transfers between devices  32.4 us (36%)
  Pallas kernels  29.3 us (33%)
  waiting for transfers between devices  26.4 us (29%)
  local copies, waits for them, and re-layouts  1.07 us (1%)
    ppermute x26, starting transfers between devices, shards(): lax.ppermute(value, axis, [(d, d ^ flip) for d in range(lax.axis_size(axi...  32.4 us
    ppermute x26, waiting for transfers between devices, shards(): lax.ppermute(value, axis, [(d, d ^ flip) for d in range(lax.axis_size(axi...  26.4 us
    pallas_call x4, Pallas kernels, forward(): call(functools.partial(forward_kernel, turns, span, deep, len(before)), (...  11.4 us
    pallas_call x3, Pallas kernels, backward(): call(functools.partial(backward_kernel, turns, span, deep), (columns,) *...  9.96 us
    pallas_call x1, Pallas kernels, shards(): call(functools.partial(front_kernel, own_tiles, ang, live), (listed, list...  6.27 us
  transfers between devices with their start and end apart: 26, of which 7 were waited for; matrix products, arithmetic and copies ran while one was open for 0% of the time, Pallas kernels for 31%

profile of v1, /device:TPU:0, one launch (start us, length us, event | category | flops | bytes accessed | tf_op | source)
XLA Modules:
  0.0 89.6 jit_solution(3223901126134475389)
XLA Ops:
  1.6 2.6 %collective-permute-start.3 = (f32[8,64,128]{2,1,0:T(8,128)S(1)}, f32[8,64,128]{2,1,0:T(8,128)S(1)}, u32[]{:S(2)}, u32[]{:S(2)}) collective-permute-start(f32[8,64,128]{2,1,0:T(8,128)S(1)} %get-tuple-element.57.refs_0_), channel_id=1, source_target_pairs={{0,2},{1,3},{2,0},{3,1},{4,6},{5,7},{6,4},{7,5},{8,10},{9,11},{10,... | collective-permute-start | bytes 786440 | tf_op jit(solution)/shard_map/ppermute | solution.py:251
  4.7 6.3 %shard_map.55 = (s32[672]{0:T(1024)S(1)}, s32[672]{0:T(1024)S(1)}, s32[672]{0:T(1024)S(1)}, s32[4]{0:T(128)S(1)}, s32[20,16,128]{2,1,0:T(8,128)S(1)}, /*index=5*/bf16[160,128,256]{2,1,0:T(8,128)(2,1)S(1)}) custom-call(s32[160]{0:T(256)} %ids_hbm.1, s32[1,8]{1,0:T(1,128)} %rays_hbm.1, s32[4]{0:T(128)S(1)} %pad_add_fusion.place, s32[32,128,128]{2,1,0:T(8,128)} %counts.1, ...), custom_call_target="tpu_custom_call" | custom-call | tf_op jit(solution)/shard_map/pallas_call | solution.py:280
  11.0 2.9 %shard_map.58.refs_2_ = f32[21,64,128]{2,1,0:T(8,128)S(1)} custom-call(s32[672]{0:T(1024)S(1)} %get-tuple-element.31.rank_of, s32[672]{0:T(1024)S(1)} %get-tuple-element.32.col_of, s32[672]{0:T(1024)S(1)} %get-tuple-element.33.tile_of, s32[4]{0:T(128)S(1)} %get-tuple-element.52.total, s32[4]{0:T(128)S(1)} %pad_add_fusion.place, ...), custom_call_target="tpu_custom_call" | custom-call | tf_op jit(solution)/shard_map/pallas_call | solution.py:308
  14.1 2.9 %shard_map.56.refs_2_ = f32[21,64,128]{2,1,0:T(8,128)S(1)} custom-call(s32[672]{0:T(1024)S(1)} %get-tuple-element.31.rank_of, s32[672]{0:T(1024)S(1)} %get-tuple-element.32.col_of, s32[672]{0:T(1024)S(1)} %get-tuple-element.33.tile_of, s32[4]{0:T(128)S(1)} %get-tuple-element.52.total, s32[4]{0:T(128)S(1)} %pad_add_fusion.place, ...), custom_call_target="tpu_custom_call" | custom-call | tf_op jit(solution)/shard_map/pallas_call | solution.py:308
  17.4 2.9 %shard_map.59 = (f32[20,16,128]{2,1,0:T(8,128)S(1)}, f32[20,16,128]{2,1,0:T(8,128)S(1)}, f32[20,16,128]{2,1,0:T(8,128)S(1)}, f32[20,16,128]{2,1,0:T(8,128)S(1)}) custom-call(s32[672]{0:T(1024)S(1)} %get-tuple-element.31.rank_of, s32[672]{0:T(1024)S(1)} %get-tuple-element.32.col_of, s32[672]{0:T(1024)S(1)} %get-tuple-element.33.tile_of, ...), custom_call_target="tpu_custom_call" | custom-call | tf_op jit(solution)/shard_map/pallas_call | solution.py:308
  20.3 2.8 %collective-permute-start.7 = (f32[20,16,128]{2,1,0:T(8,128)S(1)}, f32[20,16,128]{2,1,0:T(8,128)S(1)}, u32[]{:S(2)}, u32[]{:S(2)}) collective-permute-start(f32[20,16,128]{2,1,0:T(8,128)S(1)} %get-tuple-element.43), channel_id=1, source_target_pairs={{0,4},{4,0},{8,12},{12,8},{16,20},{20,16},{24,28},{28,24},{1,5},{5... | collective-permute-start | bytes 491528 | tf_op jit(solution)/shard_map/ppermute | solution.py:251
  23.1 1.9 %collective-permute-start.11 = (f32[20,16,128]{2,1,0:T(8,128)S(1)}, f32[20,16,128]{2,1,0:T(8,128)S(1)}, u32[]{:S(2)}, u32[]{:S(2)}) collective-permute-start(f32[20,16,128]{2,1,0:T(8,128)S(1)} %get-tuple-element.47), channel_id=1, source_target_pairs={{0,4},{4,0},{8,12},{12,8},{16,20},{20,16},{24,28},{28,24},{1,5},{5... | collective-permute-start | bytes 491528 | tf_op jit(solution)/shard_map/ppermute | solution.py:251
  25.1 2.9 %shard_map.57 = (f32[20,16,128]{2,1,0:T(8,128)S(1)}, f32[20,16,128]{2,1,0:T(8,128)S(1)}, f32[20,16,128]{2,1,0:T(8,128)S(1)}, f32[20,16,128]{2,1,0:T(8,128)S(1)}) custom-call(s32[672]{0:T(1024)S(1)} %get-tuple-element.31.rank_of, s32[672]{0:T(1024)S(1)} %get-tuple-element.32.col_of, s32[672]{0:T(1024)S(1)} %get-tuple-element.33.tile_of, ...), custom_call_target="tpu_custom_call" | custom-call | tf_op jit(solution)/shard_map/pallas_call | solution.py:308
  28.1 5.5 %collective-permute-start.8 = (f32[20,16,128]{2,1,0:T(8,128)S(1)}, f32[20,16,128]{2,1,0:T(8,128)S(1)}, u32[]{:S(2)}, u32[]{:S(2)}) collective-permute-start(f32[20,16,128]{2,1,0:T(8,128)S(1)} %shard_map.60), channel_id=1, source_target_pairs={{0,24},{4,28},{8,16},{12,20},{16,8},{20,12},{24,0},{28,4},{1,25},{... | collective-permute-start | bytes 491528 | tf_op jit(solution)/shard_map/ppermute | solution.py:251
  33.5 1.6 %collective-permute-start.10 = (f32[20,16,128]{2,1,0:T(8,128)S(1)}, f32[20,16,128]{2,1,0:T(8,128)S(1)}, u32[]{:S(2)}, u32[]{:S(2)}) collective-permute-start(f32[20,16,128]{2,1,0:T(8,128)S(1)} %shard_map.61), channel_id=1, source_target_pairs={{0,16},{4,20},{8,24},{12,28},{16,0},{20,4},{24,8},{28,12},{1,17},{... | collective-permute-start | bytes 491528 | tf_op jit(solution)/shard_map/ppermute | solution.py:251
  35.2 2.9 %collective-permute-start.12 = (f32[20,16,128]{2,1,0:T(8,128)S(1)}, f32[20,16,128]{2,1,0:T(8,128)S(1)}, u32[]{:S(2)}, u32[]{:S(2)}) collective-permute-start(f32[20,16,128]{2,1,0:T(8,128)S(1)} %shard_map.62), channel_id=1, source_target_pairs={{0,8},{4,12},{8,0},{12,4},{16,24},{20,28},{24,16},{28,20},{1,9},{5... | collective-permute-start | bytes 491528 | tf_op jit(solution)/shard_map/ppermute | solution.py:251
  38.3 7.6 %collective-permute-done.10.refs_3_ = f32[20,16,128]{2,1,0:T(8,128)S(1)} collective-permute-done((f32[20,16,128]{2,1,0:T(8,128)S(1)}, f32[20,16,128]{2,1,0:T(8,128)S(1)}, u32[]{:S(2)}, u32[]{:S(2)}) %collective-permute-start.10) | collective-permute-done | bytes 163872 | tf_op jit(solution)/shard_map/ppermute | solution.py:251
  46.0 3.4 %collective-permute-start.15 = (f32[20,16,128]{2,1,0:T(8,128)S(1)}, f32[20,16,128]{2,1,0:T(8,128)S(1)}, u32[]{:S(2)}, u32[]{:S(2)}) collective-permute-start(f32[20,16,128]{2,1,0:T(8,128)S(1)} %shard_map.63.refs_0_), channel_id=1, source_target_pairs={{0,24},{4,28},{8,16},{12,20},{16,8},{20,12},{24,0},{28,4},{1,25},{... | collective-permute-start | bytes 491528 | tf_op jit(solution)/shard_map/ppermute | solution.py:251
  50.4 1.4 %collective-permute-start.19 = (f32[20,16,128]{2,1,0:T(8,128)S(1)}, f32[20,16,128]{2,1,0:T(8,128)S(1)}, u32[]{:S(2)}, u32[]{:S(2)}) collective-permute-start(f32[20,16,128]{2,1,0:T(8,128)S(1)} %shard_map.63.refs_0_), channel_id=1, source_target_pairs={{0,4},{4,0},{8,12},{12,8},{16,20},{20,16},{24,28},{28,24},{1,5},{5... | collective-permute-start | bytes 491528 | tf_op jit(solution)/shard_map/ppermute | solution.py:251
  51.8 3.2 %collective-permute-done.15.refs_3_ = f32[20,16,128]{2,1,0:T(8,128)S(1)} collective-permute-done((f32[20,16,128]{2,1,0:T(8,128)S(1)}, f32[20,16,128]{2,1,0:T(8,128)S(1)}, u32[]{:S(2)}, u32[]{:S(2)}) %collective-permute-start.15) | collective-permute-done | bytes 163872 | tf_op jit(solution)/shard_map/ppermute | solution.py:251
  55.0 1.4 %collective-permute-start.22 = (f32[20,16,128]{2,1,0:T(8,128)S(1)}, f32[20,16,128]{2,1,0:T(8,128)S(1)}, u32[]{:S(2)}, u32[]{:S(2)}) collective-permute-start(f32[20,16,128]{2,1,0:T(8,128)S(1)} %collective-permute-done.15.refs_3_), channel_id=1, source_target_pairs={{0,4},{4,0},{8,12},{12,8},{16,20},{20,16},{24,28},{28,24},{1,5},{5... | collective-permute-start | bytes 491528 | tf_op jit(solution)/shard_map/ppermute | solution.py:251
  56.3 5.1 %collective-permute-done.14.refs_2_ = f32[20,16,128]{2,1,0:T(8,128)S(1)} collective-permute-done((f32[20,16,128]{2,1,0:T(8,128)S(1)}, f32[20,16,128]{2,1,0:T(8,128)S(1)}, u32[]{:S(2)}, u32[]{:S(2)}) %collective-permute-start.14) | collective-permute-done | bytes 163872 | tf_op jit(solution)/shard_map/ppermute | solution.py:251
  63.5 4.6 %shard_map.64 = (f32[8,64,128]{2,1,0:T(8,128)S(1)}, f32[8,64,128]{2,1,0:T(8,128)S(1)}, f32[8,64,128]{2,1,0:T(8,128)S(1)}, f32[8,64,128]{2,1,0:T(8,128)S(1)}) custom-call(s32[672]{0:T(1024)S(1)} %get-tuple-element.31.rank_of, s32[672]{0:T(1024)S(1)} %get-tuple-element.32.col_of, s32[672]{0:T(1024)S(1)} %get-tuple-element.33.tile_of, ...), custom_call_target="tpu_custom_call" | custom-call | tf_op jit(solution)/shard_map/pallas_call | solution.py:320
  69.1 3.0 %shard_map.66 = (f32[8,64,128]{2,1,0:T(8,128)S(1)}, f32[8,64,128]{2,1,0:T(8,128)S(1)}) custom-call(s32[672]{0:T(1024)S(1)} %get-tuple-element.31.rank_of, s32[672]{0:T(1024)S(1)} %get-tuple-element.32.col_of, s32[672]{0:T(1024)S(1)} %get-tuple-element.33.tile_of, s32[4]{0:T(128)S(1)} %get-tuple-element.52.total, ...), custom_call_target="tpu_custom_call" | custom-call | tf_op jit(solution)/shard_map/pallas_call | solution.py:320
  72.8 2.8 %collective-permute-start.18 = (f32[8,64,128]{2,1,0:T(8,128)S(1)}, f32[8,64,128]{2,1,0:T(8,128)S(1)}, u32[]{:S(2)}, u32[]{:S(2)}) collective-permute-start(f32[8,64,128]{2,1,0:T(8,128)S(1)} %add.31), channel_id=1, source_target_pairs={{0,2},{1,3},{2,0},{3,1},{4,6},{5,7},{6,4},{7,5},{8,10},{9,11},{10,... | collective-permute-start | bytes 786440 | tf_op jit(solution)/shard_map/ppermute | solution.py:251
  75.6 2.4 %shard_map.65 = (f32[8,64,128]{2,1,0:T(8,128)S(1)}, f32[8,64,128]{2,1,0:T(8,128)S(1)}) custom-call(s32[672]{0:T(1024)S(1)} %get-tuple-element.31.rank_of, s32[672]{0:T(1024)S(1)} %get-tuple-element.32.col_of, s32[672]{0:T(1024)S(1)} %get-tuple-element.33.tile_of, s32[4]{0:T(128)S(1)} %get-tuple-element.52.total, ...), custom_call_target="tpu_custom_call" | custom-call | tf_op jit(solution)/shard_map/pallas_call | solution.py:320
  78.9 3.9 %collective-permute-done.18.refs_1_ = f32[8,64,128]{2,1,0:T(8,128)S(1)} collective-permute-done((f32[8,64,128]{2,1,0:T(8,128)S(1)}, f32[8,64,128]{2,1,0:T(8,128)S(1)}, u32[]{:S(2)}, u32[]{:S(2)}) %collective-permute-start.18) | collective-permute-done | bytes 262176 | tf_op jit(solution)/shard_map/ppermute | solution.py:251
  82.8 5.4 %collective-permute-done.25.refs_3_ = f32[8,64,128]{2,1,0:T(8,128)S(1)} collective-permute-done((f32[8,64,128]{2,1,0:T(8,128)S(1)}, f32[8,64,128]{2,1,0:T(8,128)S(1)}, u32[]{:S(2)}, u32[]{:S(2)}) %collective-permute-start.25) | collective-permute-done | bytes 262176 | tf_op jit(solution)/shard_map/ppermute | solution.py:251
  88.1 1.4 %shard_map.67 = f32[8,128,128]{2,1,0:T(8,128)} custom-call(s32[4]{0:T(128)S(1)} %pad_add_fusion.place, f32[8,128,128]{2,1,0:T(8,128)S(1)} %copy-done, f32[8,64,128]{2,1,0:T(8,128)S(1)} %add.30.refs_0_, f32[8,64,128]{2,1,0:T(8,128)S(1)} %collective-permute-done.18.refs_1_, f32[8,64,128]{2,1,0:T(8,128)S(1)} %add.32.refs_2_, ...), custom_call_target="tpu_custom_call" | custom-call | tf_op jit(solution)/shard_map/pallas_call | solution.py:369
  (49 shorter events, 9.0 us)
Async XLA Ops:
  1.1 9.9 %collective-permute-start.4 = (f32[8,64,128]{2,1,0:T(8,128)S(1)}, f32[8,64,128]{2,1,0:T(8,128)S(1)}, u32[]{:S(2)}, u32[]{:S(2)}) collective-permute-start(f32[8,64,128]{2,1,0:T(8,128)S(1)} %get-tuple-element.57.refs_0_), channel_id=1, source_target_pairs={{0,1},{1,0},{2,3},{3,2},{4,5},{5,4},{6,7},{7,6},{8,9},{9,8},{10,11... | collective-permute-start | bytes 786440 | tf_op jit(solution)/shard_map/ppermute | solution.py:251
  1.6 12.3 %collective-permute-start.3 = (f32[8,64,128]{2,1,0:T(8,128)S(1)}, f32[8,64,128]{2,1,0:T(8,128)S(1)}, u32[]{:S(2)}, u32[]{:S(2)}) collective-permute-start(f32[8,64,128]{2,1,0:T(8,128)S(1)} %get-tuple-element.57.refs_0_), channel_id=1, source_target_pairs={{0,2},{1,3},{2,0},{3,1},{4,6},{5,7},{6,4},{7,5},{8,10},{9,11},{10,... | collective-permute-start | bytes 786440 | tf_op jit(solution)/shard_map/ppermute | solution.py:251
  4.2 9.9 %collective-permute-start.1 = (f32[8,64,128]{2,1,0:T(8,128)S(1)}, f32[8,64,128]{2,1,0:T(8,128)S(1)}, u32[]{:S(2)}, u32[]{:S(2)}) collective-permute-start(f32[8,64,128]{2,1,0:T(8,128)S(1)} %get-tuple-element.58.refs_0_), channel_id=1, source_target_pairs={{0,1},{1,0},{2,3},{3,2},{4,5},{5,4},{6,7},{7,6},{8,9},{9,8},{10,11... | collective-permute-start | bytes 786440 | tf_op jit(solution)/shard_map/ppermute | solution.py:251
  4.3 12.6 %collective-permute-start = (f32[8,64,128]{2,1,0:T(8,128)S(1)}, f32[8,64,128]{2,1,0:T(8,128)S(1)}, u32[]{:S(2)}, u32[]{:S(2)}) collective-permute-start(f32[8,64,128]{2,1,0:T(8,128)S(1)} %get-tuple-element.58.refs_0_), channel_id=1, source_target_pairs={{0,2},{1,3},{2,0},{3,1},{4,6},{5,7},{6,4},{7,5},{8,10},{9,11},{10,... | collective-permute-start | bytes 786440 | tf_op jit(solution)/shard_map/ppermute | solution.py:251
  16.9 8.2 %collective-permute-start.2 = (f32[8,64,128]{2,1,0:T(8,128)S(1)}, f32[8,64,128]{2,1,0:T(8,128)S(1)}, u32[]{:S(2)}, u32[]{:S(2)}) collective-permute-start(f32[8,64,128]{2,1,0:T(8,128)S(1)} %collective-permute-done.refs_0_), channel_id=1, source_target_pairs={{0,1},{1,0},{2,3},{3,2},{4,5},{5,4},{6,7},{7,6},{8,9},{9,8},{10,11... | collective-permute-start | bytes 786440 | tf_op jit(solution)/shard_map/ppermute | solution.py:251
  20.3 7.8 %collective-permute-start.7 = (f32[20,16,128]{2,1,0:T(8,128)S(1)}, f32[20,16,128]{2,1,0:T(8,128)S(1)}, u32[]{:S(2)}, u32[]{:S(2)}) collective-permute-start(f32[20,16,128]{2,1,0:T(8,128)S(1)} %get-tuple-element.43), channel_id=1, source_target_pairs={{0,4},{4,0},{8,12},{12,8},{16,20},{20,16},{24,28},{28,24},{1,5},{5... | collective-permute-start | bytes 491528 | tf_op jit(solution)/shard_map/ppermute | solution.py:251
  23.0 10.5 %collective-permute-start.9 = (f32[20,16,128]{2,1,0:T(8,128)S(1)}, f32[20,16,128]{2,1,0:T(8,128)S(1)}, u32[]{:S(2)}, u32[]{:S(2)}) collective-permute-start(f32[20,16,128]{2,1,0:T(8,128)S(1)} %get-tuple-element.45), channel_id=1, source_target_pairs={{0,4},{4,0},{8,12},{12,8},{16,20},{20,16},{24,28},{28,24},{1,5},{5... | collective-permute-start | bytes 491528 | tf_op jit(solution)/shard_map/ppermute | solution.py:251
  23.1 12.0 %collective-permute-start.11 = (f32[20,16,128]{2,1,0:T(8,128)S(1)}, f32[20,16,128]{2,1,0:T(8,128)S(1)}, u32[]{:S(2)}, u32[]{:S(2)}) collective-permute-start(f32[20,16,128]{2,1,0:T(8,128)S(1)} %get-tuple-element.47), channel_id=1, source_target_pairs={{0,4},{4,0},{8,12},{12,8},{16,20},{20,16},{24,28},{28,24},{1,5},{5... | collective-permute-start | bytes 491528 | tf_op jit(solution)/shard_map/ppermute | solution.py:251
  25.1 13.3 %collective-permute-start.6 = (f32[20,16,128]{2,1,0:T(8,128)S(1)}, f32[20,16,128]{2,1,0:T(8,128)S(1)}, u32[]{:S(2)}, u32[]{:S(2)}) collective-permute-start(f32[20,16,128]{2,1,0:T(8,128)S(1)} %get-tuple-element.41), channel_id=1, source_target_pairs={{0,4},{4,0},{8,12},{12,8},{16,20},{20,16},{24,28},{28,24},{1,5},{5... | collective-permute-start | bytes 491528 | tf_op jit(solution)/shard_map/ppermute | solution.py:251
  28.1 10.3 %collective-permute-start.8 = (f32[20,16,128]{2,1,0:T(8,128)S(1)}, f32[20,16,128]{2,1,0:T(8,128)S(1)}, u32[]{:S(2)}, u32[]{:S(2)}) collective-permute-start(f32[20,16,128]{2,1,0:T(8,128)S(1)} %shard_map.60), channel_id=1, source_target_pairs={{0,24},{4,28},{8,16},{12,20},{16,8},{20,12},{24,0},{28,4},{1,25},{... | collective-permute-start | bytes 491528 | tf_op jit(solution)/shard_map/ppermute | solution.py:251
  33.5 12.4 %collective-permute-start.10 = (f32[20,16,128]{2,1,0:T(8,128)S(1)}, f32[20,16,128]{2,1,0:T(8,128)S(1)}, u32[]{:S(2)}, u32[]{:S(2)}) collective-permute-start(f32[20,16,128]{2,1,0:T(8,128)S(1)} %shard_map.61), channel_id=1, source_target_pairs={{0,16},{4,20},{8,24},{12,28},{16,0},{20,4},{24,8},{28,12},{1,17},{... | collective-permute-start | bytes 491528 | tf_op jit(solution)/shard_map/ppermute | solution.py:251
  35.2 10.7 %collective-permute-start.12 = (f32[20,16,128]{2,1,0:T(8,128)S(1)}, f32[20,16,128]{2,1,0:T(8,128)S(1)}, u32[]{:S(2)}, u32[]{:S(2)}) collective-permute-start(f32[20,16,128]{2,1,0:T(8,128)S(1)} %shard_map.62), channel_id=1, source_target_pairs={{0,8},{4,12},{8,0},{12,4},{16,24},{20,28},{24,16},{28,20},{1,9},{5... | collective-permute-start | bytes 491528 | tf_op jit(solution)/shard_map/ppermute | solution.py:251
  46.0 9.0 %collective-permute-start.15 = (f32[20,16,128]{2,1,0:T(8,128)S(1)}, f32[20,16,128]{2,1,0:T(8,128)S(1)}, u32[]{:S(2)}, u32[]{:S(2)}) collective-permute-start(f32[20,16,128]{2,1,0:T(8,128)S(1)} %shard_map.63.refs_0_), channel_id=1, source_target_pairs={{0,24},{4,28},{8,16},{12,20},{16,8},{20,12},{24,0},{28,4},{1,25},{... | collective-permute-start | bytes 491528 | tf_op jit(solution)/shard_map/ppermute | solution.py:251
  49.4 12.1 %collective-permute-start.14 = (f32[20,16,128]{2,1,0:T(8,128)S(1)}, f32[20,16,128]{2,1,0:T(8,128)S(1)}, u32[]{:S(2)}, u32[]{:S(2)}) collective-permute-start(f32[20,16,128]{2,1,0:T(8,128)S(1)} %shard_map.63.refs_0_), channel_id=1, source_target_pairs={{0,16},{4,20},{8,24},{12,28},{16,0},{20,4},{24,8},{28,12},{1,17},{... | collective-permute-start | bytes 491528 | tf_op jit(solution)/shard_map/ppermute | solution.py:251
  49.4 13.2 %collective-permute-start.13 = (f32[20,16,128]{2,1,0:T(8,128)S(1)}, f32[20,16,128]{2,1,0:T(8,128)S(1)}, u32[]{:S(2)}, u32[]{:S(2)}) collective-permute-start(f32[20,16,128]{2,1,0:T(8,128)S(1)} %shard_map.63.refs_0_), channel_id=1, source_target_pairs={{0,8},{4,12},{8,0},{12,4},{16,24},{20,28},{24,16},{28,20},{1,9},{5... | collective-permute-start | bytes 491528 | tf_op jit(solution)/shard_map/ppermute | solution.py:251
  50.4 17.7 %collective-permute-start.19 = (f32[20,16,128]{2,1,0:T(8,128)S(1)}, f32[20,16,128]{2,1,0:T(8,128)S(1)}, u32[]{:S(2)}, u32[]{:S(2)}) collective-permute-start(f32[20,16,128]{2,1,0:T(8,128)S(1)} %shard_map.63.refs_0_), channel_id=1, source_target_pairs={{0,4},{4,0},{8,12},{12,8},{16,20},{20,16},{24,28},{28,24},{1,5},{5... | collective-permute-start | bytes 491528 | tf_op jit(solution)/shard_map/ppermute | solution.py:251
  55.0 13.1 %collective-permute-start.22 = (f32[20,16,128]{2,1,0:T(8,128)S(1)}, f32[20,16,128]{2,1,0:T(8,128)S(1)}, u32[]{:S(2)}, u32[]{:S(2)}) collective-permute-start(f32[20,16,128]{2,1,0:T(8,128)S(1)} %collective-permute-done.15.refs_3_), channel_id=1, source_target_pairs={{0,4},{4,0},{8,12},{12,8},{16,20},{20,16},{24,28},{28,24},{1,5},{5... | collective-permute-start | bytes 491528 | tf_op jit(solution)/shard_map/ppermute | solution.py:251
  61.4 6.7 %collective-permute-start.21 = (f32[20,16,128]{2,1,0:T(8,128)S(1)}, f32[20,16,128]{2,1,0:T(8,128)S(1)}, u32[]{:S(2)}, u32[]{:S(2)}) collective-permute-start(f32[20,16,128]{2,1,0:T(8,128)S(1)} %collective-permute-done.14.refs_2_), channel_id=1, source_target_pairs={{0,4},{4,0},{8,12},{12,8},{16,20},{20,16},{24,28},{28,24},{1,5},{5... | collective-permute-start | bytes 491528 | tf_op jit(solution)/shard_map/ppermute | solution.py:251
  62.5 6.6 %collective-permute-start.20 = (f32[20,16,128]{2,1,0:T(8,128)S(1)}, f32[20,16,128]{2,1,0:T(8,128)S(1)}, u32[]{:S(2)}, u32[]{:S(2)}) collective-permute-start(f32[20,16,128]{2,1,0:T(8,128)S(1)} %collective-permute-done.13.refs_1_), channel_id=1, source_target_pairs={{0,4},{4,0},{8,12},{12,8},{16,20},{20,16},{24,28},{28,24},{1,5},{5... | collective-permute-start | bytes 491528 | tf_op jit(solution)/shard_map/ppermute | solution.py:251
  72.1 5.9 %collective-permute-start.24 = (f32[8,64,128]{2,1,0:T(8,128)S(1)}, f32[8,64,128]{2,1,0:T(8,128)S(1)}, u32[]{:S(2)}, u32[]{:S(2)}) collective-permute-start(f32[8,64,128]{2,1,0:T(8,128)S(1)} %get-tuple-element.56), channel_id=1, source_target_pairs={{0,1},{1,0},{2,3},{3,2},{4,5},{5,4},{6,7},{7,6},{8,9},{9,8},{10,11... | collective-permute-start | bytes 786440 | tf_op jit(solution)/shard_map/ppermute | solution.py:251
  72.2 6.6 %collective-permute-start.16 = (f32[8,64,128]{2,1,0:T(8,128)S(1)}, f32[8,64,128]{2,1,0:T(8,128)S(1)}, u32[]{:S(2)}, u32[]{:S(2)}) collective-permute-start(f32[8,64,128]{2,1,0:T(8,128)S(1)} %get-tuple-element.49), channel_id=1, source_target_pairs={{0,1},{1,0},{2,3},{3,2},{4,5},{5,4},{6,7},{7,6},{8,9},{9,8},{10,11... | collective-permute-start | bytes 786440 | tf_op jit(solution)/shard_map/ppermute | solution.py:251
  72.7 6.1 %collective-permute-start.23 = (f32[8,64,128]{2,1,0:T(8,128)S(1)}, f32[8,64,128]{2,1,0:T(8,128)S(1)}, u32[]{:S(2)}, u32[]{:S(2)}) collective-permute-start(f32[8,64,128]{2,1,0:T(8,128)S(1)} %get-tuple-element.54), channel_id=1, source_target_pairs={{0,1},{1,0},{2,3},{3,2},{4,5},{5,4},{6,7},{7,6},{8,9},{9,8},{10,11... | collective-permute-start | bytes 786440 | tf_op jit(solution)/shard_map/ppermute | solution.py:251
  72.8 10.0 %collective-permute-start.18 = (f32[8,64,128]{2,1,0:T(8,128)S(1)}, f32[8,64,128]{2,1,0:T(8,128)S(1)}, u32[]{:S(2)}, u32[]{:S(2)}) collective-permute-start(f32[8,64,128]{2,1,0:T(8,128)S(1)} %add.31), channel_id=1, source_target_pairs={{0,2},{1,3},{2,0},{3,1},{4,6},{5,7},{6,4},{7,5},{8,10},{9,11},{10,... | collective-permute-start | bytes 786440 | tf_op jit(solution)/shard_map/ppermute | solution.py:251
  78.1 10.1 %collective-permute-start.25 = (f32[8,64,128]{2,1,0:T(8,128)S(1)}, f32[8,64,128]{2,1,0:T(8,128)S(1)}, u32[]{:S(2)}, u32[]{:S(2)}) collective-permute-start(f32[8,64,128]{2,1,0:T(8,128)S(1)} %add.33), channel_id=1, source_target_pairs={{0,2},{1,3},{2,0},{3,1},{4,6},{5,7},{6,4},{7,5},{8,10},{9,11},{10,... | collective-permute-start | bytes 786440 | tf_op jit(solution)/shard_map/ppermute | solution.py:251
  (3 other events, 28.4 us)

commit v2 on v1

--- a/solution.py
+++ b/solution.py
@@ -16,6 +16,7 @@
 smem = pl.BlockSpec(memory_space=pltpu.SMEM)
 vmem = pl.BlockSpec(memory_space=pltpu.VMEM)
 hbm = pl.BlockSpec(memory_space=pltpu.HBM)
+anywhere = pl.BlockSpec(memory_space=pl.ANY)
 params = pltpu.CompilerParams(vmem_limit_bytes=vmem_bytes)
 f32, bf16, i32 = jnp.float32, jnp.bfloat16, jnp.int32
 
@@ -119,23 +120,26 @@
         lax.fori_loop(0, lax.div(total[a] + unroll - 1, unroll), step, 0)
 
 
-def forward_kernel(turns, span, deep, chained, rank_of, col_of, tile_of, total, place, split, *refs):
-    tiles, refs = refs[: len(turns)], refs[len(turns) :]
+def forward_kernel(turns, sides, span, deep, chained, rank_of, col_of, tile_of, total, place, split, *refs):
+    tiles, refs = refs[: sides * len(turns)], refs[sides * len(turns) :]
     before, refs = refs[:chained], refs[chained:]
     *outs, packed, sums = refs
     own_tiles, half, width = tiles[0].shape
     piece = half // deep
-
-    for a, tile in zip(turns, tiles):
-
-        def fill(i, carry, a=a, tile=tile):
-            for k in range(deep):
-                rows = pl.ds(pl.multiple_of((place[2] ^ k) * piece, piece), piece)
-                high, low = halves(tile[i, rows, :])
-                for side in range(2):
-                    lanes = slice(side * width, (side + 1) * width)
-                    packed[a * own_tiles + i, k * piece : (k + 1) * piece, lanes] = high
-                    packed[a * own_tiles + i, half + k * piece : half + (k + 1) * piece, lanes] = low
+    rows_all = sides * half
+
+    for at, a in enumerate(turns):
+
+        def fill(i, carry, at=at, a=a):
+            for part in range(sides):
+                for k in range(deep):
+                    rows = pl.ds(pl.multiple_of((place[2] ^ k) * piece, piece), piece)
+                    first = part * half + k * piece
+                    high, low = halves(tiles[part * len(turns) + at][i, rows, :])
+                    for side in range(2):
+                        lanes = slice(side * width, (side + 1) * width)
+                        packed[a * own_tiles + i, first : first + piece, lanes] = high
+                        packed[a * own_tiles + i, rows_all + first : rows_all + first + piece, lanes] = low
             return carry
 
         lax.fori_loop(0, own_tiles, fill, 0)
@@ -145,72 +149,99 @@
         both = lax.dot_general(
             packed[col_of[j]], split[tile_of[j]], (((1,), (1,)), ((), ())), preferred_element_type=f32
         )
-        return both[:half] + both[half:]
+        return both[:rows_all] + both[rows_all:]
 
     each(turns, span, total, product, sums, rank_of)
-    if len(outs) == 1:
-        outs[0][...] = sums[...]
+    if not chained:
+        for part, out in enumerate(outs):
+            out[...] = sums[:, part * half : (part + 1) * half, :]
         return
-    for k in range(deep):
-        out = outs[k]
+    for k, out in enumerate(outs):
         out[...] = sums[: out.shape[0], k * piece : (k + 1) * piece, :]
 
 
-def backward_kernel(turns, span, deep, rank_of, col_of, tile_of, total, split, *refs):
-    blocks, refs = refs[:deep], refs[deep:]
-    *outs, packed, sums = refs
-    live, piece, width = blocks[0].shape
-    half = piece * deep
+def backward_kernel(turns, loose, layout, span, rank_of, col_of, tile_of, total, split, *refs):
+    *refs, packed, sums = refs
+    refs = list(refs)
+    blocks = [[refs.pop(0) for _ in range(parts)] for parts in layout]
+    outs, count = refs, len(layout)
+    live, _, width = blocks[0][0].shape
+    rows_all = packed.shape[1] // 2
+    piece = rows_all // count
     own_tiles = outs[0].shape[0]
-    for k in range(deep):
-
-        def fill(i, carry, k=k):
-            high, low = halves(blocks[k][i])
+    zeros = jnp.zeros((own_tiles, rows_all, width), f32)
+    for k, block in enumerate(blocks):
+
+        def fill(i, carry, k=k, block=block):
+            whole = jnp.concatenate([part[i] for part in block], axis=0)
+            high, low = halves(whole)
             packed[i, k * piece : (k + 1) * piece, :] = high
-            packed[i, half + k * piece : half + (k + 1) * piece, :] = low
+            packed[i, rows_all + k * piece : rows_all + (k + 1) * piece, :] = low
             return carry
 
         lax.fori_loop(0, live, fill, 0, unroll=4)
     for a in turns:
-        sums[a * own_tiles : (a + 1) * own_tiles] = jnp.zeros_like(outs[0])
+        sums[a * own_tiles : (a + 1) * own_tiles] = zeros
 
     def product(j):
         both = jnp.dot(packed[rank_of[j]], split[tile_of[j]], preferred_element_type=f32)
-        both = both[:half] + both[half:]
+        both = both[:rows_all] + both[rows_all:]
         return both[:, :width] + both[:, width:]
 
     each(turns, span, total, product, sums, col_of)
-    for a, out in zip(turns, outs):
-        out[...] = sums[a * own_tiles : (a + 1) * own_tiles]
-
-
-def add_kernel(left, right, out):
-    out[...] = left[...] + right[...]
-
-
-def residual_kernel(counts, *refs):
-    *terms, out = refs
-    summed = terms[0][...]
-    for term in terms[1:]:
-        summed = summed + term[...]
+    for a in turns:
+        tiles = slice(a * own_tiles, (a + 1) * own_tiles)
+        if a not in loose:
+            outs.pop(0)[...] = sums[tiles]
+            continue
+        for k in range(count):
+            outs.pop(0)[...] = sums[tiles, k * piece : (k + 1) * piece, :]
+
+
+def add_kernel(cuts, count, *refs):
+    terms, outs = refs[:count], refs[count:]
+    for first, out in zip(cuts, outs):
+        rows = out.shape[1]
+        total = None
+        for term in terms:
+            value = term[...] if term.shape[1] == rows else term[:, first : first + rows, :]
+            total = value if total is None else total + value
+        out[...] = total
+
+
+def residual_kernel(cuts, counts, *refs):
+    terms, outs = refs[: -len(cuts)], refs[-len(cuts) :]
+    height = counts.shape[1]
+    summed = 0.0
+    parts = [term[...] for term in terms if term.shape[1] == height]
+    for part in parts:
+        summed = summed + part
+    short = [term[...] for term in terms if term.shape[1] != height]
+    if short:
+        upper = sum(short[:-1])
+        summed = summed + jnp.concatenate([upper, short[-1]], axis=1)
     measured = counts[...].astype(f32)
-    out[...] = measured / blank_flux * (summed - jnp.log(blank_flux / measured))
-
-
-def update_kernel(deep, place, volume, *refs):
-    *terms, out = refs
-    half = terms[0].shape[1]
+    value = measured / blank_flux * (summed - jnp.log(blank_flux / measured))
+    for first, out in zip(cuts, outs):
+        out[...] = value[:, first : first + out.shape[1], :]
+
+
+def update_kernel(parts, deep, place, volume, *refs):
+    terms, (out, fresh, sems) = refs[: 2 * len(parts)], refs[-3:]
+    half = fresh.shape[1] // 2
     piece = half // deep
-    per_half = len(terms) // 2
-    for side in range(2):
-        base = (place[3] ^ side) * half
-        for k in range(deep):
-            rows = pl.ds(pl.multiple_of(base + (place[2] ^ k) * piece, piece), piece)
-            local = slice(k * piece, (k + 1) * piece)
-            gradient = terms[side * per_half][:, local, :]
-            for term in terms[side * per_half + 1 : (side + 1) * per_half]:
-                gradient = gradient + term[:, local, :]
-            out[:, rows, :] = volume[:, rows, :] - step_size * gradient
+    copies = []
+    for at, part in enumerate(parts):
+        left, right = terms[2 * at : 2 * at + 2]
+        for slot, (flip, k) in enumerate(part):
+            first = (place[3] ^ flip) * half + (place[2] ^ k) * piece
+            rows = pl.ds(pl.multiple_of(first, piece), piece)
+            local = slice(slot * piece, (slot + 1) * piece)
+            fresh[:, rows, :] = volume[:, rows, :] - step_size * (left[:, local, :] + right[:, local, :])
+            copies.append(pltpu.make_async_copy(fresh.at[:, rows], out.at[:, rows], sems.at[len(copies)]))
+            copies[-1].start()
+    for copy in copies:
+        copy.wait()
 
 
 def call(kernel, out_shape, in_specs, scratch=(), out_specs=None, traffic=None):
@@ -231,8 +262,13 @@
     return pltpu.with_memory_space_constraint(value, pltpu.HBM)
 
 
-def add(left, right):
-    return call(add_kernel, jax.ShapeDtypeStruct(left.shape, f32), [vmem, vmem])(left, right)
+def add(cuts, rows, *terms):
+    live, _, width = terms[0].shape
+    return call(
+        functools.partial(add_kernel, cuts, len(terms)),
+        (jax.ShapeDtypeStruct((live, rows, width), f32),) * len(cuts),
+        [vmem] * len(terms),
+    )(*terms)
 
 
 def shards(volume, projector, tile_ids, counts, ray_counts):
@@ -304,71 +340,127 @@
     rows = jax.ShapeDtypeStruct((live, piece, rays), f32)
     columns = jax.ShapeDtypeStruct((own_tiles, half, width), f32)
 
-    def forward(turns, tiles, before=(), final=True):
+    def forward(turns, sides, before=()):
+        count = len(sides)
         return call(
-            functools.partial(forward_kernel, turns, span, deep, len(before)),
-            (rows,) * deep if final else pltpu.VMEM((live + 1, half, rays), f32),
-            [smem] * 5 + [vmem] * (1 + len(turns) + len(before)),
+            functools.partial(forward_kernel, turns, count, span, deep, len(before)),
+            (rows,) * deep if before else (pltpu.VMEM((live + 1, half, rays), f32),) * count,
+            [smem] * 5 + [vmem] * (1 + count * len(turns) + len(before)),
             [
-                pltpu.VMEM((pixel_tiles + 1, 2 * half, 2 * width), bf16),
-                pltpu.VMEM((live + 1, half, rays), f32),
+                pltpu.VMEM((pixel_tiles + 1, 2 * count * half, 2 * width), bf16),
+                pltpu.VMEM((live + 1, count * half, rays), f32),
             ],
-            traffic=None,
-        )(*lists, total, place, split, *[tiles[a] for a in turns], *before)
-
-    def backward(turns, blocks, total):
-        parts = call(
-            functools.partial(backward_kernel, turns, span, deep),
-            (columns,) * len(turns),
-            [smem] * 4 + [vmem] * (1 + deep),
+        )(*lists, total, place, split, *[tiles[a] for tiles in sides for a in turns], *before)
+
+    def backward(turns, part, total, loose=()):
+        count = len(part)
+        height = piece * count
+        made = call(
+            functools.partial(backward_kernel, turns, loose, [len(blocks[spot]) for spot in part], span),
+            sum(
+                (
+                    (jax.ShapeDtypeStruct((own_tiles, piece, width), f32),) * count
+                    if a in loose
+                    else (jax.ShapeDtypeStruct((own_tiles, height, width), f32),)
+                    for a in turns
+                ),
+                (),
+            ),
+            [smem] * 4 + [vmem] * (1 + sum(len(blocks[spot]) for spot in part)),
             [
-                pltpu.VMEM((live + 1, 2 * half, rays), bf16),
-                pltpu.VMEM((pixel_tiles + 1, half, width), f32),
+                pltpu.VMEM((live + 1, 2 * height, rays), bf16),
+                pltpu.VMEM((pixel_tiles + 1, height, width), f32),
             ],
-            traffic=None,
-        )(*lists, total, split, *blocks)
-        return dict(zip(turns, parts))
+        )(*lists, total, split, *[block for spot in part for block in blocks[spot]])
+        made = list(made)
+        return {a: [made.pop(0) for _ in range(count if a in loose else 1)] for a in turns}
 
     turns = tuple(range(ang))
     early = tuple(k for k in turns if k < 2)
     late = turns[2:]
-    far_sums = forward(early, far_tiles, (), False)
-    near_sums = forward(early, near_tiles, (), False)
-    far_tiles = relay(far_tiles, far_sums)
+    far_sums, near_sums = forward(early, (far_tiles, near_tiles))
+    far_tiles = relay(far_tiles, total)
     near_tiles = relay(near_tiles, near_sums)
-    far_parts = forward(late, far_tiles, (after(far_sums, near_sums),))
-    order = list(range(deep - 1, -1, -1))
+    far_parts = forward(late, (far_tiles,), (far_sums,))
+    order = [k for k in (3, 2, 1) if k < deep] + list(range(4, deep)) + [0]
     crossed = {k: across(far_parts[k], "pix", 1) for k in order}
-    near_parts = forward(late, near_tiles, (near_sums,))
-    arrived = [across(add(near_parts[k], crossed[k]), "pix", 2 * k) for k in order if k]
-    own = call(
-        residual_kernel, jax.ShapeDtypeStruct((live, piece, rays), f32), [vmem] * (3 + len(arrived))
-    )(picked, near_parts[0], crossed[0], *arrived)
-
-    near_blocks = [own] + [across(own, "pix", 2 * k) for k in range(1, deep)]
-    far_blocks = [across(block, "pix", 1) for block in near_blocks]
-
-    def gather(blocks, total, cuts, *others):
-        odd, parts = {}, {}
-        for at, cut in enumerate(cuts):
-            if at:
-                total = after(total, *others)
-            made = backward(cut, blocks, total)
-            odd.update({k ^ 1: across(part, "ang", 1) for k, part in made.items() if k & 1})
-            parts.update({k: part for k, part in made.items() if not k & 1})
-        parts = {k: part + odd[k] for k, part in parts.items()}
-        for bit in angle_bits[1:-1]:
+    near_parts = forward(late, (near_tiles,), (near_sums,))
+    def residual(cuts, heights, *terms):
+        return call(
+            functools.partial(residual_kernel, cuts),
+            tuple(jax.ShapeDtypeStruct((live, height, rays), f32) for height in heights),
+            [vmem] * (1 + len(terms)),
+        )(picked, *terms)
+
+    side_of = lambda value, k: across(value, "pix", 2 * k)
+    cut = piece // 2
+    if deep == 4:
+        first, rest = add((0, cut), cut, near_parts[3], crossed[3])
+        came = [side_of(first, 3)]
+        passed = side_of(rest, 1)
+        (first,) = add((0,), cut, near_parts[2], crossed[2])
+        came.append(side_of(first, 2))
+        (rest,) = add((cut,), cut, near_parts[2], crossed[2], after(passed, came[0]))
+        rest = side_of(rest, 2)
+        (one,) = add((0,), piece, after(near_parts[1], first), crossed[1])
+        whole_one = side_of(one, 1)
+        own, first, last = residual(
+            (0, 0, cut), (piece, cut, cut), near_parts[0], crossed[0], *came, rest, whole_one
+        )
+        last_two = side_of(last, 2)
+        near_one = side_of(own, 1)
+        first_three = side_of(first, 3)
+        first_two = side_of(first, 2)
+        last_three = side_of(last_two, 1)
+        near_blocks = [(own,), (near_one,), (first_two, last_two), (first_three, last_three)]
+    else:
+        came = [side_of(add((0,), piece, near_parts[k], crossed[k])[0], k) for k in order if k]
+        (own,) = residual((0,), (piece,), near_parts[0], crossed[0], *came)
+        near_blocks = [(own,)] + [(side_of(own, k),) for k in range(1, deep)]
+    far_blocks = [tuple(across(part, "pix", 1) for part in parts) for parts in near_blocks]
+    blocks = {(0, k): parts for k, parts in enumerate(near_blocks)}
+    blocks.update({(1, k): parts for k, parts in enumerate(far_blocks)})
+    arrival = [k for k in (1, 3, 2) if k < deep] + list(range(4, deep))
+    near_all = [(0, k) for k in [0] + arrival]
+    far_all = [(1, k) for k in [0] + arrival]
+    top = angle_bits[-1]
+    lower, upper = turns[:top], turns[top:]
+
+    def join(parts):
+        return jnp.concatenate(parts, axis=1) if len(parts) > 1 else parts[0]
+
+    def fold(parts, *others):
+        parts = dict(parts)
+        for bit in angle_bits[:-1]:
             for k in [k for k in parts if k & bit]:
-                moved = across(parts.pop(k), "ang", bit)
-                parts[k ^ bit] = parts[k ^ bit] + moved
-        last = parts[angle_bits[-1]]
-        return [parts[0], across(last, "ang", angle_bits[-1])], last
-
-    terms, sent = gather(near_blocks, total, (turns,))
-    terms = terms + gather(far_blocks, total, (turns[1::2], turns[::2]), sent)[0]
-    return call(
-        functools.partial(update_kernel, deep), jax.ShapeDtypeStruct(volume.shape, f32), [smem] + [vmem] * 5
-    )(place, volume, *terms)
+                moved = [across(after(part, *others), "ang", bit) for part in parts.pop(k)]
+                parts[k ^ bit] = [join(parts[k ^ bit]) + join(moved)]
+        return parts[min(parts)][0]
+
+    def whole(part, total, *others):
+        made = backward(turns, part, total, upper[1::2])
+        return fold({k: made[k] for k in lower}, *others), fold({k: made[k] for k in upper}, *others)
+
+    def update(parts, terms, *started):
+        return pl.pallas_call(
+            functools.partial(update_kernel, parts, deep),
+            out_shape=jax.ShapeDtypeStruct(volume.shape, f32),
+            in_specs=[smem] + [vmem] * (1 + len(terms)) + [anywhere] * len(started),
+            out_specs=anywhere,
+            scratch_shapes=[pltpu.VMEM(volume.shape, f32), pltpu.SemaphoreType.DMA((2 * deep,))],
+            input_output_aliases={2 + len(terms): 0} if started else {},
+            compiler_params=params,
+        )(place, volume, *terms, *started)
+
+    made = backward(turns, near_all, total)
+    up_near = fold({k: made[k] for k in upper})
+    low_near = fold({k: made[k] for k in lower})
+    up_far = fold(backward(upper, far_all, total))
+    low_far = fold(backward(lower, far_all, after(total, up_near, up_far)))
+    came_near = across(up_near, "ang", top)
+    came_far = across(up_far, "ang", top)
+    begun = update((near_all,), (low_near, came_near))
+    return update((far_all,), (low_far, came_far), begun)
 
 
 def solution(mesh):

time: 89.8 us -> 87.9 us (0.979)
  waiting for transfers between devices: 26.4 us -> 21.6 us
  starting transfers between devices: 32.4 us -> 34.5 us
  Pallas kernels: 29.3 us -> 30.9 us
    ppermute x26 -> x32, waiting for transfers between devices: 26.4 us -> 21.6 us  [shards(): lax.ppermute(value, axis, [(d, d ^ flip) for d in range(lax.axis_size(axi...]
    ppermute x26 -> x32, starting transfers between devices: 32.4 us -> 34.5 us  [shards(): lax.ppermute(value, axis, [(d, d ^ flip) for d in range(lax.axis_size(axi...]
    pallas_call x12 -> x13, Pallas kernels: 23 us -> 24.5 us  [the longest x3 11.2 us: backward(): call(functools.partial(backward_kernel, turns, loose, [len(blocks[spot])...]
  transfers between devices with their start and end apart: 26 -> 32, of which waited for: 7 -> 9; matrix products, arithmetic and copies ran while one was open for 0% -> 0% of each run, Pallas kernels for 31% -> 33%
where the time goes in v2:
time: 87.9 us; the launch traced here: 88.5 us
  starting transfers between devices  34.5 us (39%)
  Pallas kernels  30.9 us (35%)
  waiting for transfers between devices  21.6 us (25%)
  local copies, waits for them, and re-layouts  1.07 us (1%)
    ppermute x32, starting transfers between devices, shards(): lax.ppermute(value, axis, [(d, d ^ flip) for d in range(lax.axis_size(axi...  34.5 us
    ppermute x32, waiting for transfers between devices, shards(): lax.ppermute(value, axis, [(d, d ^ flip) for d in range(lax.axis_size(axi...  21.6 us
    pallas_call x3, Pallas kernels, backward(): call(functools.partial(backward_kernel, turns, loose, [len(blocks[spot])...  11.2 us
    pallas_call x3, Pallas kernels, forward(): call(functools.partial(forward_kernel, turns, count, span, deep, len(befo...  10.5 us
    pallas_call x1, Pallas kernels, shards(): call(functools.partial(front_kernel, own_tiles, ang, live), (listed, list...  6.42 us
    pallas_call x2, Pallas kernels, update(): pl.pallas_call(functools.partial(update_kernel, parts, deep), out_shape=j...  2.64 us
  transfers between devices with their start and end apart: 32, of which 9 were waited for; matrix products, arithmetic and copies ran while one was open for 0% of the time, Pallas kernels for 33%

profile of v2, /device:TPU:0, one launch (start us, length us, event | category | flops | bytes accessed | tf_op | source)
XLA Modules:
  0.0 88.5 jit_solution(2021575428472008127)
XLA Ops:
  1.1 3.0 %collective-permute-start.4 = (f32[8,64,128]{2,1,0:T(8,128)S(1)}, f32[8,64,128]{2,1,0:T(8,128)S(1)}, u32[]{:S(2)}, u32[]{:S(2)}) collective-permute-start(f32[8,64,128]{2,1,0:T(8,128)S(1)} %get-tuple-element.73.refs_0_), channel_id=1, source_target_pairs={{0,2},{1,3},{2,0},{3,1},{4,6},{5,7},{6,4},{7,5},{8,10},{9,11},{10,... | collective-permute-start | bytes 786440 | tf_op jit(solution)/shard_map/ppermute | solution.py:287
  4.7 6.4 %shard_map.55 = (s32[672]{0:T(1024)S(1)}, s32[672]{0:T(1024)S(1)}, s32[672]{0:T(1024)S(1)}, s32[4]{0:T(128)S(1)}, s32[20,16,128]{2,1,0:T(8,128)S(1)}, /*index=5*/bf16[160,128,256]{2,1,0:T(8,128)(2,1)S(1)}) custom-call(s32[160]{0:T(256)} %ids_hbm.1, s32[1,8]{1,0:T(1,128)} %rays_hbm.1, s32[4]{0:T(128)S(1)} %pad_add_fusion.place, s32[32,128,128]{2,1,0:T(8,128)} %counts.1, ...), custom_call_target="tpu_custom_call" | custom-call | tf_op jit(solution)/shard_map/pallas_call | solution.py:316
  11.3 4.8 %shard_map.56 = (f32[21,64,128]{2,1,0:T(8,128)S(1)}, f32[21,64,128]{2,1,0:T(8,128)S(1)}) custom-call(s32[672]{0:T(1024)S(1)} %get-tuple-element.39.rank_of, s32[672]{0:T(1024)S(1)} %get-tuple-element.40.col_of, s32[672]{0:T(1024)S(1)} %get-tuple-element.41.tile_of, s32[4]{0:T(128)S(1)} %get-tuple-element.68.total, s32[4]{0:T(128)S(1)} %pad_add_fusion.place, ...), custom_call_target="tpu_custom_call" | custom-call | tf_op jit(solution)/shard_map/pallas_call | solution.py:345
  16.2 2.9 %shard_map.58 = (f32[20,16,128]{2,1,0:T(8,128)S(1)}, f32[20,16,128]{2,1,0:T(8,128)S(1)}, f32[20,16,128]{2,1,0:T(8,128)S(1)}, f32[20,16,128]{2,1,0:T(8,128)S(1)}) custom-call(s32[672]{0:T(1024)S(1)} %get-tuple-element.39.rank_of, s32[672]{0:T(1024)S(1)} %get-tuple-element.40.col_of, s32[672]{0:T(1024)S(1)} %get-tuple-element.41.tile_of, ...), custom_call_target="tpu_custom_call" | custom-call | tf_op jit(solution)/shard_map/pallas_call | solution.py:345
  19.0 1.8 %collective-permute-start.7 = (f32[20,16,128]{2,1,0:T(8,128)S(1)}, f32[20,16,128]{2,1,0:T(8,128)S(1)}, u32[]{:S(2)}, u32[]{:S(2)}) collective-permute-start(f32[20,16,128]{2,1,0:T(8,128)S(1)} %get-tuple-element.52), channel_id=1, source_target_pairs={{0,4},{4,0},{8,12},{12,8},{16,20},{20,16},{24,28},{28,24},{1,5},{5... | collective-permute-start | bytes 491528 | tf_op jit(solution)/shard_map/ppermute | solution.py:287
  21.1 1.7 %collective-permute-start.13 = (f32[20,16,128]{2,1,0:T(8,128)S(1)}, f32[20,16,128]{2,1,0:T(8,128)S(1)}, u32[]{:S(2)}, u32[]{:S(2)}) collective-permute-start(f32[20,16,128]{2,1,0:T(8,128)S(1)} %get-tuple-element.60), channel_id=1, source_target_pairs={{0,4},{4,0},{8,12},{12,8},{16,20},{20,16},{24,28},{28,24},{1,5},{5... | collective-permute-start | bytes 491528 | tf_op jit(solution)/shard_map/ppermute | solution.py:287
  23.2 2.9 %shard_map.57 = (f32[20,16,128]{2,1,0:T(8,128)S(1)}, f32[20,16,128]{2,1,0:T(8,128)S(1)}, f32[20,16,128]{2,1,0:T(8,128)S(1)}, f32[20,16,128]{2,1,0:T(8,128)S(1)}) custom-call(s32[672]{0:T(1024)S(1)} %get-tuple-element.39.rank_of, s32[672]{0:T(1024)S(1)} %get-tuple-element.40.col_of, s32[672]{0:T(1024)S(1)} %get-tuple-element.41.tile_of, ...), custom_call_target="tpu_custom_call" | custom-call | tf_op jit(solution)/shard_map/pallas_call | solution.py:345
  26.2 4.9 %collective-permute-start.8 = (f32[20,8,128]{2,1,0:T(8,128)S(1)}, f32[20,8,128]{2,1,0:T(8,128)S(1)}, u32[]{:S(2)}, u32[]{:S(2)}) collective-permute-start(f32[20,8,128]{2,1,0:T(8,128)S(1)} %get-tuple-element.53), channel_id=1, source_target_pairs={{0,24},{4,28},{8,16},{12,20},{16,8},{20,12},{24,0},{28,4},{1,25},{... | collective-permute-start | bytes 245768 | tf_op jit(solution)/shard_map/ppermute | solution.py:287
  31.1 2.1 %collective-permute-done.13.refs_1_ = f32[20,16,128]{2,1,0:T(8,128)S(1)} collective-permute-done((f32[20,16,128]{2,1,0:T(8,128)S(1)}, f32[20,16,128]{2,1,0:T(8,128)S(1)}, u32[]{:S(2)}, u32[]{:S(2)}) %collective-permute-start.13) | collective-permute-done | bytes 163872 | tf_op jit(solution)/shard_map/ppermute | solution.py:287
  33.2 3.0 %collective-permute-start.14 = (f32[20,16,128]{2,1,0:T(8,128)S(1)}, f32[20,16,128]{2,1,0:T(8,128)S(1)}, u32[]{:S(2)}, u32[]{:S(2)}) collective-permute-start(f32[20,16,128]{2,1,0:T(8,128)S(1)} %shard_map.62), channel_id=1, source_target_pairs={{0,8},{4,12},{8,0},{12,4},{16,24},{20,28},{24,16},{28,20},{1,9},{5... | collective-permute-start | bytes 491528 | tf_op jit(solution)/shard_map/ppermute | solution.py:287
  36.2 1.9 %collective-permute-start.10 = (f32[20,8,128]{2,1,0:T(8,128)S(1)}, f32[20,8,128]{2,1,0:T(8,128)S(1)}, u32[]{:S(2)}, u32[]{:S(2)}) collective-permute-start(f32[20,8,128]{2,1,0:T(8,128)S(1)} %shard_map.60), channel_id=1, source_target_pairs={{0,16},{4,20},{8,24},{12,28},{16,0},{20,4},{24,8},{28,12},{1,17},{... | collective-permute-start | bytes 245768 | tf_op jit(solution)/shard_map/ppermute | solution.py:287
  39.2 3.8 %collective-permute-done.10.refs_3_ = f32[20,8,128]{2,1,0:T(8,128)S(1)} collective-permute-done((f32[20,8,128]{2,1,0:T(8,128)S(1)}, f32[20,8,128]{2,1,0:T(8,128)S(1)}, u32[]{:S(2)}, u32[]{:S(2)}) %collective-permute-start.10) | collective-permute-done | bytes 81952 | tf_op jit(solution)/shard_map/ppermute | solution.py:287
  43.0 2.6 %collective-permute-done.12.refs_4_ = f32[20,8,128]{2,1,0:T(8,128)S(1)} collective-permute-done((f32[20,8,128]{2,1,0:T(8,128)S(1)}, f32[20,8,128]{2,1,0:T(8,128)S(1)}, u32[]{:S(2)}, u32[]{:S(2)}) %collective-permute-start.12) | collective-permute-done | bytes 81952 | tf_op jit(solution)/shard_map/ppermute | solution.py:287
  47.2 2.6 %collective-permute-start.17 = (f32[20,8,128]{2,1,0:T(8,128)S(1)}, f32[20,8,128]{2,1,0:T(8,128)S(1)}, u32[]{:S(2)}, u32[]{:S(2)}) collective-permute-start(f32[20,8,128]{2,1,0:T(8,128)S(1)} %get-tuple-element.63), channel_id=1, source_target_pairs={{0,16},{4,20},{8,24},{12,28},{16,0},{20,4},{24,8},{28,12},{1,17},{... | collective-permute-start | bytes 245768 | tf_op jit(solution)/shard_map/ppermute | solution.py:287
  49.8 1.7 %collective-permute-start.16 = (f32[20,8,128]{2,1,0:T(8,128)S(1)}, f32[20,8,128]{2,1,0:T(8,128)S(1)}, u32[]{:S(2)}, u32[]{:S(2)}) collective-permute-start(f32[20,8,128]{2,1,0:T(8,128)S(1)} %get-tuple-element.62), channel_id=1, source_target_pairs={{0,24},{4,28},{8,16},{12,20},{16,8},{20,12},{24,0},{28,4},{1,25},{... | collective-permute-start | bytes 245768 | tf_op jit(solution)/shard_map/ppermute | solution.py:287
  51.5 5.5 %collective-permute-done.17.refs_5_ = f32[20,8,128]{2,1,0:T(8,128)S(1)} collective-permute-done((f32[20,8,128]{2,1,0:T(8,128)S(1)}, f32[20,8,128]{2,1,0:T(8,128)S(1)}, u32[]{:S(2)}, u32[]{:S(2)}) %collective-permute-start.17) | collective-permute-done | bytes 81952 | tf_op jit(solution)/shard_map/ppermute | solution.py:287
  57.1 2.0 %collective-permute-start.26 = (f32[20,8,128]{2,1,0:T(8,128)S(1)}, f32[20,8,128]{2,1,0:T(8,128)S(1)}, u32[]{:S(2)}, u32[]{:S(2)}) collective-permute-start(f32[20,8,128]{2,1,0:T(8,128)S(1)} %collective-permute-done.17.refs_5_), channel_id=1, source_target_pairs={{0,4},{4,0},{8,12},{12,8},{16,20},{20,16},{24,28},{28,24},{1,5},{5... | collective-permute-start | bytes 245768 | tf_op jit(solution)/shard_map/ppermute | solution.py:287
  59.2 1.9 %collective-permute-start.25 = (f32[20,8,128]{2,1,0:T(8,128)S(1)}, f32[20,8,128]{2,1,0:T(8,128)S(1)}, u32[]{:S(2)}, u32[]{:S(2)}) collective-permute-start(f32[20,8,128]{2,1,0:T(8,128)S(1)} %collective-permute-done.19.refs_4_), channel_id=1, source_target_pairs={{0,4},{4,0},{8,12},{12,8},{16,20},{20,16},{24,28},{28,24},{1,5},{5... | collective-permute-start | bytes 245768 | tf_op jit(solution)/shard_map/ppermute | solution.py:287
  61.5 5.2 %shard_map.64 = (f32[8,64,128]{2,1,0:T(8,128)S(1)}, f32[8,64,128]{2,1,0:T(8,128)S(1)}, f32[8,64,128]{2,1,0:T(8,128)S(1)}, f32[8,64,128]{2,1,0:T(8,128)S(1)}) custom-call(s32[672]{0:T(1024)S(1)} %get-tuple-element.39.rank_of, s32[672]{0:T(1024)S(1)} %get-tuple-element.40.col_of, s32[672]{0:T(1024)S(1)} %get-tuple-element.41.tile_of, ...), custom_call_target="tpu_custom_call" | custom-call | tf_op jit(solution)/shard_map/pallas_call | solution.py:358
  66.8 2.7 %shard_map.65 = (f32[8,64,128]{2,1,0:T(8,128)S(1)}, f32[8,64,128]{2,1,0:T(8,128)S(1)}) custom-call(s32[672]{0:T(1024)S(1)} %get-tuple-element.39.rank_of, s32[672]{0:T(1024)S(1)} %get-tuple-element.40.col_of, s32[672]{0:T(1024)S(1)} %get-tuple-element.41.tile_of, s32[4]{0:T(128)S(1)} %get-tuple-element.68.total, ...), custom_call_target="tpu_custom_call" | custom-call | tf_op jit(solution)/shard_map/pallas_call | solution.py:358
  70.5 4.5 %collective-permute-start.31 = (f32[8,64,128]{2,1,0:T(8,128)S(1)}, f32[8,64,128]{2,1,0:T(8,128)S(1)}, u32[]{:S(2)}, u32[]{:S(2)}) collective-permute-start(f32[8,64,128]{2,1,0:T(8,128)S(1)} %add.30), channel_id=1, source_target_pairs={{0,2},{1,3},{2,0},{3,1},{4,6},{5,7},{6,4},{7,5},{8,10},{9,11},{10,... | collective-permute-start | bytes 786440 | tf_op jit(solution)/shard_map/ppermute | solution.py:287
  75.0 3.3 %shard_map.66 = (f32[8,64,128]{2,1,0:T(8,128)S(1)}, f32[8,64,128]{2,1,0:T(8,128)S(1)}) custom-call(s32[672]{0:T(1024)S(1)} %get-tuple-element.39.rank_of, s32[672]{0:T(1024)S(1)} %get-tuple-element.40.col_of, s32[672]{0:T(1024)S(1)} %get-tuple-element.41.tile_of, s32[4]{0:T(128)S(1)} %get-tuple-element.68.total, ...), custom_call_target="tpu_custom_call" | custom-call | tf_op jit(solution)/shard_map/pallas_call | solution.py:358
  78.9 2.8 %collective-permute-done.31.refs_1_ = f32[8,64,128]{2,1,0:T(8,128)S(1)} collective-permute-done((f32[8,64,128]{2,1,0:T(8,128)S(1)}, f32[8,64,128]{2,1,0:T(8,128)S(1)}, u32[]{:S(2)}, u32[]{:S(2)}) %collective-permute-start.31) | collective-permute-done | bytes 262176 | tf_op jit(solution)/shard_map/ppermute | solution.py:287
  83.1 4.1 %collective-permute-done.29.refs_1_ = f32[8,64,128]{2,1,0:T(8,128)S(1)} collective-permute-done((f32[8,64,128]{2,1,0:T(8,128)S(1)}, f32[8,64,128]{2,1,0:T(8,128)S(1)}, u32[]{:S(2)}, u32[]{:S(2)}) %collective-permute-start.29) | collective-permute-done | bytes 262176 | tf_op jit(solution)/shard_map/ppermute | solution.py:287
  (62 shorter events, 10.1 us)
Async XLA Ops:
  1.1 10.2 %collective-permute-start.4 = (f32[8,64,128]{2,1,0:T(8,128)S(1)}, f32[8,64,128]{2,1,0:T(8,128)S(1)}, u32[]{:S(2)}, u32[]{:S(2)}) collective-permute-start(f32[8,64,128]{2,1,0:T(8,128)S(1)} %get-tuple-element.73.refs_0_), channel_id=1, source_target_pairs={{0,2},{1,3},{2,0},{3,1},{4,6},{5,7},{6,4},{7,5},{8,10},{9,11},{10,... | collective-permute-start | bytes 786440 | tf_op jit(solution)/shard_map/ppermute | solution.py:287
  4.1 7.1 %collective-permute-start.1 = (f32[8,64,128]{2,1,0:T(8,128)S(1)}, f32[8,64,128]{2,1,0:T(8,128)S(1)}, u32[]{:S(2)}, u32[]{:S(2)}) collective-permute-start(f32[8,64,128]{2,1,0:T(8,128)S(1)} %get-tuple-element.73.refs_0_), channel_id=1, source_target_pairs={{0,1},{1,0},{2,3},{3,2},{4,5},{5,4},{6,7},{7,6},{8,9},{9,8},{10,11... | collective-permute-start | bytes 786440 | tf_op jit(solution)/shard_map/ppermute | solution.py:287
  4.1 11.9 %collective-permute-start = (f32[8,64,128]{2,1,0:T(8,128)S(1)}, f32[8,64,128]{2,1,0:T(8,128)S(1)}, u32[]{:S(2)}, u32[]{:S(2)}) collective-permute-start(f32[8,64,128]{2,1,0:T(8,128)S(1)} %get-tuple-element.74.refs_2_), channel_id=1, source_target_pairs={{0,2},{1,3},{2,0},{3,1},{4,6},{5,7},{6,4},{7,5},{8,10},{9,11},{10,... | collective-permute-start | bytes 786440 | tf_op jit(solution)/shard_map/ppermute | solution.py:287
  16.0 7.1 %collective-permute-start.3 = (f32[8,64,128]{2,1,0:T(8,128)S(1)}, f32[8,64,128]{2,1,0:T(8,128)S(1)}, u32[]{:S(2)}, u32[]{:S(2)}) collective-permute-start(f32[8,64,128]{2,1,0:T(8,128)S(1)} %collective-permute-done.refs_0_), channel_id=1, source_target_pairs={{0,1},{1,0},{2,3},{3,2},{4,5},{5,4},{6,7},{7,6},{8,9},{9,8},{10,11... | collective-permute-start | bytes 786440 | tf_op jit(solution)/shard_map/ppermute | solution.py:287
  19.0 7.1 %collective-permute-start.7 = (f32[20,16,128]{2,1,0:T(8,128)S(1)}, f32[20,16,128]{2,1,0:T(8,128)S(1)}, u32[]{:S(2)}, u32[]{:S(2)}) collective-permute-start(f32[20,16,128]{2,1,0:T(8,128)S(1)} %get-tuple-element.52), channel_id=1, source_target_pairs={{0,4},{4,0},{8,12},{12,8},{16,20},{20,16},{24,28},{28,24},{1,5},{5... | collective-permute-start | bytes 491528 | tf_op jit(solution)/shard_map/ppermute | solution.py:287
  20.8 10.3 %collective-permute-start.9 = (f32[20,16,128]{2,1,0:T(8,128)S(1)}, f32[20,16,128]{2,1,0:T(8,128)S(1)}, u32[]{:S(2)}, u32[]{:S(2)}) collective-permute-start(f32[20,16,128]{2,1,0:T(8,128)S(1)} %get-tuple-element.55), channel_id=1, source_target_pairs={{0,4},{4,0},{8,12},{12,8},{16,20},{20,16},{24,28},{28,24},{1,5},{5... | collective-permute-start | bytes 491528 | tf_op jit(solution)/shard_map/ppermute | solution.py:287
  21.1 12.1 %collective-permute-start.13 = (f32[20,16,128]{2,1,0:T(8,128)S(1)}, f32[20,16,128]{2,1,0:T(8,128)S(1)}, u32[]{:S(2)}, u32[]{:S(2)}) collective-permute-start(f32[20,16,128]{2,1,0:T(8,128)S(1)} %get-tuple-element.60), channel_id=1, source_target_pairs={{0,4},{4,0},{8,12},{12,8},{16,20},{20,16},{24,28},{28,24},{1,5},{5... | collective-permute-start | bytes 491528 | tf_op jit(solution)/shard_map/ppermute | solution.py:287
  22.9 16.3 %collective-permute-start.6 = (f32[20,16,128]{2,1,0:T(8,128)S(1)}, f32[20,16,128]{2,1,0:T(8,128)S(1)}, u32[]{:S(2)}, u32[]{:S(2)}) collective-permute-start(f32[20,16,128]{2,1,0:T(8,128)S(1)} %get-tuple-element.50), channel_id=1, source_target_pairs={{0,4},{4,0},{8,12},{12,8},{16,20},{20,16},{24,28},{28,24},{1,5},{5... | collective-permute-start | bytes 491528 | tf_op jit(solution)/shard_map/ppermute | solution.py:287
  26.2 11.9 %collective-permute-start.8 = (f32[20,8,128]{2,1,0:T(8,128)S(1)}, f32[20,8,128]{2,1,0:T(8,128)S(1)}, u32[]{:S(2)}, u32[]{:S(2)}) collective-permute-start(f32[20,8,128]{2,1,0:T(8,128)S(1)} %get-tuple-element.53), channel_id=1, source_target_pairs={{0,24},{4,28},{8,16},{12,20},{16,8},{20,12},{24,0},{28,4},{1,25},{... | collective-permute-start | bytes 245768 | tf_op jit(solution)/shard_map/ppermute | solution.py:287
  31.1 7.0 %collective-permute-start.11 = (f32[20,8,128]{2,1,0:T(8,128)S(1)}, f32[20,8,128]{2,1,0:T(8,128)S(1)}, u32[]{:S(2)}, u32[]{:S(2)}) collective-permute-start(f32[20,8,128]{2,1,0:T(8,128)S(1)} %get-tuple-element.56), channel_id=1, source_target_pairs={{0,8},{4,12},{8,0},{12,4},{16,24},{20,28},{24,16},{28,20},{1,9},{5... | collective-permute-start | bytes 245768 | tf_op jit(solution)/shard_map/ppermute | solution.py:287
  33.2 12.4 %collective-permute-start.14 = (f32[20,16,128]{2,1,0:T(8,128)S(1)}, f32[20,16,128]{2,1,0:T(8,128)S(1)}, u32[]{:S(2)}, u32[]{:S(2)}) collective-permute-start(f32[20,16,128]{2,1,0:T(8,128)S(1)} %shard_map.62), channel_id=1, source_target_pairs={{0,8},{4,12},{8,0},{12,4},{16,24},{20,28},{24,16},{28,20},{1,9},{5... | collective-permute-start | bytes 491528 | tf_op jit(solution)/shard_map/ppermute | solution.py:287
  38.1 7.5 %collective-permute-start.12 = (f32[20,8,128]{2,1,0:T(8,128)S(1)}, f32[20,8,128]{2,1,0:T(8,128)S(1)}, u32[]{:S(2)}, u32[]{:S(2)}) collective-permute-start(f32[20,8,128]{2,1,0:T(8,128)S(1)} %shard_map.61), channel_id=1, source_target_pairs={{0,16},{4,20},{8,24},{12,28},{16,0},{20,4},{24,8},{28,12},{1,17},{... | collective-permute-start | bytes 245768 | tf_op jit(solution)/shard_map/ppermute | solution.py:287
  45.7 11.3 %collective-permute-start.15 = (f32[20,16,128]{2,1,0:T(8,128)S(1)}, f32[20,16,128]{2,1,0:T(8,128)S(1)}, u32[]{:S(2)}, u32[]{:S(2)}) collective-permute-start(f32[20,16,128]{2,1,0:T(8,128)S(1)} %get-tuple-element.61.refs_0_), channel_id=1, source_target_pairs={{0,8},{4,12},{8,0},{12,4},{16,24},{20,28},{24,16},{28,20},{1,9},{5... | collective-permute-start | bytes 491528 | tf_op jit(solution)/shard_map/ppermute | solution.py:287
  45.8 13.4 %collective-permute-start.21 = (f32[20,16,128]{2,1,0:T(8,128)S(1)}, f32[20,16,128]{2,1,0:T(8,128)S(1)}, u32[]{:S(2)}, u32[]{:S(2)}) collective-permute-start(f32[20,16,128]{2,1,0:T(8,128)S(1)} %get-tuple-element.61.refs_0_), channel_id=1, source_target_pairs={{0,4},{4,0},{8,12},{12,8},{16,20},{20,16},{24,28},{28,24},{1,5},{5... | collective-permute-start | bytes 491528 | tf_op jit(solution)/shard_map/ppermute | solution.py:287
  47.2 9.8 %collective-permute-start.17 = (f32[20,8,128]{2,1,0:T(8,128)S(1)}, f32[20,8,128]{2,1,0:T(8,128)S(1)}, u32[]{:S(2)}, u32[]{:S(2)}) collective-permute-start(f32[20,8,128]{2,1,0:T(8,128)S(1)} %get-tuple-element.63), channel_id=1, source_target_pairs={{0,16},{4,20},{8,24},{12,28},{16,0},{20,4},{24,8},{28,12},{1,17},{... | collective-permute-start | bytes 245768 | tf_op jit(solution)/shard_map/ppermute | solution.py:287
  49.8 7.3 %collective-permute-start.16 = (f32[20,8,128]{2,1,0:T(8,128)S(1)}, f32[20,8,128]{2,1,0:T(8,128)S(1)}, u32[]{:S(2)}, u32[]{:S(2)}) collective-permute-start(f32[20,8,128]{2,1,0:T(8,128)S(1)} %get-tuple-element.62), channel_id=1, source_target_pairs={{0,24},{4,28},{8,16},{12,20},{16,8},{20,12},{24,0},{28,4},{1,25},{... | collective-permute-start | bytes 245768 | tf_op jit(solution)/shard_map/ppermute | solution.py:287
  51.5 7.6 %collective-permute-start.19 = (f32[20,8,128]{2,1,0:T(8,128)S(1)}, f32[20,8,128]{2,1,0:T(8,128)S(1)}, u32[]{:S(2)}, u32[]{:S(2)}) collective-permute-start(f32[20,8,128]{2,1,0:T(8,128)S(1)} %get-tuple-element.62), channel_id=1, source_target_pairs={{0,16},{4,20},{8,24},{12,28},{16,0},{20,4},{24,8},{28,12},{1,17},{... | collective-permute-start | bytes 245768 | tf_op jit(solution)/shard_map/ppermute | solution.py:287
  57.1 9.7 %collective-permute-start.22 = (f32[20,16,128]{2,1,0:T(8,128)S(1)}, f32[20,16,128]{2,1,0:T(8,128)S(1)}, u32[]{:S(2)}, u32[]{:S(2)}) collective-permute-start(f32[20,16,128]{2,1,0:T(8,128)S(1)} %collective-permute-done.15.refs_1_), channel_id=1, source_target_pairs={{0,4},{4,0},{8,12},{12,8},{16,20},{20,16},{24,28},{28,24},{1,5},{5... | collective-permute-start | bytes 491528 | tf_op jit(solution)/shard_map/ppermute | solution.py:287
  57.1 9.7 %collective-permute-start.26 = (f32[20,8,128]{2,1,0:T(8,128)S(1)}, f32[20,8,128]{2,1,0:T(8,128)S(1)}, u32[]{:S(2)}, u32[]{:S(2)}) collective-permute-start(f32[20,8,128]{2,1,0:T(8,128)S(1)} %collective-permute-done.17.refs_5_), channel_id=1, source_target_pairs={{0,4},{4,0},{8,12},{12,8},{16,20},{20,16},{24,28},{28,24},{1,5},{5... | collective-permute-start | bytes 245768 | tf_op jit(solution)/shard_map/ppermute | solution.py:287
  59.1 7.6 %collective-permute-start.23 = (f32[20,8,128]{2,1,0:T(8,128)S(1)}, f32[20,8,128]{2,1,0:T(8,128)S(1)}, u32[]{:S(2)}, u32[]{:S(2)}) collective-permute-start(f32[20,8,128]{2,1,0:T(8,128)S(1)} %collective-permute-done.16.refs_2_), channel_id=1, source_target_pairs={{0,4},{4,0},{8,12},{12,8},{16,20},{20,16},{24,28},{28,24},{1,5},{5... | collective-permute-start | bytes 245768 | tf_op jit(solution)/shard_map/ppermute | solution.py:287
  59.2 7.6 %collective-permute-start.25 = (f32[20,8,128]{2,1,0:T(8,128)S(1)}, f32[20,8,128]{2,1,0:T(8,128)S(1)}, u32[]{:S(2)}, u32[]{:S(2)}) collective-permute-start(f32[20,8,128]{2,1,0:T(8,128)S(1)} %collective-permute-done.19.refs_4_), channel_id=1, source_target_pairs={{0,4},{4,0},{8,12},{12,8},{16,20},{20,16},{24,28},{28,24},{1,5},{5... | collective-permute-start | bytes 245768 | tf_op jit(solution)/shard_map/ppermute | solution.py:287
  70.4 8.5 %collective-permute-start.30 = (f32[8,64,128]{2,1,0:T(8,128)S(1)}, f32[8,64,128]{2,1,0:T(8,128)S(1)}, u32[]{:S(2)}, u32[]{:S(2)}) collective-permute-start(f32[8,64,128]{2,1,0:T(8,128)S(1)} %get-tuple-element.72), channel_id=1, source_target_pairs={{0,1},{1,0},{2,3},{3,2},{4,5},{5,4},{6,7},{7,6},{8,9},{9,8},{10,11... | collective-permute-start | bytes 786440 | tf_op jit(solution)/shard_map/ppermute | solution.py:287
  70.5 11.2 %collective-permute-start.31 = (f32[8,64,128]{2,1,0:T(8,128)S(1)}, f32[8,64,128]{2,1,0:T(8,128)S(1)}, u32[]{:S(2)}, u32[]{:S(2)}) collective-permute-start(f32[8,64,128]{2,1,0:T(8,128)S(1)} %add.30), channel_id=1, source_target_pairs={{0,2},{1,3},{2,0},{3,1},{4,6},{5,7},{6,4},{7,5},{8,10},{9,11},{10,... | collective-permute-start | bytes 786440 | tf_op jit(solution)/shard_map/ppermute | solution.py:287
  78.4 8.7 %collective-permute-start.29 = (f32[8,64,128]{2,1,0:T(8,128)S(1)}, f32[8,64,128]{2,1,0:T(8,128)S(1)}, u32[]{:S(2)}, u32[]{:S(2)}) collective-permute-start(f32[8,64,128]{2,1,0:T(8,128)S(1)} %add.31), channel_id=1, source_target_pairs={{0,2},{1,3},{2,0},{3,1},{4,6},{5,7},{6,4},{7,5},{8,10},{9,11},{10,... | collective-permute-start | bytes 786440 | tf_op jit(solution)/shard_map/ppermute | solution.py:287
  (9 other events, 57.4 us)

commit v3 on v2

--- a/solution.py
+++ b/solution.py
@@ -9,7 +9,7 @@
 
 blank_flux = 4096.0
 step_size = 0.5
-unroll = 8
+unroll = 20
 group = 8
 vmem_bytes = 40 * 1024 * 1024
 
@@ -43,7 +43,7 @@
     piece = picked.shape[1]
     width = block.shape[2]
     start = pl.multiple_of(place[0], piece)
-    for a in range(angles):
+    for a in range(2):
         total[a] = 0
 
     def slot(j, rank):
@@ -70,9 +70,10 @@
             fetch(t, n)
             col = lax.rem(value, pixel_tiles)
             turn = lax.div(col, own_tiles) ^ place[1]
-            at = total[turn]
-            total[turn] = at + 1
-            at = turn * span + at
+            group_of = lax.div(turn, angles // 2)
+            at = total[group_of]
+            total[group_of] = at + 1
+            at = group_of * span + at
             rank_of[at] = rank
             col_of[at] = turn * own_tiles + lax.rem(col, own_tiles)
             tile_of[at] = n
@@ -87,7 +88,7 @@
         return carry
 
     lax.fori_loop(n, groups * group, fill, 0)
-    for a in range(angles):
+    for a in range(2):
         for extra in range(unroll):
             at = a * span + total[a] + extra
             rank_of[at] = live_total
@@ -107,8 +108,8 @@
     pltpu.make_async_copy(picked, picked, sem).wait()
 
 
-def each(turns, span, total, product, sums, index):
-    for a in turns:
+def each(lists, span, total, product, sums, index):
+    for a in lists:
 
         def step(i, carry, a=a):
             base = a * span + i * unroll
@@ -120,7 +121,7 @@
         lax.fori_loop(0, lax.div(total[a] + unroll - 1, unroll), step, 0)
 
 
-def forward_kernel(turns, sides, span, deep, chained, rank_of, col_of, tile_of, total, place, split, *refs):
+def forward_kernel(turns, lists, sides, span, deep, chained, rank_of, col_of, tile_of, total, place, split, *refs):
     tiles, refs = refs[: sides * len(turns)], refs[sides * len(turns) :]
     before, refs = refs[:chained], refs[chained:]
     *outs, packed, sums = refs
@@ -151,7 +152,7 @@
         )
         return both[:rows_all] + both[rows_all:]
 
-    each(turns, span, total, product, sums, rank_of)
+    each(lists, span, total, product, sums, rank_of)
     if not chained:
         for part, out in enumerate(outs):
             out[...] = sums[:, part * half : (part + 1) * half, :]
@@ -160,21 +161,17 @@
         out[...] = sums[: out.shape[0], k * piece : (k + 1) * piece, :]
 
 
-def backward_kernel(turns, loose, layout, span, rank_of, col_of, tile_of, total, split, *refs):
+def backward_kernel(turns, lists, loose, count, span, rank_of, col_of, tile_of, total, split, *refs):
     *refs, packed, sums = refs
-    refs = list(refs)
-    blocks = [[refs.pop(0) for _ in range(parts)] for parts in layout]
-    outs, count = refs, len(layout)
-    live, _, width = blocks[0][0].shape
-    rows_all = packed.shape[1] // 2
-    piece = rows_all // count
+    blocks, outs = refs[:count], list(refs[count:])
+    live, piece, width = blocks[0].shape
+    rows_all = piece * count
     own_tiles = outs[0].shape[0]
     zeros = jnp.zeros((own_tiles, rows_all, width), f32)
     for k, block in enumerate(blocks):
 
         def fill(i, carry, k=k, block=block):
-            whole = jnp.concatenate([part[i] for part in block], axis=0)
-            high, low = halves(whole)
+            high, low = halves(block[i])
             packed[i, k * piece : (k + 1) * piece, :] = high
             packed[i, rows_all + k * piece : rows_all + (k + 1) * piece, :] = low
             return carry
@@ -188,7 +185,7 @@
         both = both[:rows_all] + both[rows_all:]
         return both[:, :width] + both[:, width:]
 
-    each(turns, span, total, product, sums, col_of)
+    each(lists, span, total, product, sums, col_of)
     for a in turns:
         tiles = slice(a * own_tiles, (a + 1) * own_tiles)
         if a not in loose:
@@ -198,32 +195,17 @@
             outs.pop(0)[...] = sums[tiles, k * piece : (k + 1) * piece, :]
 
 
-def add_kernel(cuts, count, *refs):
-    terms, outs = refs[:count], refs[count:]
-    for first, out in zip(cuts, outs):
-        rows = out.shape[1]
-        total = None
-        for term in terms:
-            value = term[...] if term.shape[1] == rows else term[:, first : first + rows, :]
-            total = value if total is None else total + value
-        out[...] = total
-
-
-def residual_kernel(cuts, counts, *refs):
-    terms, outs = refs[: -len(cuts)], refs[-len(cuts) :]
-    height = counts.shape[1]
-    summed = 0.0
-    parts = [term[...] for term in terms if term.shape[1] == height]
-    for part in parts:
-        summed = summed + part
-    short = [term[...] for term in terms if term.shape[1] != height]
-    if short:
-        upper = sum(short[:-1])
-        summed = summed + jnp.concatenate([upper, short[-1]], axis=1)
+def add_kernel(left, right, out):
+    out[...] = left[...] + right[...]
+
+
+def residual_kernel(counts, *refs):
+    *terms, out = refs
+    summed = terms[0][...]
+    for term in terms[1:]:
+        summed = summed + term[...]
     measured = counts[...].astype(f32)
-    value = measured / blank_flux * (summed - jnp.log(blank_flux / measured))
-    for first, out in zip(cuts, outs):
-        out[...] = value[:, first : first + out.shape[1], :]
+    out[...] = measured / blank_flux * (summed - jnp.log(blank_flux / measured))
 
 
 def update_kernel(parts, deep, place, volume, *refs):
@@ -244,7 +226,7 @@
         copy.wait()
 
 
-def call(kernel, out_shape, in_specs, scratch=(), out_specs=None, traffic=None):
+def call(kernel, out_shape, in_specs, scratch=(), out_specs=None):
     if out_specs is None:
         out_specs = jax.tree.map(lambda leaf: vmem, out_shape)
     return pl.pallas_call(
@@ -254,7 +236,6 @@
         out_specs=out_specs,
         scratch_shapes=list(scratch),
         compiler_params=params,
-        cost_estimate=None if traffic is None else pl.CostEstimate(flops=0, bytes_accessed=traffic, transcendentals=0),
     )
 
 
@@ -262,13 +243,8 @@
     return pltpu.with_memory_space_constraint(value, pltpu.HBM)
 
 
-def add(cuts, rows, *terms):
-    live, _, width = terms[0].shape
-    return call(
-        functools.partial(add_kernel, cuts, len(terms)),
-        (jax.ShapeDtypeStruct((live, rows, width), f32),) * len(cuts),
-        [vmem] * len(terms),
-    )(*terms)
+def add(left, right):
+    return call(add_kernel, jax.ShapeDtypeStruct(left.shape, f32), [vmem] * 2)(left, right)
 
 
 def shards(volume, projector, tile_ids, counts, ray_counts):
@@ -311,15 +287,14 @@
 
     span = tile_count + unroll
     stored = -(-tile_count // group) * group
-    heavy = projector.size * 4
-    listed = jax.ShapeDtypeStruct((ang * span,), i32)
+    listed = jax.ShapeDtypeStruct((2 * span,), i32)
     rank_of, col_of, tile_of, total, picked, split = call(
         functools.partial(front_kernel, own_tiles, ang, live),
         (
             listed,
             listed,
             listed,
-            jax.ShapeDtypeStruct((ang,), i32),
+            jax.ShapeDtypeStruct((2,), i32),
             jax.ShapeDtypeStruct((live, piece, rays), i32),
             pltpu.VMEM((stored, rays, 2 * width), bf16),
         ),
@@ -334,16 +309,17 @@
             pltpu.SemaphoreType.DMA((2,)),
         ],
         (smem, smem, smem, smem, vmem, vmem),
-        None,
     )(in_hbm(tile_ids), in_hbm(ray_counts), place, in_hbm(counts), in_hbm(projector))
     lists = (rank_of, col_of, tile_of)
     rows = jax.ShapeDtypeStruct((live, piece, rays), f32)
-    columns = jax.ShapeDtypeStruct((own_tiles, half, width), f32)
+
+    def lists_of(turns):
+        return sorted({a // (ang // 2) for a in turns})
 
     def forward(turns, sides, before=()):
         count = len(sides)
         return call(
-            functools.partial(forward_kernel, turns, count, span, deep, len(before)),
+            functools.partial(forward_kernel, turns, lists_of(turns), count, span, deep, len(before)),
             (rows,) * deep if before else (pltpu.VMEM((live + 1, half, rays), f32),) * count,
             [smem] * 5 + [vmem] * (1 + count * len(turns) + len(before)),
             [
@@ -356,7 +332,7 @@
         count = len(part)
         height = piece * count
         made = call(
-            functools.partial(backward_kernel, turns, loose, [len(blocks[spot]) for spot in part], span),
+            functools.partial(backward_kernel, turns, lists_of(turns), loose, count, span),
             sum(
                 (
                     (jax.ShapeDtypeStruct((own_tiles, piece, width), f32),) * count
@@ -366,63 +342,34 @@
                 ),
                 (),
             ),
-            [smem] * 4 + [vmem] * (1 + sum(len(blocks[spot]) for spot in part)),
+            [smem] * 4 + [vmem] * (1 + count),
             [
                 pltpu.VMEM((live + 1, 2 * height, rays), bf16),
                 pltpu.VMEM((pixel_tiles + 1, height, width), f32),
             ],
-        )(*lists, total, split, *[block for spot in part for block in blocks[spot]])
+        )(*lists, total, split, *[blocks[spot] for spot in part])
         made = list(made)
         return {a: [made.pop(0) for _ in range(count if a in loose else 1)] for a in turns}
 
     turns = tuple(range(ang))
-    early = tuple(k for k in turns if k < 2)
-    late = turns[2:]
+    early, late = turns[: ang // 2], turns[ang // 2 :]
+    if ang > 4:
+        far_tiles, near_tiles = relay(far_tiles, total), relay(near_tiles, total)
     far_sums, near_sums = forward(early, (far_tiles, near_tiles))
-    far_tiles = relay(far_tiles, total)
-    near_tiles = relay(near_tiles, near_sums)
+    if ang <= 4:
+        far_tiles, near_tiles = relay(far_tiles, total), relay(near_tiles, near_sums)
     far_parts = forward(late, (far_tiles,), (far_sums,))
-    order = [k for k in (3, 2, 1) if k < deep] + list(range(4, deep)) + [0]
+    order = list(range(deep - 1, -1, -1))
     crossed = {k: across(far_parts[k], "pix", 1) for k in order}
     near_parts = forward(late, (near_tiles,), (near_sums,))
-    def residual(cuts, heights, *terms):
-        return call(
-            functools.partial(residual_kernel, cuts),
-            tuple(jax.ShapeDtypeStruct((live, height, rays), f32) for height in heights),
-            [vmem] * (1 + len(terms)),
-        )(picked, *terms)
-
     side_of = lambda value, k: across(value, "pix", 2 * k)
-    cut = piece // 2
-    if deep == 4:
-        first, rest = add((0, cut), cut, near_parts[3], crossed[3])
-        came = [side_of(first, 3)]
-        passed = side_of(rest, 1)
-        (first,) = add((0,), cut, near_parts[2], crossed[2])
-        came.append(side_of(first, 2))
-        (rest,) = add((cut,), cut, near_parts[2], crossed[2], after(passed, came[0]))
-        rest = side_of(rest, 2)
-        (one,) = add((0,), piece, after(near_parts[1], first), crossed[1])
-        whole_one = side_of(one, 1)
-        own, first, last = residual(
-            (0, 0, cut), (piece, cut, cut), near_parts[0], crossed[0], *came, rest, whole_one
-        )
-        last_two = side_of(last, 2)
-        near_one = side_of(own, 1)
-        first_three = side_of(first, 3)
-        first_two = side_of(first, 2)
-        last_three = side_of(last_two, 1)
-        near_blocks = [(own,), (near_one,), (first_two, last_two), (first_three, last_three)]
-    else:
-        came = [side_of(add((0,), piece, near_parts[k], crossed[k])[0], k) for k in order if k]
-        (own,) = residual((0,), (piece,), near_parts[0], crossed[0], *came)
-        near_blocks = [(own,)] + [(side_of(own, k),) for k in range(1, deep)]
-    far_blocks = [tuple(across(part, "pix", 1) for part in parts) for parts in near_blocks]
-    blocks = {(0, k): parts for k, parts in enumerate(near_blocks)}
-    blocks.update({(1, k): parts for k, parts in enumerate(far_blocks)})
+    came = [side_of(add(near_parts[k], crossed[k]), k) for k in order if k]
+    own = call(residual_kernel, rows, [vmem] * (3 + len(came)))(picked, near_parts[0], crossed[0], *came)
+    near_blocks = [own] + [side_of(own, k) for k in range(1, deep)]
+    blocks = {(0, k): block for k, block in enumerate(near_blocks)}
     arrival = [k for k in (1, 3, 2) if k < deep] + list(range(4, deep))
-    near_all = [(0, k) for k in [0] + arrival]
-    far_all = [(1, k) for k in [0] + arrival]
+    for k in [0] + arrival[:-1]:
+        blocks[1, k] = across(near_blocks[k], "pix", 1)
     top = angle_bits[-1]
     lower, upper = turns[:top], turns[top:]
 
@@ -452,15 +399,22 @@
             compiler_params=params,
         )(place, volume, *terms, *started)
 
-    made = backward(turns, near_all, total)
-    up_near = fold({k: made[k] for k in upper})
-    low_near = fold({k: made[k] for k in lower})
-    up_far = fold(backward(upper, far_all, total))
-    low_far = fold(backward(lower, far_all, after(total, up_near, up_far)))
-    came_near = across(up_near, "ang", top)
-    came_far = across(up_far, "ang", top)
-    begun = update((near_all,), (low_near, came_near))
-    return update((far_all,), (low_far, came_far), begun)
+    head = [(0, 0), (0, arrival[0]), (0, arrival[1]), (1, 0)]
+    tail = [(1, arrival[-1])]
+    middle = [(side, k) for k in arrival for side in range(2) if (side, k) not in head + tail]
+    made = backward(turns, head, total, upper[1::2])
+    blocks[tail[0]] = across(after(near_blocks[arrival[-1]], made[0][0]), "pix", 1)
+    low_head, up_head = fold({k: made[k] for k in lower}), fold({k: made[k] for k in upper})
+    came_head = across(up_head, "ang", top)
+    made = backward(turns, middle, total)
+    ties = [blocks[tail[0]]]
+    low_middle, up_middle = fold({k: made[k] for k in lower}, *ties), fold({k: made[k] for k in upper}, *ties)
+    came_middle = across(up_middle, "ang", top)
+    made = backward(turns, tail, after(total, up_head, up_middle))
+    low_tail, up_tail = fold({k: made[k] for k in lower}), fold({k: made[k] for k in upper})
+    came_tail = across(up_tail, "ang", top)
+    begun = update((head,), (low_head, came_head))
+    return update((middle, tail), (low_middle, came_middle, low_tail, came_tail), begun)
 
 
 def solution(mesh):

time: 87.9 us -> 83.2 us (0.947); the launches traced: 88.5 us -> 82 us
  starting transfers between devices: 34.5 us -> 27.8 us
  waiting for transfers between devices: 21.6 us -> 24.8 us
  Pallas kernels: 30.9 us -> 27.8 us
    ppermute x32, starting transfers between devices: 34.5 us -> 27.8 us  [shards(): lax.ppermute(value, axis, [(d, d ^ flip) for d in range(lax.axis_size(axi...]
    ppermute x32, waiting for transfers between devices: 21.6 us -> 24.8 us  [shards(): lax.ppermute(value, axis, [(d, d ^ flip) for d in range(lax.axis_size(axi...]
    pallas_call x11 -> x10, Pallas kernels: 21.8 us -> 18.8 us  [the longest x3 10 us: backward(): call(functools.partial(backward_kernel, turns, lists_of(turns), loose, co...]
  transfers between devices with their start and end apart: 32 -> 32, of which waited for: 9 -> 13; matrix products, arithmetic and copies ran while one was open for 0% -> 0% of each run, Pallas kernels for 33% -> 32%
where the time goes in v3:
time: 83.2 us; the launch traced here: 82 us
  starting transfers between devices  27.8 us (33%)
  Pallas kernels  27.8 us (33%)
  waiting for transfers between devices  24.8 us (30%)
  local copies, waits for them, and re-layouts  1.07 us (1%)
    ppermute x32, starting transfers between devices, shards(): lax.ppermute(value, axis, [(d, d ^ flip) for d in range(lax.axis_size(axi...  27.8 us
    ppermute x32, waiting for transfers between devices, shards(): lax.ppermute(value, axis, [(d, d ^ flip) for d in range(lax.axis_size(axi...  24.8 us
    pallas_call x3, Pallas kernels, backward(): call(functools.partial(backward_kernel, turns, lists_of(turns), loose, co...  10 us
    pallas_call x3, Pallas kernels, forward(): call(functools.partial(forward_kernel, turns, lists_of(turns), count, spa...  8.65 us
    pallas_call x1, Pallas kernels, shards(): call(functools.partial(front_kernel, own_tiles, ang, live), (listed, list...  6.39 us
    pallas_call x2, Pallas kernels, update(): pl.pallas_call(functools.partial(update_kernel, parts, deep), out_shape=j...  2.64 us
  transfers between devices with their start and end apart: 32, of which 13 were waited for; matrix products, arithmetic and copies ran while one was open for 0% of the time, Pallas kernels for 32%

profile of v3, /device:TPU:0, one launch (start us, length us, event | category | flops | bytes accessed | tf_op | source)
XLA Modules:
  0.0 82.0 jit_solution(3751862231657861629)
XLA Ops:
  1.1 3.0 %collective-permute-start.4 = (f32[8,64,128]{2,1,0:T(8,128)S(1)}, f32[8,64,128]{2,1,0:T(8,128)S(1)}, u32[]{:S(2)}, u32[]{:S(2)}) collective-permute-start(f32[8,64,128]{2,1,0:T(8,128)S(1)} %get-tuple-element.79.refs_0_), channel_id=1, source_target_pairs={{0,2},{1,3},{2,0},{3,1},{4,6},{5,7},{6,4},{7,5},{8,10},{9,11},{10,... | collective-permute-start | bytes 786440 | tf_op jit(solution)/shard_map/ppermute | solution.py:263
  4.7 6.4 %shard_map.55 = (s32[360]{0:T(512)S(1)}, s32[360]{0:T(512)S(1)}, s32[360]{0:T(512)S(1)}, s32[2]{0:T(128)S(1)}, s32[20,16,128]{2,1,0:T(8,128)S(1)}, /*index=5*/bf16[160,128,256]{2,1,0:T(8,128)(2,1)S(1)}) custom-call(s32[160]{0:T(256)} %ids_hbm.1, s32[1,8]{1,0:T(1,128)} %rays_hbm.1, s32[4]{0:T(128)S(1)} %pad_add_fusion.place, s32[32,128,128]{2,1,0:T(8,128)} %counts.1, ...), custom_call_target="tpu_custom_call" | custom-call | tf_op jit(solution)/shard_map/pallas_call | solution.py:291
  11.3 3.7 %shard_map.56 = (f32[21,64,128]{2,1,0:T(8,128)S(1)}, f32[21,64,128]{2,1,0:T(8,128)S(1)}) custom-call(s32[360]{0:T(512)S(1)} %get-tuple-element.42.rank_of, s32[360]{0:T(512)S(1)} %get-tuple-element.43.col_of, s32[360]{0:T(512)S(1)} %get-tuple-element.44.tile_of, s32[2]{0:T(128)S(1)} %get-tuple-element.73.total, s32[4]{0:T(128)S(1)} %pad_add_fusion.place, ...), custom_call_target="tpu_custom_call" | custom-call | tf_op jit(solution)/shard_map/pallas_call | solution.py:321
  16.0 2.5 %shard_map.58 = (f32[20,16,128]{2,1,0:T(8,128)S(1)}, f32[20,16,128]{2,1,0:T(8,128)S(1)}, f32[20,16,128]{2,1,0:T(8,128)S(1)}, f32[20,16,128]{2,1,0:T(8,128)S(1)}) custom-call(s32[360]{0:T(512)S(1)} %get-tuple-element.42.rank_of, s32[360]{0:T(512)S(1)} %get-tuple-element.43.col_of, s32[360]{0:T(512)S(1)} %get-tuple-element.44.tile_of, ...), custom_call_target="tpu_custom_call" | custom-call | tf_op jit(solution)/shard_map/pallas_call | solution.py:321
  18.5 1.8 %collective-permute-start.7 = (f32[20,16,128]{2,1,0:T(8,128)S(1)}, f32[20,16,128]{2,1,0:T(8,128)S(1)}, u32[]{:S(2)}, u32[]{:S(2)}) collective-permute-start(f32[20,16,128]{2,1,0:T(8,128)S(1)} %get-tuple-element.55), channel_id=1, source_target_pairs={{0,4},{4,0},{8,12},{12,8},{16,20},{20,16},{24,28},{28,24},{1,5},{5... | collective-permute-start | bytes 491528 | tf_op jit(solution)/shard_map/ppermute | solution.py:263
  20.6 1.7 %collective-permute-start.11 = (f32[20,16,128]{2,1,0:T(8,128)S(1)}, f32[20,16,128]{2,1,0:T(8,128)S(1)}, u32[]{:S(2)}, u32[]{:S(2)}) collective-permute-start(f32[20,16,128]{2,1,0:T(8,128)S(1)} %get-tuple-element.59), channel_id=1, source_target_pairs={{0,4},{4,0},{8,12},{12,8},{16,20},{20,16},{24,28},{28,24},{1,5},{5... | collective-permute-start | bytes 491528 | tf_op jit(solution)/shard_map/ppermute | solution.py:263
  22.6 2.5 %shard_map.57 = (f32[20,16,128]{2,1,0:T(8,128)S(1)}, f32[20,16,128]{2,1,0:T(8,128)S(1)}, f32[20,16,128]{2,1,0:T(8,128)S(1)}, f32[20,16,128]{2,1,0:T(8,128)S(1)}) custom-call(s32[360]{0:T(512)S(1)} %get-tuple-element.42.rank_of, s32[360]{0:T(512)S(1)} %get-tuple-element.43.col_of, s32[360]{0:T(512)S(1)} %get-tuple-element.44.tile_of, ...), custom_call_target="tpu_custom_call" | custom-call | tf_op jit(solution)/shard_map/pallas_call | solution.py:321
  25.6 3.9 %collective-permute-start.8 = (f32[20,16,128]{2,1,0:T(8,128)S(1)}, f32[20,16,128]{2,1,0:T(8,128)S(1)}, u32[]{:S(2)}, u32[]{:S(2)}) collective-permute-start(f32[20,16,128]{2,1,0:T(8,128)S(1)} %shard_map.59), channel_id=1, source_target_pairs={{0,24},{4,28},{8,16},{12,20},{16,8},{20,12},{24,0},{28,4},{1,25},{... | collective-permute-start | bytes 491528 | tf_op jit(solution)/shard_map/ppermute | solution.py:263
  29.5 2.5 %collective-permute-start.10 = (f32[20,16,128]{2,1,0:T(8,128)S(1)}, f32[20,16,128]{2,1,0:T(8,128)S(1)}, u32[]{:S(2)}, u32[]{:S(2)}) collective-permute-start(f32[20,16,128]{2,1,0:T(8,128)S(1)} %shard_map.60), channel_id=1, source_target_pairs={{0,16},{4,20},{8,24},{12,28},{16,0},{20,4},{24,8},{28,12},{1,17},{... | collective-permute-start | bytes 491528 | tf_op jit(solution)/shard_map/ppermute | solution.py:263
  32.6 1.4 %collective-permute-start.12 = (f32[20,16,128]{2,1,0:T(8,128)S(1)}, f32[20,16,128]{2,1,0:T(8,128)S(1)}, u32[]{:S(2)}, u32[]{:S(2)}) collective-permute-start(f32[20,16,128]{2,1,0:T(8,128)S(1)} %shard_map.61), channel_id=1, source_target_pairs={{0,8},{4,12},{8,0},{12,4},{16,24},{20,28},{24,16},{28,20},{1,9},{5... | collective-permute-start | bytes 491528 | tf_op jit(solution)/shard_map/ppermute | solution.py:263
  34.0 1.7 %collective-permute-done.6.refs_1_ = f32[20,16,128]{2,1,0:T(8,128)S(1)} collective-permute-done((f32[20,16,128]{2,1,0:T(8,128)S(1)}, f32[20,16,128]{2,1,0:T(8,128)S(1)}, u32[]{:S(2)}, u32[]{:S(2)}) %collective-permute-start.6) | collective-permute-done | bytes 163872 | tf_op jit(solution)/shard_map/ppermute | solution.py:263
  35.7 7.5 %collective-permute-done.10.refs_3_ = f32[20,16,128]{2,1,0:T(8,128)S(1)} collective-permute-done((f32[20,16,128]{2,1,0:T(8,128)S(1)}, f32[20,16,128]{2,1,0:T(8,128)S(1)}, u32[]{:S(2)}, u32[]{:S(2)}) %collective-permute-start.10) | collective-permute-done | bytes 163872 | tf_op jit(solution)/shard_map/ppermute | solution.py:263
  43.4 2.3 %collective-permute-start.15 = (f32[20,16,128]{2,1,0:T(8,128)S(1)}, f32[20,16,128]{2,1,0:T(8,128)S(1)}, u32[]{:S(2)}, u32[]{:S(2)}) collective-permute-start(f32[20,16,128]{2,1,0:T(8,128)S(1)} %shard_map.62.refs_0_), channel_id=1, source_target_pairs={{0,24},{4,28},{8,16},{12,20},{16,8},{20,12},{24,0},{28,4},{1,25},{... | collective-permute-start | bytes 491528 | tf_op jit(solution)/shard_map/ppermute | solution.py:263
  45.7 1.5 %collective-permute-start.18 = (f32[20,16,128]{2,1,0:T(8,128)S(1)}, f32[20,16,128]{2,1,0:T(8,128)S(1)}, u32[]{:S(2)}, u32[]{:S(2)}) collective-permute-start(f32[20,16,128]{2,1,0:T(8,128)S(1)} %shard_map.62.refs_0_), channel_id=1, source_target_pairs={{0,4},{4,0},{8,12},{12,8},{16,20},{20,16},{24,28},{28,24},{1,5},{5... | collective-permute-start | bytes 491528 | tf_op jit(solution)/shard_map/ppermute | solution.py:263
  48.1 3.2 %collective-permute-done.13.refs_1_ = f32[20,16,128]{2,1,0:T(8,128)S(1)} collective-permute-done((f32[20,16,128]{2,1,0:T(8,128)S(1)}, f32[20,16,128]{2,1,0:T(8,128)S(1)}, u32[]{:S(2)}, u32[]{:S(2)}) %collective-permute-start.13) | collective-permute-done | bytes 163872 | tf_op jit(solution)/shard_map/ppermute | solution.py:263
  51.6 2.4 %collective-permute-done.15.refs_2_ = f32[20,16,128]{2,1,0:T(8,128)S(1)} collective-permute-done((f32[20,16,128]{2,1,0:T(8,128)S(1)}, f32[20,16,128]{2,1,0:T(8,128)S(1)}, u32[]{:S(2)}, u32[]{:S(2)}) %collective-permute-start.15) | collective-permute-done | bytes 163872 | tf_op jit(solution)/shard_map/ppermute | solution.py:263
  55.3 4.0 %shard_map.64 = (f32[8,64,128]{2,1,0:T(8,128)S(1)}, f32[8,64,128]{2,1,0:T(8,128)S(1)}, f32[8,64,128]{2,1,0:T(8,128)S(1)}, f32[8,16,128]{2,1,0:T(8,128)S(1)}, f32...) custom-call(s32[360]{0:T(512)S(1)} %get-tuple-element.42.rank_of, ...), custom_call_target="tpu_custom_call" | custom-call | tf_op jit(solution)/shard_map/pallas_call | solution.py:334
  59.2 1.6 %collective-permute-done.17.refs_2_ = f32[20,16,128]{2,1,0:T(8,128)S(1)} collective-permute-done((f32[20,16,128]{2,1,0:T(8,128)S(1)}, f32[20,16,128]{2,1,0:T(8,128)S(1)}, u32[]{:S(2)}, u32[]{:S(2)}) %collective-permute-start.17) | collective-permute-done | bytes 163872 | tf_op jit(solution)/shard_map/ppermute | solution.py:263
  62.6 3.4 %shard_map.63 = (f32[8,48,128]{2,1,0:T(8,128)S(1)}, f32[8,48,128]{2,1,0:T(8,128)S(1)}, f32[8,48,128]{2,1,0:T(8,128)S(1)}, f32[8,48,128]{2,1,0:T(8,128)S(1)}) custom-call(s32[360]{0:T(512)S(1)} %get-tuple-element.42.rank_of, s32[360]{0:T(512)S(1)} %get-tuple-element.43.col_of, s32[360]{0:T(512)S(1)} %get-tuple-element.44.tile_of, ...), custom_call_target="tpu_custom_call" | custom-call | tf_op jit(solution)/shard_map/pallas_call | solution.py:334
  66.7 1.4 %collective-permute-start.31 = (f32[8,64,128]{2,1,0:T(8,128)S(1)}, f32[8,64,128]{2,1,0:T(8,128)S(1)}, u32[]{:S(2)}, u32[]{:S(2)}) collective-permute-start(f32[8,64,128]{2,1,0:T(8,128)S(1)} %maximum_add_fusion), channel_id=1, source_target_pairs={{0,2},{1,3},{2,0},{3,1},{4,6},{5,7},{6,4},{7,5},{8,10},{9,11},{10,... | collective-permute-start | bytes 786440 | tf_op jit(solution)/shard_map/ppermute | solution.py:263
  69.4 2.6 %shard_map.65 = (f32[8,16,128]{2,1,0:T(8,128)S(1)}, f32[8,16,128]{2,1,0:T(8,128)S(1)}, f32[8,16,128]{2,1,0:T(8,128)S(1)}, f32[8,16,128]{2,1,0:T(8,128)S(1)}) custom-call(s32[360]{0:T(512)S(1)} %get-tuple-element.42.rank_of, s32[360]{0:T(512)S(1)} %get-tuple-element.43.col_of, s32[360]{0:T(512)S(1)} %get-tuple-element.44.tile_of, ...), custom_call_target="tpu_custom_call" | custom-call | tf_op jit(solution)/shard_map/pallas_call | solution.py:334
  74.5 1.5 %collective-permute-done.31.refs_1_ = f32[8,64,128]{2,1,0:T(8,128)S(1)} collective-permute-done((f32[8,64,128]{2,1,0:T(8,128)S(1)}, f32[8,64,128]{2,1,0:T(8,128)S(1)}, u32[]{:S(2)}, u32[]{:S(2)}) %collective-permute-start.31) | collective-permute-done | bytes 262176 | tf_op jit(solution)/shard_map/ppermute | solution.py:263
  75.9 1.3 %shard_map.66.refs_4_ = f32[8,128,128]{2,1,0:T(8,128)} custom-call(s32[4]{0:T(128)S(1)} %pad_add_fusion.place, f32[8,128,128]{2,1,0:T(8,128)S(1)} %copy-done, f32[8,64,128]{2,1,0:T(8,128)S(1)} %add.41.refs_0_, f32[8,64,128]{2,1,0:T(8,128)S(1)} %collective-permute-done.31.refs_1_), custom_call_target="tpu_custom_call" | custom-call | tf_op jit(solution)/shard_map/pallas_call | solution.py:392
  77.4 3.3 %collective-permute-done.29.refs_3_ = f32[8,16,128]{2,1,0:T(8,128)S(1)} collective-permute-done((f32[8,16,128]{2,1,0:T(8,128)S(1)}, f32[8,16,128]{2,1,0:T(8,128)S(1)}, u32[]{:S(2)}, u32[]{:S(2)}) %collective-permute-start.29) | collective-permute-done | bytes 65568 | tf_op jit(solution)/shard_map/ppermute | solution.py:263
  (63 shorter events, 14.9 us)
Async XLA Ops:
  1.1 10.2 %collective-permute-start.4 = (f32[8,64,128]{2,1,0:T(8,128)S(1)}, f32[8,64,128]{2,1,0:T(8,128)S(1)}, u32[]{:S(2)}, u32[]{:S(2)}) collective-permute-start(f32[8,64,128]{2,1,0:T(8,128)S(1)} %get-tuple-element.79.refs_0_), channel_id=1, source_target_pairs={{0,2},{1,3},{2,0},{3,1},{4,6},{5,7},{6,4},{7,5},{8,10},{9,11},{10,... | collective-permute-start | bytes 786440 | tf_op jit(solution)/shard_map/ppermute | solution.py:263
  4.1 7.2 %collective-permute-start.1 = (f32[8,64,128]{2,1,0:T(8,128)S(1)}, f32[8,64,128]{2,1,0:T(8,128)S(1)}, u32[]{:S(2)}, u32[]{:S(2)}) collective-permute-start(f32[8,64,128]{2,1,0:T(8,128)S(1)} %get-tuple-element.79.refs_0_), channel_id=1, source_target_pairs={{0,1},{1,0},{2,3},{3,2},{4,5},{5,4},{6,7},{7,6},{8,9},{9,8},{10,11... | collective-permute-start | bytes 786440 | tf_op jit(solution)/shard_map/ppermute | solution.py:263
  4.1 11.9 %collective-permute-start = (f32[8,64,128]{2,1,0:T(8,128)S(1)}, f32[8,64,128]{2,1,0:T(8,128)S(1)}, u32[]{:S(2)}, u32[]{:S(2)}) collective-permute-start(f32[8,64,128]{2,1,0:T(8,128)S(1)} %get-tuple-element.80.refs_2_), channel_id=1, source_target_pairs={{0,2},{1,3},{2,0},{3,1},{4,6},{5,7},{6,4},{7,5},{8,10},{9,11},{10,... | collective-permute-start | bytes 786440 | tf_op jit(solution)/shard_map/ppermute | solution.py:263
  4.3 7.1 %collective-permute-start.2 = (f32[8,64,128]{2,1,0:T(8,128)S(1)}, f32[8,64,128]{2,1,0:T(8,128)S(1)}, u32[]{:S(2)}, u32[]{:S(2)}) collective-permute-start(f32[8,64,128]{2,1,0:T(8,128)S(1)} %get-tuple-element.80.refs_2_), channel_id=1, source_target_pairs={{0,1},{1,0},{2,3},{3,2},{4,5},{5,4},{6,7},{7,6},{8,9},{9,8},{10,11... | collective-permute-start | bytes 786440 | tf_op jit(solution)/shard_map/ppermute | solution.py:263
  16.0 6.6 %collective-permute-start.3 = (f32[8,64,128]{2,1,0:T(8,128)S(1)}, f32[8,64,128]{2,1,0:T(8,128)S(1)}, u32[]{:S(2)}, u32[]{:S(2)}) collective-permute-start(f32[8,64,128]{2,1,0:T(8,128)S(1)} %collective-permute-done.refs_0_), channel_id=1, source_target_pairs={{0,1},{1,0},{2,3},{3,2},{4,5},{5,4},{6,7},{7,6},{8,9},{9,8},{10,11... | collective-permute-start | bytes 786440 | tf_op jit(solution)/shard_map/ppermute | solution.py:263
  18.5 7.1 %collective-permute-start.7 = (f32[20,16,128]{2,1,0:T(8,128)S(1)}, f32[20,16,128]{2,1,0:T(8,128)S(1)}, u32[]{:S(2)}, u32[]{:S(2)}) collective-permute-start(f32[20,16,128]{2,1,0:T(8,128)S(1)} %get-tuple-element.55), channel_id=1, source_target_pairs={{0,4},{4,0},{8,12},{12,8},{16,20},{20,16},{24,28},{28,24},{1,5},{5... | collective-permute-start | bytes 491528 | tf_op jit(solution)/shard_map/ppermute | solution.py:263
  20.3 9.2 %collective-permute-start.9 = (f32[20,16,128]{2,1,0:T(8,128)S(1)}, f32[20,16,128]{2,1,0:T(8,128)S(1)}, u32[]{:S(2)}, u32[]{:S(2)}) collective-permute-start(f32[20,16,128]{2,1,0:T(8,128)S(1)} %get-tuple-element.57), channel_id=1, source_target_pairs={{0,4},{4,0},{8,12},{12,8},{16,20},{20,16},{24,28},{28,24},{1,5},{5... | collective-permute-start | bytes 491528 | tf_op jit(solution)/shard_map/ppermute | solution.py:263
  20.6 12.0 %collective-permute-start.11 = (f32[20,16,128]{2,1,0:T(8,128)S(1)}, f32[20,16,128]{2,1,0:T(8,128)S(1)}, u32[]{:S(2)}, u32[]{:S(2)}) collective-permute-start(f32[20,16,128]{2,1,0:T(8,128)S(1)} %get-tuple-element.59), channel_id=1, source_target_pairs={{0,4},{4,0},{8,12},{12,8},{16,20},{20,16},{24,28},{28,24},{1,5},{5... | collective-permute-start | bytes 491528 | tf_op jit(solution)/shard_map/ppermute | solution.py:263
  22.3 13.4 %collective-permute-start.6 = (f32[20,16,128]{2,1,0:T(8,128)S(1)}, f32[20,16,128]{2,1,0:T(8,128)S(1)}, u32[]{:S(2)}, u32[]{:S(2)}) collective-permute-start(f32[20,16,128]{2,1,0:T(8,128)S(1)} %get-tuple-element.53), channel_id=1, source_target_pairs={{0,4},{4,0},{8,12},{12,8},{16,20},{20,16},{24,28},{28,24},{1,5},{5... | collective-permute-start | bytes 491528 | tf_op jit(solution)/shard_map/ppermute | solution.py:263
  25.6 10.1 %collective-permute-start.8 = (f32[20,16,128]{2,1,0:T(8,128)S(1)}, f32[20,16,128]{2,1,0:T(8,128)S(1)}, u32[]{:S(2)}, u32[]{:S(2)}) collective-permute-start(f32[20,16,128]{2,1,0:T(8,128)S(1)} %shard_map.59), channel_id=1, source_target_pairs={{0,24},{4,28},{8,16},{12,20},{16,8},{20,12},{24,0},{28,4},{1,25},{... | collective-permute-start | bytes 491528 | tf_op jit(solution)/shard_map/ppermute | solution.py:263
  29.5 13.7 %collective-permute-start.10 = (f32[20,16,128]{2,1,0:T(8,128)S(1)}, f32[20,16,128]{2,1,0:T(8,128)S(1)}, u32[]{:S(2)}, u32[]{:S(2)}) collective-permute-start(f32[20,16,128]{2,1,0:T(8,128)S(1)} %shard_map.60), channel_id=1, source_target_pairs={{0,16},{4,20},{8,24},{12,28},{16,0},{20,4},{24,8},{28,12},{1,17},{... | collective-permute-start | bytes 491528 | tf_op jit(solution)/shard_map/ppermute | solution.py:263
  32.6 10.6 %collective-permute-start.12 = (f32[20,16,128]{2,1,0:T(8,128)S(1)}, f32[20,16,128]{2,1,0:T(8,128)S(1)}, u32[]{:S(2)}, u32[]{:S(2)}) collective-permute-start(f32[20,16,128]{2,1,0:T(8,128)S(1)} %shard_map.61), channel_id=1, source_target_pairs={{0,8},{4,12},{8,0},{12,4},{16,24},{20,28},{24,16},{28,20},{1,9},{5... | collective-permute-start | bytes 491528 | tf_op jit(solution)/shard_map/ppermute | solution.py:263
  43.4 7.9 %collective-permute-start.13 = (f32[20,16,128]{2,1,0:T(8,128)S(1)}, f32[20,16,128]{2,1,0:T(8,128)S(1)}, u32[]{:S(2)}, u32[]{:S(2)}) collective-permute-start(f32[20,16,128]{2,1,0:T(8,128)S(1)} %shard_map.62.refs_0_), channel_id=1, source_target_pairs={{0,8},{4,12},{8,0},{12,4},{16,24},{20,28},{24,16},{28,20},{1,9},{5... | collective-permute-start | bytes 491528 | tf_op jit(solution)/shard_map/ppermute | solution.py:263
  43.4 10.6 %collective-permute-start.15 = (f32[20,16,128]{2,1,0:T(8,128)S(1)}, f32[20,16,128]{2,1,0:T(8,128)S(1)}, u32[]{:S(2)}, u32[]{:S(2)}) collective-permute-start(f32[20,16,128]{2,1,0:T(8,128)S(1)} %shard_map.62.refs_0_), channel_id=1, source_target_pairs={{0,24},{4,28},{8,16},{12,20},{16,8},{20,12},{24,0},{28,4},{1,25},{... | collective-permute-start | bytes 491528 | tf_op jit(solution)/shard_map/ppermute | solution.py:263
  45.7 9.5 %collective-permute-start.18 = (f32[20,16,128]{2,1,0:T(8,128)S(1)}, f32[20,16,128]{2,1,0:T(8,128)S(1)}, u32[]{:S(2)}, u32[]{:S(2)}) collective-permute-start(f32[20,16,128]{2,1,0:T(8,128)S(1)} %shard_map.62.refs_0_), channel_id=1, source_target_pairs={{0,4},{4,0},{8,12},{12,8},{16,20},{20,16},{24,28},{28,24},{1,5},{5... | collective-permute-start | bytes 491528 | tf_op jit(solution)/shard_map/ppermute | solution.py:263
  47.2 13.6 %collective-permute-start.17 = (f32[20,16,128]{2,1,0:T(8,128)S(1)}, f32[20,16,128]{2,1,0:T(8,128)S(1)}, u32[]{:S(2)}, u32[]{:S(2)}) collective-permute-start(f32[20,16,128]{2,1,0:T(8,128)S(1)} %shard_map.62.refs_0_), channel_id=1, source_target_pairs={{0,16},{4,20},{8,24},{12,28},{16,0},{20,4},{24,8},{28,12},{1,17},{... | collective-permute-start | bytes 491528 | tf_op jit(solution)/shard_map/ppermute | solution.py:263
  51.2 10.8 %collective-permute-start.14 = (f32[20,16,128]{2,1,0:T(8,128)S(1)}, f32[20,16,128]{2,1,0:T(8,128)S(1)}, u32[]{:S(2)}, u32[]{:S(2)}) collective-permute-start(f32[20,16,128]{2,1,0:T(8,128)S(1)} %collective-permute-done.13.refs_1_), channel_id=1, source_target_pairs={{0,4},{4,0},{8,12},{12,8},{16,20},{20,16},{24,28},{28,24},{1,5},{5... | collective-permute-start | bytes 491528 | tf_op jit(solution)/shard_map/ppermute | solution.py:263
  54.0 8.0 %collective-permute-start.16 = (f32[20,16,128]{2,1,0:T(8,128)S(1)}, f32[20,16,128]{2,1,0:T(8,128)S(1)}, u32[]{:S(2)}, u32[]{:S(2)}) collective-permute-start(f32[20,16,128]{2,1,0:T(8,128)S(1)} %collective-permute-done.15.refs_2_), channel_id=1, source_target_pairs={{0,4},{4,0},{8,12},{12,8},{16,20},{20,16},{24,28},{28,24},{1,5},{5... | collective-permute-start | bytes 491528 | tf_op jit(solution)/shard_map/ppermute | solution.py:263
  60.8 5.3 %collective-permute-start.19 = (f32[20,16,128]{2,1,0:T(8,128)S(1)}, f32[20,16,128]{2,1,0:T(8,128)S(1)}, u32[]{:S(2)}, u32[]{:S(2)}) collective-permute-start(f32[20,16,128]{2,1,0:T(8,128)S(1)} %collective-permute-done.17.refs_2_), channel_id=1, source_target_pairs={{0,4},{4,0},{8,12},{12,8},{16,20},{20,16},{24,28},{28,24},{1,5},{5... | collective-permute-start | bytes 491528 | tf_op jit(solution)/shard_map/ppermute | solution.py:263
  66.1 7.3 %collective-permute-start.30 = (f32[8,64,128]{2,1,0:T(8,128)S(1)}, f32[8,64,128]{2,1,0:T(8,128)S(1)}, u32[]{:S(2)}, u32[]{:S(2)}) collective-permute-start(f32[8,64,128]{2,1,0:T(8,128)S(1)} %get-tuple-element.78), channel_id=1, source_target_pairs={{0,1},{1,0},{2,3},{3,2},{4,5},{5,4},{6,7},{7,6},{8,9},{9,8},{10,11... | collective-permute-start | bytes 786440 | tf_op jit(solution)/shard_map/ppermute | solution.py:263
  66.7 9.2 %collective-permute-start.31 = (f32[8,64,128]{2,1,0:T(8,128)S(1)}, f32[8,64,128]{2,1,0:T(8,128)S(1)}, u32[]{:S(2)}, u32[]{:S(2)}) collective-permute-start(f32[8,64,128]{2,1,0:T(8,128)S(1)} %maximum_add_fusion), channel_id=1, source_target_pairs={{0,2},{1,3},{2,0},{3,1},{4,6},{5,7},{6,4},{7,5},{8,10},{9,11},{10,... | collective-permute-start | bytes 786440 | tf_op jit(solution)/shard_map/ppermute | solution.py:263
  68.1 9.2 %collective-permute-start.20 = (f32[8,48,128]{2,1,0:T(8,128)S(1)}, f32[8,48,128]{2,1,0:T(8,128)S(1)}, u32[]{:S(2)}, u32[]{:S(2)}) collective-permute-start(f32[8,48,128]{2,1,0:T(8,128)S(1)} %get-tuple-element.64), channel_id=1, source_target_pairs={{0,1},{1,0},{2,3},{3,2},{4,5},{5,4},{6,7},{7,6},{8,9},{9,8},{10,11... | collective-permute-start | bytes 589832 | tf_op jit(solution)/shard_map/ppermute | solution.py:263
  68.1 12.5 %collective-permute-start.22 = (f32[8,48,128]{2,1,0:T(8,128)S(1)}, f32[8,48,128]{2,1,0:T(8,128)S(1)}, u32[]{:S(2)}, u32[]{:S(2)}) collective-permute-start(f32[8,48,128]{2,1,0:T(8,128)S(1)} %add.37), channel_id=1, source_target_pairs={{0,2},{1,3},{2,0},{3,1},{4,6},{5,7},{6,4},{7,5},{8,10},{9,11},{10,... | collective-permute-start | bytes 589832 | tf_op jit(solution)/shard_map/ppermute | solution.py:263
  73.5 7.2 %collective-permute-start.29 = (f32[8,16,128]{2,1,0:T(8,128)S(1)}, f32[8,16,128]{2,1,0:T(8,128)S(1)}, u32[]{:S(2)}, u32[]{:S(2)}) collective-permute-start(f32[8,16,128]{2,1,0:T(8,128)S(1)} %add.40), channel_id=1, source_target_pairs={{0,2},{1,3},{2,0},{3,1},{4,6},{5,7},{6,4},{7,5},{8,10},{9,11},{10,... | collective-permute-start | bytes 196616 | tf_op jit(solution)/shard_map/ppermute | solution.py:263
  (9 other events, 44.5 us)

commit v4 on v3

--- a/solution.py
+++ b/solution.py
@@ -365,9 +365,12 @@
     side_of = lambda value, k: across(value, "pix", 2 * k)
     came = [side_of(add(near_parts[k], crossed[k]), k) for k in order if k]
     own = call(residual_kernel, rows, [vmem] * (3 + len(came)))(picked, near_parts[0], crossed[0], *came)
-    near_blocks = [own] + [side_of(own, k) for k in range(1, deep)]
-    blocks = {(0, k): block for k, block in enumerate(near_blocks)}
-    arrival = [k for k in (1, 3, 2) if k < deep] + list(range(4, deep))
+    arrival = [k for k in (1, 2, 3) if k < deep] + list(range(4, deep))
+    blocks = {(0, 0): own}
+    for k in arrival[:-1]:
+        blocks[0, k] = side_of(own, k)
+    blocks[0, arrival[-1]] = side_of(after(own, blocks[0, arrival[0]]), arrival[-1])
+    near_blocks = [blocks[0, k] for k in range(deep)]
     for k in [0] + arrival[:-1]:
         blocks[1, k] = across(near_blocks[k], "pix", 1)
     top = angle_bits[-1]

time: 83.2 us -> 83.1 us (level)
  waiting for transfers between devices: 24.8 us -> 20.7 us
  starting transfers between devices: 27.8 us -> 31.8 us
    ppermute x32, waiting for transfers between devices: 24.8 us -> 20.7 us  [shards(): lax.ppermute(value, axis, [(d, d ^ flip) for d in range(lax.axis_size(axi...]
    ppermute x32, starting transfers between devices: 27.8 us -> 31.8 us  [shards(): lax.ppermute(value, axis, [(d, d ^ flip) for d in range(lax.axis_size(axi...]
  transfers between devices with their start and end apart: 32 -> 32, of which waited for: 13 -> 10; matrix products, arithmetic and copies ran while one was open for 0% -> 0% of each run, Pallas kernels for 32% -> 32%
where the time goes in v4:
time: 83.1 us; the launch traced here: 81.8 us
  starting transfers between devices  31.8 us (38%)
  Pallas kernels  27.8 us (33%)
  waiting for transfers between devices  20.7 us (25%)
  local copies, waits for them, and re-layouts  1.07 us (1%)
    ppermute x32, starting transfers between devices, shards(): lax.ppermute(value, axis, [(d, d ^ flip) for d in range(lax.axis_size(axi...  31.8 us
    ppermute x32, waiting for transfers between devices, shards(): lax.ppermute(value, axis, [(d, d ^ flip) for d in range(lax.axis_size(axi...  20.7 us
    pallas_call x3, Pallas kernels, backward(): call(functools.partial(backward_kernel, turns, lists_of(turns), loose, co...  9.99 us
    pallas_call x3, Pallas kernels, forward(): call(functools.partial(forward_kernel, turns, lists_of(turns), count, spa...  8.66 us
    pallas_call x1, Pallas kernels, shards(): call(functools.partial(front_kernel, own_tiles, ang, live), (listed, list...  6.41 us
    pallas_call x2, Pallas kernels, update(): pl.pallas_call(functools.partial(update_kernel, parts, deep), out_shape=j...  2.64 us
  transfers between devices with their start and end apart: 32, of which 10 were waited for; matrix products, arithmetic and copies ran while one was open for 0% of the time, Pallas kernels for 32%

profile of v4, /device:TPU:0, one launch (start us, length us, event | category | flops | bytes accessed | tf_op | source)
XLA Modules:
  0.0 81.8 jit_solution(11194506020217243586)
XLA Ops:
  1.1 3.0 %collective-permute-start.4 = (f32[8,64,128]{2,1,0:T(8,128)S(1)}, f32[8,64,128]{2,1,0:T(8,128)S(1)}, u32[]{:S(2)}, u32[]{:S(2)}) collective-permute-start(f32[8,64,128]{2,1,0:T(8,128)S(1)} %get-tuple-element.81.refs_0_), channel_id=1, source_target_pairs={{0,2},{1,3},{2,0},{3,1},{4,6},{5,7},{6,4},{7,5},{8,10},{9,11},{10,... | collective-permute-start | bytes 786440 | tf_op jit(solution)/shard_map/ppermute | solution.py:263
  4.7 6.4 %shard_map.55 = (s32[360]{0:T(512)S(1)}, s32[360]{0:T(512)S(1)}, s32[360]{0:T(512)S(1)}, s32[2]{0:T(128)S(1)}, s32[20,16,128]{2,1,0:T(8,128)S(1)}, /*index=5*/bf16[160,128,256]{2,1,0:T(8,128)(2,1)S(1)}) custom-call(s32[160]{0:T(256)} %ids_hbm.1, s32[1,8]{1,0:T(1,128)} %rays_hbm.1, s32[4]{0:T(128)S(1)} %pad_add_fusion.place, s32[32,128,128]{2,1,0:T(8,128)} %counts.1, ...), custom_call_target="tpu_custom_call" | custom-call | tf_op jit(solution)/shard_map/pallas_call | solution.py:291
  11.3 3.7 %shard_map.56 = (f32[21,64,128]{2,1,0:T(8,128)S(1)}, f32[21,64,128]{2,1,0:T(8,128)S(1)}) custom-call(s32[360]{0:T(512)S(1)} %get-tuple-element.43.rank_of, s32[360]{0:T(512)S(1)} %get-tuple-element.44.col_of, s32[360]{0:T(512)S(1)} %get-tuple-element.45.tile_of, s32[2]{0:T(128)S(1)} %get-tuple-element.75.total, s32[4]{0:T(128)S(1)} %pad_add_fusion.place, ...), custom_call_target="tpu_custom_call" | custom-call | tf_op jit(solution)/shard_map/pallas_call | solution.py:321
  16.0 2.5 %shard_map.58 = (f32[20,16,128]{2,1,0:T(8,128)S(1)}, f32[20,16,128]{2,1,0:T(8,128)S(1)}, f32[20,16,128]{2,1,0:T(8,128)S(1)}, f32[20,16,128]{2,1,0:T(8,128)S(1)}) custom-call(s32[360]{0:T(512)S(1)} %get-tuple-element.43.rank_of, s32[360]{0:T(512)S(1)} %get-tuple-element.44.col_of, s32[360]{0:T(512)S(1)} %get-tuple-element.45.tile_of, ...), custom_call_target="tpu_custom_call" | custom-call | tf_op jit(solution)/shard_map/pallas_call | solution.py:321
  18.5 1.8 %collective-permute-start.7 = (f32[20,16,128]{2,1,0:T(8,128)S(1)}, f32[20,16,128]{2,1,0:T(8,128)S(1)}, u32[]{:S(2)}, u32[]{:S(2)}) collective-permute-start(f32[20,16,128]{2,1,0:T(8,128)S(1)} %get-tuple-element.56), channel_id=1, source_target_pairs={{0,4},{4,0},{8,12},{12,8},{16,20},{20,16},{24,28},{28,24},{1,5},{5... | collective-permute-start | bytes 491528 | tf_op jit(solution)/shard_map/ppermute | solution.py:263
  20.6 1.7 %collective-permute-start.11 = (f32[20,16,128]{2,1,0:T(8,128)S(1)}, f32[20,16,128]{2,1,0:T(8,128)S(1)}, u32[]{:S(2)}, u32[]{:S(2)}) collective-permute-start(f32[20,16,128]{2,1,0:T(8,128)S(1)} %get-tuple-element.60), channel_id=1, source_target_pairs={{0,4},{4,0},{8,12},{12,8},{16,20},{20,16},{24,28},{28,24},{1,5},{5... | collective-permute-start | bytes 491528 | tf_op jit(solution)/shard_map/ppermute | solution.py:263
  22.6 2.5 %shard_map.57 = (f32[20,16,128]{2,1,0:T(8,128)S(1)}, f32[20,16,128]{2,1,0:T(8,128)S(1)}, f32[20,16,128]{2,1,0:T(8,128)S(1)}, f32[20,16,128]{2,1,0:T(8,128)S(1)}) custom-call(s32[360]{0:T(512)S(1)} %get-tuple-element.43.rank_of, s32[360]{0:T(512)S(1)} %get-tuple-element.44.col_of, s32[360]{0:T(512)S(1)} %get-tuple-element.45.tile_of, ...), custom_call_target="tpu_custom_call" | custom-call | tf_op jit(solution)/shard_map/pallas_call | solution.py:321
  25.6 3.9 %collective-permute-start.8 = (f32[20,16,128]{2,1,0:T(8,128)S(1)}, f32[20,16,128]{2,1,0:T(8,128)S(1)}, u32[]{:S(2)}, u32[]{:S(2)}) collective-permute-start(f32[20,16,128]{2,1,0:T(8,128)S(1)} %shard_map.59), channel_id=1, source_target_pairs={{0,24},{4,28},{8,16},{12,20},{16,8},{20,12},{24,0},{28,4},{1,25},{... | collective-permute-start | bytes 491528 | tf_op jit(solution)/shard_map/ppermute | solution.py:263
  29.5 3.1 %collective-permute-start.10 = (f32[20,16,128]{2,1,0:T(8,128)S(1)}, f32[20,16,128]{2,1,0:T(8,128)S(1)}, u32[]{:S(2)}, u32[]{:S(2)}) collective-permute-start(f32[20,16,128]{2,1,0:T(8,128)S(1)} %shard_map.60), channel_id=1, source_target_pairs={{0,16},{4,20},{8,24},{12,28},{16,0},{20,4},{24,8},{28,12},{1,17},{... | collective-permute-start | bytes 491528 | tf_op jit(solution)/shard_map/ppermute | solution.py:263
  32.6 1.9 %collective-permute-start.12 = (f32[20,16,128]{2,1,0:T(8,128)S(1)}, f32[20,16,128]{2,1,0:T(8,128)S(1)}, u32[]{:S(2)}, u32[]{:S(2)}) collective-permute-start(f32[20,16,128]{2,1,0:T(8,128)S(1)} %shard_map.61), channel_id=1, source_target_pairs={{0,8},{4,12},{8,0},{12,4},{16,24},{20,28},{24,16},{28,20},{1,9},{5... | collective-permute-start | bytes 491528 | tf_op jit(solution)/shard_map/ppermute | solution.py:263
  35.7 7.1 %collective-permute-done.10.refs_3_ = f32[20,16,128]{2,1,0:T(8,128)S(1)} collective-permute-done((f32[20,16,128]{2,1,0:T(8,128)S(1)}, f32[20,16,128]{2,1,0:T(8,128)S(1)}, u32[]{:S(2)}, u32[]{:S(2)}) %collective-permute-start.10) | collective-permute-done | bytes 163872 | tf_op jit(solution)/shard_map/ppermute | solution.py:263
  43.1 3.2 %collective-permute-start.15 = (f32[20,16,128]{2,1,0:T(8,128)S(1)}, f32[20,16,128]{2,1,0:T(8,128)S(1)}, u32[]{:S(2)}, u32[]{:S(2)}) collective-permute-start(f32[20,16,128]{2,1,0:T(8,128)S(1)} %shard_map.62.refs_0_), channel_id=1, source_target_pairs={{0,16},{4,20},{8,24},{12,28},{16,0},{20,4},{24,8},{28,12},{1,17},{... | collective-permute-start | bytes 491528 | tf_op jit(solution)/shard_map/ppermute | solution.py:263
  46.2 1.4 %collective-permute-start.18 = (f32[20,16,128]{2,1,0:T(8,128)S(1)}, f32[20,16,128]{2,1,0:T(8,128)S(1)}, u32[]{:S(2)}, u32[]{:S(2)}) collective-permute-start(f32[20,16,128]{2,1,0:T(8,128)S(1)} %shard_map.62.refs_0_), channel_id=1, source_target_pairs={{0,4},{4,0},{8,12},{12,8},{16,20},{20,16},{24,28},{28,24},{1,5},{5... | collective-permute-start | bytes 491528 | tf_op jit(solution)/shard_map/ppermute | solution.py:263
  47.7 3.4 %collective-permute-done.13.refs_1_ = f32[20,16,128]{2,1,0:T(8,128)S(1)} collective-permute-done((f32[20,16,128]{2,1,0:T(8,128)S(1)}, f32[20,16,128]{2,1,0:T(8,128)S(1)}, u32[]{:S(2)}, u32[]{:S(2)}) %collective-permute-start.13) | collective-permute-done | bytes 163872 | tf_op jit(solution)/shard_map/ppermute | solution.py:263
  51.1 1.8 %collective-permute-start.17 = (f32[20,16,128]{2,1,0:T(8,128)S(1)}, f32[20,16,128]{2,1,0:T(8,128)S(1)}, u32[]{:S(2)}, u32[]{:S(2)}) collective-permute-start(f32[20,16,128]{2,1,0:T(8,128)S(1)} %shard_map.62.refs_0_), channel_id=1, source_target_pairs={{0,24},{4,28},{8,16},{12,20},{16,8},{20,12},{24,0},{28,4},{1,25},{... | collective-permute-start | bytes 491528 | tf_op jit(solution)/shard_map/ppermute | solution.py:263
  52.9 1.5 %collective-permute-start.14 = (f32[20,16,128]{2,1,0:T(8,128)S(1)}, f32[20,16,128]{2,1,0:T(8,128)S(1)}, u32[]{:S(2)}, u32[]{:S(2)}) collective-permute-start(f32[20,16,128]{2,1,0:T(8,128)S(1)} %collective-permute-done.13.refs_1_), channel_id=1, source_target_pairs={{0,4},{4,0},{8,12},{12,8},{16,20},{20,16},{24,28},{28,24},{1,5},{5... | collective-permute-start | bytes 491528 | tf_op jit(solution)/shard_map/ppermute | solution.py:263
  54.9 4.0 %shard_map.64 = (f32[8,64,128]{2,1,0:T(8,128)S(1)}, f32[8,64,128]{2,1,0:T(8,128)S(1)}, f32[8,64,128]{2,1,0:T(8,128)S(1)}, f32[8,16,128]{2,1,0:T(8,128)S(1)}, f32...) custom-call(s32[360]{0:T(512)S(1)} %get-tuple-element.43.rank_of, ...), custom_call_target="tpu_custom_call" | custom-call | tf_op jit(solution)/shard_map/pallas_call | solution.py:334
  60.5 1.5 %collective-permute-done.16.refs_1_ = f32[20,16,128]{2,1,0:T(8,128)S(1)} collective-permute-done((f32[20,16,128]{2,1,0:T(8,128)S(1)}, f32[20,16,128]{2,1,0:T(8,128)S(1)}, u32[]{:S(2)}, u32[]{:S(2)}) %collective-permute-start.16) | collective-permute-done | bytes 163872 | tf_op jit(solution)/shard_map/ppermute | solution.py:263
  62.0 3.4 %shard_map.63 = (f32[8,48,128]{2,1,0:T(8,128)S(1)}, f32[8,48,128]{2,1,0:T(8,128)S(1)}, f32[8,48,128]{2,1,0:T(8,128)S(1)}, f32[8,48,128]{2,1,0:T(8,128)S(1)}) custom-call(s32[360]{0:T(512)S(1)} %get-tuple-element.43.rank_of, s32[360]{0:T(512)S(1)} %get-tuple-element.44.col_of, s32[360]{0:T(512)S(1)} %get-tuple-element.45.tile_of, ...), custom_call_target="tpu_custom_call" | custom-call | tf_op jit(solution)/shard_map/pallas_call | solution.py:334
  66.2 1.8 %collective-permute-start.31 = (f32[8,64,128]{2,1,0:T(8,128)S(1)}, f32[8,64,128]{2,1,0:T(8,128)S(1)}, u32[]{:S(2)}, u32[]{:S(2)}) collective-permute-start(f32[8,64,128]{2,1,0:T(8,128)S(1)} %maximum_add_fusion), channel_id=1, source_target_pairs={{0,2},{1,3},{2,0},{3,1},{4,6},{5,7},{6,4},{7,5},{8,10},{9,11},{10,... | collective-permute-start | bytes 786440 | tf_op jit(solution)/shard_map/ppermute | solution.py:263
  69.3 2.6 %shard_map.65 = (f32[8,16,128]{2,1,0:T(8,128)S(1)}, f32[8,16,128]{2,1,0:T(8,128)S(1)}, f32[8,16,128]{2,1,0:T(8,128)S(1)}, f32[8,16,128]{2,1,0:T(8,128)S(1)}) custom-call(s32[360]{0:T(512)S(1)} %get-tuple-element.43.rank_of, s32[360]{0:T(512)S(1)} %get-tuple-element.44.col_of, s32[360]{0:T(512)S(1)} %get-tuple-element.45.tile_of, ...), custom_call_target="tpu_custom_call" | custom-call | tf_op jit(solution)/shard_map/pallas_call | solution.py:334
  75.4 1.3 %shard_map.66.refs_4_ = f32[8,128,128]{2,1,0:T(8,128)} custom-call(s32[4]{0:T(128)S(1)} %pad_add_fusion.place, f32[8,128,128]{2,1,0:T(8,128)S(1)} %copy-done, f32[8,64,128]{2,1,0:T(8,128)S(1)} %add.41.refs_0_, f32[8,64,128]{2,1,0:T(8,128)S(1)} %collective-permute-done.31.refs_1_), custom_call_target="tpu_custom_call" | custom-call | tf_op jit(solution)/shard_map/pallas_call | solution.py:395
  76.8 3.8 %collective-permute-done.29.refs_3_ = f32[8,16,128]{2,1,0:T(8,128)S(1)} collective-permute-done((f32[8,16,128]{2,1,0:T(8,128)S(1)}, f32[8,16,128]{2,1,0:T(8,128)S(1)}, u32[]{:S(2)}, u32[]{:S(2)}) %collective-permute-start.29) | collective-permute-done | bytes 65568 | tf_op jit(solution)/shard_map/ppermute | solution.py:263
  80.5 1.3 %shard_map.67 = f32[8,128,128]{2,1,0:T(8,128)} custom-call(s32[4]{0:T(128)S(1)} %pad_add_fusion.place, f32[8,128,128]{2,1,0:T(8,128)S(1)} %copy-done, f32[8,48,128]{2,1,0:T(8,128)S(1)} %add.36.refs_0_, f32[8,48,128]{2,1,0:T(8,128)S(1)} %collective-permute-done.22.refs_1_, f32[8,16,128]{2,1,0:T(8,128)S(1)} %add.39.refs_2_, ...), custom_call_target="tpu_custom_call", output_to_operand_aliasing={{}: (6, {})} | custom-call | tf_op jit(solution)/shard_map/pallas_call | solution.py:395
  (63 shorter events, 13.1 us)
Async XLA Ops:
  1.1 10.2 %collective-permute-start.4 = (f32[8,64,128]{2,1,0:T(8,128)S(1)}, f32[8,64,128]{2,1,0:T(8,128)S(1)}, u32[]{:S(2)}, u32[]{:S(2)}) collective-permute-start(f32[8,64,128]{2,1,0:T(8,128)S(1)} %get-tuple-element.81.refs_0_), channel_id=1, source_target_pairs={{0,2},{1,3},{2,0},{3,1},{4,6},{5,7},{6,4},{7,5},{8,10},{9,11},{10,... | collective-permute-start | bytes 786440 | tf_op jit(solution)/shard_map/ppermute | solution.py:263
  4.1 7.2 %collective-permute-start.1 = (f32[8,64,128]{2,1,0:T(8,128)S(1)}, f32[8,64,128]{2,1,0:T(8,128)S(1)}, u32[]{:S(2)}, u32[]{:S(2)}) collective-permute-start(f32[8,64,128]{2,1,0:T(8,128)S(1)} %get-tuple-element.81.refs_0_), channel_id=1, source_target_pairs={{0,1},{1,0},{2,3},{3,2},{4,5},{5,4},{6,7},{7,6},{8,9},{9,8},{10,11... | collective-permute-start | bytes 786440 | tf_op jit(solution)/shard_map/ppermute | solution.py:263
  4.1 11.9 %collective-permute-start = (f32[8,64,128]{2,1,0:T(8,128)S(1)}, f32[8,64,128]{2,1,0:T(8,128)S(1)}, u32[]{:S(2)}, u32[]{:S(2)}) collective-permute-start(f32[8,64,128]{2,1,0:T(8,128)S(1)} %get-tuple-element.82.refs_2_), channel_id=1, source_target_pairs={{0,2},{1,3},{2,0},{3,1},{4,6},{5,7},{6,4},{7,5},{8,10},{9,11},{10,... | collective-permute-start | bytes 786440 | tf_op jit(solution)/shard_map/ppermute | solution.py:263
  4.3 7.1 %collective-permute-start.2 = (f32[8,64,128]{2,1,0:T(8,128)S(1)}, f32[8,64,128]{2,1,0:T(8,128)S(1)}, u32[]{:S(2)}, u32[]{:S(2)}) collective-permute-start(f32[8,64,128]{2,1,0:T(8,128)S(1)} %get-tuple-element.82.refs_2_), channel_id=1, source_target_pairs={{0,1},{1,0},{2,3},{3,2},{4,5},{5,4},{6,7},{7,6},{8,9},{9,8},{10,11... | collective-permute-start | bytes 786440 | tf_op jit(solution)/shard_map/ppermute | solution.py:263
  16.0 6.6 %collective-permute-start.3 = (f32[8,64,128]{2,1,0:T(8,128)S(1)}, f32[8,64,128]{2,1,0:T(8,128)S(1)}, u32[]{:S(2)}, u32[]{:S(2)}) collective-permute-start(f32[8,64,128]{2,1,0:T(8,128)S(1)} %collective-permute-done.refs_0_), channel_id=1, source_target_pairs={{0,1},{1,0},{2,3},{3,2},{4,5},{5,4},{6,7},{7,6},{8,9},{9,8},{10,11... | collective-permute-start | bytes 786440 | tf_op jit(solution)/shard_map/ppermute | solution.py:263
  18.5 7.1 %collective-permute-start.7 = (f32[20,16,128]{2,1,0:T(8,128)S(1)}, f32[20,16,128]{2,1,0:T(8,128)S(1)}, u32[]{:S(2)}, u32[]{:S(2)}) collective-permute-start(f32[20,16,128]{2,1,0:T(8,128)S(1)} %get-tuple-element.56), channel_id=1, source_target_pairs={{0,4},{4,0},{8,12},{12,8},{16,20},{20,16},{24,28},{28,24},{1,5},{5... | collective-permute-start | bytes 491528 | tf_op jit(solution)/shard_map/ppermute | solution.py:263
  20.3 9.2 %collective-permute-start.9 = (f32[20,16,128]{2,1,0:T(8,128)S(1)}, f32[20,16,128]{2,1,0:T(8,128)S(1)}, u32[]{:S(2)}, u32[]{:S(2)}) collective-permute-start(f32[20,16,128]{2,1,0:T(8,128)S(1)} %get-tuple-element.58), channel_id=1, source_target_pairs={{0,4},{4,0},{8,12},{12,8},{16,20},{20,16},{24,28},{28,24},{1,5},{5... | collective-permute-start | bytes 491528 | tf_op jit(solution)/shard_map/ppermute | solution.py:263
  20.6 12.0 %collective-permute-start.11 = (f32[20,16,128]{2,1,0:T(8,128)S(1)}, f32[20,16,128]{2,1,0:T(8,128)S(1)}, u32[]{:S(2)}, u32[]{:S(2)}) collective-permute-start(f32[20,16,128]{2,1,0:T(8,128)S(1)} %get-tuple-element.60), channel_id=1, source_target_pairs={{0,4},{4,0},{8,12},{12,8},{16,20},{20,16},{24,28},{28,24},{1,5},{5... | collective-permute-start | bytes 491528 | tf_op jit(solution)/shard_map/ppermute | solution.py:263
  22.3 13.4 %collective-permute-start.6 = (f32[20,16,128]{2,1,0:T(8,128)S(1)}, f32[20,16,128]{2,1,0:T(8,128)S(1)}, u32[]{:S(2)}, u32[]{:S(2)}) collective-permute-start(f32[20,16,128]{2,1,0:T(8,128)S(1)} %get-tuple-element.54), channel_id=1, source_target_pairs={{0,4},{4,0},{8,12},{12,8},{16,20},{20,16},{24,28},{28,24},{1,5},{5... | collective-permute-start | bytes 491528 | tf_op jit(solution)/shard_map/ppermute | solution.py:263
  25.6 10.1 %collective-permute-start.8 = (f32[20,16,128]{2,1,0:T(8,128)S(1)}, f32[20,16,128]{2,1,0:T(8,128)S(1)}, u32[]{:S(2)}, u32[]{:S(2)}) collective-permute-start(f32[20,16,128]{2,1,0:T(8,128)S(1)} %shard_map.59), channel_id=1, source_target_pairs={{0,24},{4,28},{8,16},{12,20},{16,8},{20,12},{24,0},{28,4},{1,25},{... | collective-permute-start | bytes 491528 | tf_op jit(solution)/shard_map/ppermute | solution.py:263
  29.5 13.4 %collective-permute-start.10 = (f32[20,16,128]{2,1,0:T(8,128)S(1)}, f32[20,16,128]{2,1,0:T(8,128)S(1)}, u32[]{:S(2)}, u32[]{:S(2)}) collective-permute-start(f32[20,16,128]{2,1,0:T(8,128)S(1)} %shard_map.60), channel_id=1, source_target_pairs={{0,16},{4,20},{8,24},{12,28},{16,0},{20,4},{24,8},{28,12},{1,17},{... | collective-permute-start | bytes 491528 | tf_op jit(solution)/shard_map/ppermute | solution.py:263
  32.6 10.2 %collective-permute-start.12 = (f32[20,16,128]{2,1,0:T(8,128)S(1)}, f32[20,16,128]{2,1,0:T(8,128)S(1)}, u32[]{:S(2)}, u32[]{:S(2)}) collective-permute-start(f32[20,16,128]{2,1,0:T(8,128)S(1)} %shard_map.61), channel_id=1, source_target_pairs={{0,8},{4,12},{8,0},{12,4},{16,24},{20,28},{24,16},{28,20},{1,9},{5... | collective-permute-start | bytes 491528 | tf_op jit(solution)/shard_map/ppermute | solution.py:263
  43.0 8.1 %collective-permute-start.13 = (f32[20,16,128]{2,1,0:T(8,128)S(1)}, f32[20,16,128]{2,1,0:T(8,128)S(1)}, u32[]{:S(2)}, u32[]{:S(2)}) collective-permute-start(f32[20,16,128]{2,1,0:T(8,128)S(1)} %shard_map.62.refs_0_), channel_id=1, source_target_pairs={{0,8},{4,12},{8,0},{12,4},{16,24},{20,28},{24,16},{28,20},{1,9},{5... | collective-permute-start | bytes 491528 | tf_op jit(solution)/shard_map/ppermute | solution.py:263
  43.1 11.4 %collective-permute-start.15 = (f32[20,16,128]{2,1,0:T(8,128)S(1)}, f32[20,16,128]{2,1,0:T(8,128)S(1)}, u32[]{:S(2)}, u32[]{:S(2)}) collective-permute-start(f32[20,16,128]{2,1,0:T(8,128)S(1)} %shard_map.62.refs_0_), channel_id=1, source_target_pairs={{0,16},{4,20},{8,24},{12,28},{16,0},{20,4},{24,8},{28,12},{1,17},{... | collective-permute-start | bytes 491528 | tf_op jit(solution)/shard_map/ppermute | solution.py:263
  46.2 8.7 %collective-permute-start.18 = (f32[20,16,128]{2,1,0:T(8,128)S(1)}, f32[20,16,128]{2,1,0:T(8,128)S(1)}, u32[]{:S(2)}, u32[]{:S(2)}) collective-permute-start(f32[20,16,128]{2,1,0:T(8,128)S(1)} %shard_map.62.refs_0_), channel_id=1, source_target_pairs={{0,4},{4,0},{8,12},{12,8},{16,20},{20,16},{24,28},{28,24},{1,5},{5... | collective-permute-start | bytes 491528 | tf_op jit(solution)/shard_map/ppermute | solution.py:263
  51.1 7.9 %collective-permute-start.17 = (f32[20,16,128]{2,1,0:T(8,128)S(1)}, f32[20,16,128]{2,1,0:T(8,128)S(1)}, u32[]{:S(2)}, u32[]{:S(2)}) collective-permute-start(f32[20,16,128]{2,1,0:T(8,128)S(1)} %shard_map.62.refs_0_), channel_id=1, source_target_pairs={{0,24},{4,28},{8,16},{12,20},{16,8},{20,12},{24,0},{28,4},{1,25},{... | collective-permute-start | bytes 491528 | tf_op jit(solution)/shard_map/ppermute | solution.py:263
  52.9 7.6 %collective-permute-start.14 = (f32[20,16,128]{2,1,0:T(8,128)S(1)}, f32[20,16,128]{2,1,0:T(8,128)S(1)}, u32[]{:S(2)}, u32[]{:S(2)}) collective-permute-start(f32[20,16,128]{2,1,0:T(8,128)S(1)} %collective-permute-done.13.refs_1_), channel_id=1, source_target_pairs={{0,4},{4,0},{8,12},{12,8},{16,20},{20,16},{24,28},{28,24},{1,5},{5... | collective-permute-start | bytes 491528 | tf_op jit(solution)/shard_map/ppermute | solution.py:263
  54.4 7.6 %collective-permute-start.16 = (f32[20,16,128]{2,1,0:T(8,128)S(1)}, f32[20,16,128]{2,1,0:T(8,128)S(1)}, u32[]{:S(2)}, u32[]{:S(2)}) collective-permute-start(f32[20,16,128]{2,1,0:T(8,128)S(1)} %collective-permute-done.15.refs_2_), channel_id=1, source_target_pairs={{0,4},{4,0},{8,12},{12,8},{16,20},{20,16},{24,28},{28,24},{1,5},{5... | collective-permute-start | bytes 491528 | tf_op jit(solution)/shard_map/ppermute | solution.py:263
  58.9 6.5 %collective-permute-start.19 = (f32[20,16,128]{2,1,0:T(8,128)S(1)}, f32[20,16,128]{2,1,0:T(8,128)S(1)}, u32[]{:S(2)}, u32[]{:S(2)}) collective-permute-start(f32[20,16,128]{2,1,0:T(8,128)S(1)} %collective-permute-done.17.refs_2_), channel_id=1, source_target_pairs={{0,4},{4,0},{8,12},{12,8},{16,20},{20,16},{24,28},{28,24},{1,5},{5... | collective-permute-start | bytes 491528 | tf_op jit(solution)/shard_map/ppermute | solution.py:263
  65.5 7.9 %collective-permute-start.30 = (f32[8,64,128]{2,1,0:T(8,128)S(1)}, f32[8,64,128]{2,1,0:T(8,128)S(1)}, u32[]{:S(2)}, u32[]{:S(2)}) collective-permute-start(f32[8,64,128]{2,1,0:T(8,128)S(1)} %get-tuple-element.80), channel_id=1, source_target_pairs={{0,1},{1,0},{2,3},{3,2},{4,5},{5,4},{6,7},{7,6},{8,9},{9,8},{10,11... | collective-permute-start | bytes 786440 | tf_op jit(solution)/shard_map/ppermute | solution.py:263
  66.2 9.2 %collective-permute-start.31 = (f32[8,64,128]{2,1,0:T(8,128)S(1)}, f32[8,64,128]{2,1,0:T(8,128)S(1)}, u32[]{:S(2)}, u32[]{:S(2)}) collective-permute-start(f32[8,64,128]{2,1,0:T(8,128)S(1)} %maximum_add_fusion), channel_id=1, source_target_pairs={{0,2},{1,3},{2,0},{3,1},{4,6},{5,7},{6,4},{7,5},{8,10},{9,11},{10,... | collective-permute-start | bytes 786440 | tf_op jit(solution)/shard_map/ppermute | solution.py:263
  67.9 8.7 %collective-permute-start.20 = (f32[8,48,128]{2,1,0:T(8,128)S(1)}, f32[8,48,128]{2,1,0:T(8,128)S(1)}, u32[]{:S(2)}, u32[]{:S(2)}) collective-permute-start(f32[8,48,128]{2,1,0:T(8,128)S(1)} %get-tuple-element.66), channel_id=1, source_target_pairs={{0,1},{1,0},{2,3},{3,2},{4,5},{5,4},{6,7},{7,6},{8,9},{9,8},{10,11... | collective-permute-start | bytes 589832 | tf_op jit(solution)/shard_map/ppermute | solution.py:263
  68.1 12.4 %collective-permute-start.22 = (f32[8,48,128]{2,1,0:T(8,128)S(1)}, f32[8,48,128]{2,1,0:T(8,128)S(1)}, u32[]{:S(2)}, u32[]{:S(2)}) collective-permute-start(f32[8,48,128]{2,1,0:T(8,128)S(1)} %add.37), channel_id=1, source_target_pairs={{0,2},{1,3},{2,0},{3,1},{4,6},{5,7},{6,4},{7,5},{8,10},{9,11},{10,... | collective-permute-start | bytes 589832 | tf_op jit(solution)/shard_map/ppermute | solution.py:263
  73.4 7.1 %collective-permute-start.29 = (f32[8,16,128]{2,1,0:T(8,128)S(1)}, f32[8,16,128]{2,1,0:T(8,128)S(1)}, u32[]{:S(2)}, u32[]{:S(2)}) collective-permute-start(f32[8,16,128]{2,1,0:T(8,128)S(1)} %add.40), channel_id=1, source_target_pairs={{0,2},{1,3},{2,0},{3,1},{4,6},{5,7},{6,4},{7,5},{8,10},{9,11},{10,... | collective-permute-start | bytes 196616 | tf_op jit(solution)/shard_map/ppermute | solution.py:263
  (9 other events, 47.0 us)

commit v5 on v4

--- a/solution.py
+++ b/solution.py
@@ -407,13 +407,14 @@
     middle = [(side, k) for k in arrival for side in range(2) if (side, k) not in head + tail]
     made = backward(turns, head, total, upper[1::2])
     blocks[tail[0]] = across(after(near_blocks[arrival[-1]], made[0][0]), "pix", 1)
-    low_head, up_head = fold({k: made[k] for k in lower}), fold({k: made[k] for k in upper})
+    ties = [blocks[1, k] for k in arrival[:-1]]
+    low_head, up_head = fold({k: made[k] for k in lower}), fold({k: made[k] for k in upper}, *ties)
     came_head = across(up_head, "ang", top)
     made = backward(turns, middle, total)
     ties = [blocks[tail[0]]]
     low_middle, up_middle = fold({k: made[k] for k in lower}, *ties), fold({k: made[k] for k in upper}, *ties)
     came_middle = across(up_middle, "ang", top)
-    made = backward(turns, tail, after(total, up_head, up_middle))
+    made = backward(turns, tail, after(total, came_head, up_middle))
     low_tail, up_tail = fold({k: made[k] for k in lower}), fold({k: made[k] for k in upper})
     came_tail = across(up_tail, "ang", top)
     begun = update((head,), (low_head, came_head))

time: 83.1 us -> 80.9 us (0.974); the launches traced: 81.8 us -> 80.7 us
  starting transfers between devices: 31.8 us -> 35.6 us
  waiting for transfers between devices: 20.7 us -> 18.1 us
  Pallas kernels: 27.8 us -> 25.6 us
    ppermute x32, starting transfers between devices: 31.8 us -> 35.6 us  [shards(): lax.ppermute(value, axis, [(d, d ^ flip) for d in range(lax.axis_size(axi...]
    ppermute x32, waiting for transfers between devices: 20.7 us -> 18.1 us  [shards(): lax.ppermute(value, axis, [(d, d ^ flip) for d in range(lax.axis_size(axi...]
    pallas_call x3, Pallas kernels: 9.99 us -> 8.73 us  [backward(): call(functools.partial(backward_kernel, turns, lists_of(turns), loose, co...]
    pallas_call x3, Pallas kernels: 8.66 us -> 7.79 us  [forward(): call(functools.partial(forward_kernel, turns, lists_of(turns), count, spa...]
  transfers between devices with their start and end apart: 32 -> 32, of which waited for: 10 -> 13; matrix products, arithmetic and copies ran while one was open for 0% -> 0% of each run, Pallas kernels for 32% -> 30%
where the time goes in v5:
time: 80.9 us; the launch traced here: 80.7 us
  starting transfers between devices  35.6 us (44%)
  Pallas kernels  25.6 us (32%)
  waiting for transfers between devices  18.1 us (22%)
  local copies, waits for them, and re-layouts  1.07 us (1%)
    ppermute x32, starting transfers between devices, shards(): lax.ppermute(value, axis, [(d, d ^ flip) for d in range(lax.axis_size(axi...  35.6 us
    ppermute x32, waiting for transfers between devices, shards(): lax.ppermute(value, axis, [(d, d ^ flip) for d in range(lax.axis_size(axi...  18.1 us
    pallas_call x3, Pallas kernels, backward(): call(functools.partial(backward_kernel, turns, lists_of(turns), loose, co...  8.73 us
    pallas_call x3, Pallas kernels, forward(): call(functools.partial(forward_kernel, turns, lists_of(turns), count, spa...  7.79 us
    pallas_call x1, Pallas kernels, shards(): call(functools.partial(front_kernel, own_tiles, ang, live), (listed, list...  6.29 us
    pallas_call x2, Pallas kernels, update(): pl.pallas_call(functools.partial(update_kernel, parts, deep), out_shape=j...  2.64 us
  transfers between devices with their start and end apart: 32, of which 13 were waited for; matrix products, arithmetic and copies ran while one was open for 0% of the time, Pallas kernels for 30%

profile of v5, /device:TPU:0, one launch (start us, length us, event | category | flops | bytes accessed | tf_op | source)
XLA Modules:
  0.0 80.7 jit_solution(8006942999932290217)
XLA Ops:
  1.1 3.0 %collective-permute-start.4 = (f32[8,64,128]{2,1,0:T(8,128)S(1)}, f32[8,64,128]{2,1,0:T(8,128)S(1)}, u32[]{:S(2)}, u32[]{:S(2)}) collective-permute-start(f32[8,64,128]{2,1,0:T(8,128)S(1)} %get-tuple-element.89.refs_0_), channel_id=1, source_target_pairs={{0,2},{1,3},{2,0},{3,1},{4,6},{5,7},{6,4},{7,5},{8,10},{9,11},{10,... | collective-permute-start | bytes 786440 | tf_op jit(solution)/shard_map/ppermute | solution.py:263
  4.7 6.3 %shard_map.55 = (s32[360]{0:T(512)S(1)}, s32[360]{0:T(512)S(1)}, s32[360]{0:T(512)S(1)}, s32[2]{0:T(128)S(1)}, s32[20,16,128]{2,1,0:T(8,128)S(1)}, /*index=5*/bf16[160,128,256]{2,1,0:T(8,128)(2,1)S(1)}) custom-call(s32[160]{0:T(256)} %ids_hbm.1, s32[1,8]{1,0:T(1,128)} %rays_hbm.1, s32[4]{0:T(128)S(1)} %pad_add_fusion.place, s32[32,128,128]{2,1,0:T(8,128)} %counts.1, ...), custom_call_target="tpu_custom_call" | custom-call | tf_op jit(solution)/shard_map/pallas_call | solution.py:291
  11.4 2.8 %shard_map.56 = (f32[21,64,128]{2,1,0:T(8,128)S(1)}, f32[21,64,128]{2,1,0:T(8,128)S(1)}) custom-call(s32[360]{0:T(512)S(1)} %get-tuple-element.47.rank_of, s32[360]{0:T(512)S(1)} %get-tuple-element.48.col_of, s32[360]{0:T(512)S(1)} %get-tuple-element.49.tile_of, s32[2]{0:T(128)S(1)} %get-tuple-element.83.total, s32[4]{0:T(128)S(1)} %pad_add_fusion.place, ...), custom_call_target="tpu_custom_call" | custom-call | tf_op jit(solution)/shard_map/pallas_call | solution.py:321
  14.3 1.7 %collective-permute-done.refs_0_ = f32[8,64,128]{2,1,0:T(8,128)S(1)} collective-permute-done((f32[8,64,128]{2,1,0:T(8,128)S(1)}, f32[8,64,128]{2,1,0:T(8,128)S(1)}, u32[]{:S(2)}, u32[]{:S(2)}) %collective-permute-start) | collective-permute-done | bytes 262176 | tf_op jit(solution)/shard_map/ppermute | solution.py:263
  16.0 2.5 %shard_map.58 = (f32[20,16,128]{2,1,0:T(8,128)S(1)}, f32[20,16,128]{2,1,0:T(8,128)S(1)}, f32[20,16,128]{2,1,0:T(8,128)S(1)}, f32[20,16,128]{2,1,0:T(8,128)S(1)}) custom-call(s32[360]{0:T(512)S(1)} %get-tuple-element.47.rank_of, s32[360]{0:T(512)S(1)} %get-tuple-element.48.col_of, s32[360]{0:T(512)S(1)} %get-tuple-element.49.tile_of, ...), custom_call_target="tpu_custom_call" | custom-call | tf_op jit(solution)/shard_map/pallas_call | solution.py:321
  18.5 1.8 %collective-permute-start.7 = (f32[20,16,128]{2,1,0:T(8,128)S(1)}, f32[20,16,128]{2,1,0:T(8,128)S(1)}, u32[]{:S(2)}, u32[]{:S(2)}) collective-permute-start(f32[20,16,128]{2,1,0:T(8,128)S(1)} %get-tuple-element.60), channel_id=1, source_target_pairs={{0,4},{4,0},{8,12},{12,8},{16,20},{20,16},{24,28},{28,24},{1,5},{5... | collective-permute-start | bytes 491528 | tf_op jit(solution)/shard_map/ppermute | solution.py:263
  20.6 1.7 %collective-permute-start.11 = (f32[20,16,128]{2,1,0:T(8,128)S(1)}, f32[20,16,128]{2,1,0:T(8,128)S(1)}, u32[]{:S(2)}, u32[]{:S(2)}) collective-permute-start(f32[20,16,128]{2,1,0:T(8,128)S(1)} %get-tuple-element.64), channel_id=1, source_target_pairs={{0,4},{4,0},{8,12},{12,8},{16,20},{20,16},{24,28},{28,24},{1,5},{5... | collective-permute-start | bytes 491528 | tf_op jit(solution)/shard_map/ppermute | solution.py:263
  22.6 2.5 %shard_map.57 = (f32[20,16,128]{2,1,0:T(8,128)S(1)}, f32[20,16,128]{2,1,0:T(8,128)S(1)}, f32[20,16,128]{2,1,0:T(8,128)S(1)}, f32[20,16,128]{2,1,0:T(8,128)S(1)}) custom-call(s32[360]{0:T(512)S(1)} %get-tuple-element.47.rank_of, s32[360]{0:T(512)S(1)} %get-tuple-element.48.col_of, s32[360]{0:T(512)S(1)} %get-tuple-element.49.tile_of, ...), custom_call_target="tpu_custom_call" | custom-call | tf_op jit(solution)/shard_map/pallas_call | solution.py:321
  25.6 3.9 %collective-permute-start.8 = (f32[20,16,128]{2,1,0:T(8,128)S(1)}, f32[20,16,128]{2,1,0:T(8,128)S(1)}, u32[]{:S(2)}, u32[]{:S(2)}) collective-permute-start(f32[20,16,128]{2,1,0:T(8,128)S(1)} %shard_map.59), channel_id=1, source_target_pairs={{0,24},{4,28},{8,16},{12,20},{16,8},{20,12},{24,0},{28,4},{1,25},{... | collective-permute-start | bytes 491528 | tf_op jit(solution)/shard_map/ppermute | solution.py:263
  29.5 2.5 %collective-permute-start.10 = (f32[20,16,128]{2,1,0:T(8,128)S(1)}, f32[20,16,128]{2,1,0:T(8,128)S(1)}, u32[]{:S(2)}, u32[]{:S(2)}) collective-permute-start(f32[20,16,128]{2,1,0:T(8,128)S(1)} %shard_map.60), channel_id=1, source_target_pairs={{0,16},{4,20},{8,24},{12,28},{16,0},{20,4},{24,8},{28,12},{1,17},{... | collective-permute-start | bytes 491528 | tf_op jit(solution)/shard_map/ppermute | solution.py:263
  32.6 1.9 %collective-permute-start.12 = (f32[20,16,128]{2,1,0:T(8,128)S(1)}, f32[20,16,128]{2,1,0:T(8,128)S(1)}, u32[]{:S(2)}, u32[]{:S(2)}) collective-permute-start(f32[20,16,128]{2,1,0:T(8,128)S(1)} %shard_map.61), channel_id=1, source_target_pairs={{0,8},{4,12},{8,0},{12,4},{16,24},{20,28},{24,16},{28,20},{1,9},{5... | collective-permute-start | bytes 491528 | tf_op jit(solution)/shard_map/ppermute | solution.py:263
  35.7 7.1 %collective-permute-done.10.refs_3_ = f32[20,16,128]{2,1,0:T(8,128)S(1)} collective-permute-done((f32[20,16,128]{2,1,0:T(8,128)S(1)}, f32[20,16,128]{2,1,0:T(8,128)S(1)}, u32[]{:S(2)}, u32[]{:S(2)}) %collective-permute-start.10) | collective-permute-done | bytes 163872 | tf_op jit(solution)/shard_map/ppermute | solution.py:263
  43.0 3.2 %collective-permute-start.15 = (f32[20,16,128]{2,1,0:T(8,128)S(1)}, f32[20,16,128]{2,1,0:T(8,128)S(1)}, u32[]{:S(2)}, u32[]{:S(2)}) collective-permute-start(f32[20,16,128]{2,1,0:T(8,128)S(1)} %shard_map.62.refs_0_), channel_id=1, source_target_pairs={{0,16},{4,20},{8,24},{12,28},{16,0},{20,4},{24,8},{28,12},{1,17},{... | collective-permute-start | bytes 491528 | tf_op jit(solution)/shard_map/ppermute | solution.py:263
  46.2 1.5 %collective-permute-start.18 = (f32[20,16,128]{2,1,0:T(8,128)S(1)}, f32[20,16,128]{2,1,0:T(8,128)S(1)}, u32[]{:S(2)}, u32[]{:S(2)}) collective-permute-start(f32[20,16,128]{2,1,0:T(8,128)S(1)} %shard_map.62.refs_0_), channel_id=1, source_target_pairs={{0,4},{4,0},{8,12},{12,8},{16,20},{20,16},{24,28},{28,24},{1,5},{5... | collective-permute-start | bytes 491528 | tf_op jit(solution)/shard_map/ppermute | solution.py:263
  47.7 3.4 %collective-permute-done.13.refs_1_ = f32[20,16,128]{2,1,0:T(8,128)S(1)} collective-permute-done((f32[20,16,128]{2,1,0:T(8,128)S(1)}, f32[20,16,128]{2,1,0:T(8,128)S(1)}, u32[]{:S(2)}, u32[]{:S(2)}) %collective-permute-start.13) | collective-permute-done | bytes 163872 | tf_op jit(solution)/shard_map/ppermute | solution.py:263
  51.0 1.5 %collective-permute-start.14 = (f32[20,16,128]{2,1,0:T(8,128)S(1)}, f32[20,16,128]{2,1,0:T(8,128)S(1)}, u32[]{:S(2)}, u32[]{:S(2)}) collective-permute-start(f32[20,16,128]{2,1,0:T(8,128)S(1)} %collective-permute-done.13.refs_1_), channel_id=1, source_target_pairs={{0,4},{4,0},{8,12},{12,8},{16,20},{20,16},{24,28},{28,24},{1,5},{5... | collective-permute-start | bytes 491528 | tf_op jit(solution)/shard_map/ppermute | solution.py:263
  52.8 1.6 %collective-permute-start.16 = (f32[20,16,128]{2,1,0:T(8,128)S(1)}, f32[20,16,128]{2,1,0:T(8,128)S(1)}, u32[]{:S(2)}, u32[]{:S(2)}) collective-permute-start(f32[20,16,128]{2,1,0:T(8,128)S(1)} %collective-permute-done.15.refs_2_), channel_id=1, source_target_pairs={{0,4},{4,0},{8,12},{12,8},{16,20},{20,16},{24,28},{28,24},{1,5},{5... | collective-permute-start | bytes 491528 | tf_op jit(solution)/shard_map/ppermute | solution.py:263
  54.3 1.9 %collective-permute-start.17 = (f32[20,16,128]{2,1,0:T(8,128)S(1)}, f32[20,16,128]{2,1,0:T(8,128)S(1)}, u32[]{:S(2)}, u32[]{:S(2)}) collective-permute-start(f32[20,16,128]{2,1,0:T(8,128)S(1)} %shard_map.62.refs_0_), channel_id=1, source_target_pairs={{0,24},{4,28},{8,16},{12,20},{16,8},{20,12},{24,0},{28,4},{1,25},{... | collective-permute-start | bytes 491528 | tf_op jit(solution)/shard_map/ppermute | solution.py:263
  56.3 3.5 %shard_map.64 = (f32[8,64,128]{2,1,0:T(8,128)S(1)}, f32[8,64,128]{2,1,0:T(8,128)S(1)}, f32[8,64,128]{2,1,0:T(8,128)S(1)}, f32[8,16,128]{2,1,0:T(8,128)S(1)}, f32...) custom-call(s32[360]{0:T(512)S(1)} %get-tuple-element.47.rank_of, ...), custom_call_target="tpu_custom_call" | custom-call | tf_op jit(solution)/shard_map/pallas_call | solution.py:334
  62.0 2.4 %collective-permute-start.27 = (f32[8,64,128]{2,1,0:T(8,128)S(1)}, f32[8,64,128]{2,1,0:T(8,128)S(1)}, u32[]{:S(2)}, u32[]{:S(2)}) collective-permute-start(f32[8,64,128]{2,1,0:T(8,128)S(1)} %maximum_add_fusion), channel_id=1, source_target_pairs={{0,2},{1,3},{2,0},{3,1},{4,6},{5,7},{6,4},{7,5},{8,10},{9,11},{10,... | collective-permute-start | bytes 786440 | tf_op jit(solution)/shard_map/ppermute | solution.py:263
  64.4 3.0 %shard_map.63 = (f32[8,48,128]{2,1,0:T(8,128)S(1)}, f32[8,48,128]{2,1,0:T(8,128)S(1)}, f32[8,48,128]{2,1,0:T(8,128)S(1)}, f32[8,48,128]{2,1,0:T(8,128)S(1)}) custom-call(s32[360]{0:T(512)S(1)} %get-tuple-element.47.rank_of, s32[360]{0:T(512)S(1)} %get-tuple-element.48.col_of, s32[360]{0:T(512)S(1)} %get-tuple-element.49.tile_of, ...), custom_call_target="tpu_custom_call" | custom-call | tf_op jit(solution)/shard_map/pallas_call | solution.py:334
  69.1 2.0 %collective-permute-start.22 = (f32[8,48,128]{2,1,0:T(8,128)S(1)}, f32[8,48,128]{2,1,0:T(8,128)S(1)}, u32[]{:S(2)}, u32[]{:S(2)}) collective-permute-start(f32[8,48,128]{2,1,0:T(8,128)S(1)} %add.37), channel_id=1, source_target_pairs={{0,2},{1,3},{2,0},{3,1},{4,6},{5,7},{6,4},{7,5},{8,10},{9,11},{10,... | collective-permute-start | bytes 589832 | tf_op jit(solution)/shard_map/ppermute | solution.py:263
  71.2 2.3 %shard_map.65 = (f32[8,16,128]{2,1,0:T(8,128)S(1)}, f32[8,16,128]{2,1,0:T(8,128)S(1)}, f32[8,16,128]{2,1,0:T(8,128)S(1)}, f32[8,16,128]{2,1,0:T(8,128)S(1)}) custom-call(s32[360]{0:T(512)S(1)} %get-tuple-element.47.rank_of, s32[360]{0:T(512)S(1)} %get-tuple-element.48.col_of, s32[360]{0:T(512)S(1)} %get-tuple-element.49.tile_of, ...), custom_call_target="tpu_custom_call" | custom-call | tf_op jit(solution)/shard_map/pallas_call | solution.py:334
  74.8 2.1 %collective-permute-start.30 = (f32[8,16,128]{2,1,0:T(8,128)S(1)}, f32[8,16,128]{2,1,0:T(8,128)S(1)}, u32[]{:S(2)}, u32[]{:S(2)}) collective-permute-start(f32[8,16,128]{2,1,0:T(8,128)S(1)} %add.40), channel_id=1, source_target_pairs={{0,2},{1,3},{2,0},{3,1},{4,6},{5,7},{6,4},{7,5},{8,10},{9,11},{10,... | collective-permute-start | bytes 196616 | tf_op jit(solution)/shard_map/ppermute | solution.py:263
  (63 shorter events, 14.4 us)
Async XLA Ops:
  1.1 10.2 %collective-permute-start.4 = (f32[8,64,128]{2,1,0:T(8,128)S(1)}, f32[8,64,128]{2,1,0:T(8,128)S(1)}, u32[]{:S(2)}, u32[]{:S(2)}) collective-permute-start(f32[8,64,128]{2,1,0:T(8,128)S(1)} %get-tuple-element.89.refs_0_), channel_id=1, source_target_pairs={{0,2},{1,3},{2,0},{3,1},{4,6},{5,7},{6,4},{7,5},{8,10},{9,11},{10,... | collective-permute-start | bytes 786440 | tf_op jit(solution)/shard_map/ppermute | solution.py:263
  4.1 7.3 %collective-permute-start.1 = (f32[8,64,128]{2,1,0:T(8,128)S(1)}, f32[8,64,128]{2,1,0:T(8,128)S(1)}, u32[]{:S(2)}, u32[]{:S(2)}) collective-permute-start(f32[8,64,128]{2,1,0:T(8,128)S(1)} %get-tuple-element.89.refs_0_), channel_id=1, source_target_pairs={{0,1},{1,0},{2,3},{3,2},{4,5},{5,4},{6,7},{7,6},{8,9},{9,8},{10,11... | collective-permute-start | bytes 786440 | tf_op jit(solution)/shard_map/ppermute | solution.py:263
  4.1 11.9 %collective-permute-start = (f32[8,64,128]{2,1,0:T(8,128)S(1)}, f32[8,64,128]{2,1,0:T(8,128)S(1)}, u32[]{:S(2)}, u32[]{:S(2)}) collective-permute-start(f32[8,64,128]{2,1,0:T(8,128)S(1)} %get-tuple-element.90.refs_2_), channel_id=1, source_target_pairs={{0,2},{1,3},{2,0},{3,1},{4,6},{5,7},{6,4},{7,5},{8,10},{9,11},{10,... | collective-permute-start | bytes 786440 | tf_op jit(solution)/shard_map/ppermute | solution.py:263
  4.3 7.2 %collective-permute-start.2 = (f32[8,64,128]{2,1,0:T(8,128)S(1)}, f32[8,64,128]{2,1,0:T(8,128)S(1)}, u32[]{:S(2)}, u32[]{:S(2)}) collective-permute-start(f32[8,64,128]{2,1,0:T(8,128)S(1)} %get-tuple-element.90.refs_2_), channel_id=1, source_target_pairs={{0,1},{1,0},{2,3},{3,2},{4,5},{5,4},{6,7},{7,6},{8,9},{9,8},{10,11... | collective-permute-start | bytes 786440 | tf_op jit(solution)/shard_map/ppermute | solution.py:263
  11.2 4.8 %collective-permute-start.5 = (f32[8,64,128]{2,1,0:T(8,128)S(1)}, f32[8,64,128]{2,1,0:T(8,128)S(1)}, u32[]{:S(2)}, u32[]{:S(2)}) collective-permute-start(f32[8,64,128]{2,1,0:T(8,128)S(1)} %collective-permute-done.4.refs_0_), channel_id=1, source_target_pairs={{0,1},{1,0},{2,3},{3,2},{4,5},{5,4},{6,7},{7,6},{8,9},{9,8},{10,11... | collective-permute-start | bytes 786440 | tf_op jit(solution)/shard_map/ppermute | solution.py:263
  16.0 6.6 %collective-permute-start.3 = (f32[8,64,128]{2,1,0:T(8,128)S(1)}, f32[8,64,128]{2,1,0:T(8,128)S(1)}, u32[]{:S(2)}, u32[]{:S(2)}) collective-permute-start(f32[8,64,128]{2,1,0:T(8,128)S(1)} %collective-permute-done.refs_0_), channel_id=1, source_target_pairs={{0,1},{1,0},{2,3},{3,2},{4,5},{5,4},{6,7},{7,6},{8,9},{9,8},{10,11... | collective-permute-start | bytes 786440 | tf_op jit(solution)/shard_map/ppermute | solution.py:263
  18.5 7.1 %collective-permute-start.7 = (f32[20,16,128]{2,1,0:T(8,128)S(1)}, f32[20,16,128]{2,1,0:T(8,128)S(1)}, u32[]{:S(2)}, u32[]{:S(2)}) collective-permute-start(f32[20,16,128]{2,1,0:T(8,128)S(1)} %get-tuple-element.60), channel_id=1, source_target_pairs={{0,4},{4,0},{8,12},{12,8},{16,20},{20,16},{24,28},{28,24},{1,5},{5... | collective-permute-start | bytes 491528 | tf_op jit(solution)/shard_map/ppermute | solution.py:263
  20.3 9.2 %collective-permute-start.9 = (f32[20,16,128]{2,1,0:T(8,128)S(1)}, f32[20,16,128]{2,1,0:T(8,128)S(1)}, u32[]{:S(2)}, u32[]{:S(2)}) collective-permute-start(f32[20,16,128]{2,1,0:T(8,128)S(1)} %get-tuple-element.62), channel_id=1, source_target_pairs={{0,4},{4,0},{8,12},{12,8},{16,20},{20,16},{24,28},{28,24},{1,5},{5... | collective-permute-start | bytes 491528 | tf_op jit(solution)/shard_map/ppermute | solution.py:263
  20.6 12.0 %collective-permute-start.11 = (f32[20,16,128]{2,1,0:T(8,128)S(1)}, f32[20,16,128]{2,1,0:T(8,128)S(1)}, u32[]{:S(2)}, u32[]{:S(2)}) collective-permute-start(f32[20,16,128]{2,1,0:T(8,128)S(1)} %get-tuple-element.64), channel_id=1, source_target_pairs={{0,4},{4,0},{8,12},{12,8},{16,20},{20,16},{24,28},{28,24},{1,5},{5... | collective-permute-start | bytes 491528 | tf_op jit(solution)/shard_map/ppermute | solution.py:263
  22.3 13.4 %collective-permute-start.6 = (f32[20,16,128]{2,1,0:T(8,128)S(1)}, f32[20,16,128]{2,1,0:T(8,128)S(1)}, u32[]{:S(2)}, u32[]{:S(2)}) collective-permute-start(f32[20,16,128]{2,1,0:T(8,128)S(1)} %get-tuple-element.58), channel_id=1, source_target_pairs={{0,4},{4,0},{8,12},{12,8},{16,20},{20,16},{24,28},{28,24},{1,5},{5... | collective-permute-start | bytes 491528 | tf_op jit(solution)/shard_map/ppermute | solution.py:263
  25.6 10.1 %collective-permute-start.8 = (f32[20,16,128]{2,1,0:T(8,128)S(1)}, f32[20,16,128]{2,1,0:T(8,128)S(1)}, u32[]{:S(2)}, u32[]{:S(2)}) collective-permute-start(f32[20,16,128]{2,1,0:T(8,128)S(1)} %shard_map.59), channel_id=1, source_target_pairs={{0,24},{4,28},{8,16},{12,20},{16,8},{20,12},{24,0},{28,4},{1,25},{... | collective-permute-start | bytes 491528 | tf_op jit(solution)/shard_map/ppermute | solution.py:263
  29.5 13.4 %collective-permute-start.10 = (f32[20,16,128]{2,1,0:T(8,128)S(1)}, f32[20,16,128]{2,1,0:T(8,128)S(1)}, u32[]{:S(2)}, u32[]{:S(2)}) collective-permute-start(f32[20,16,128]{2,1,0:T(8,128)S(1)} %shard_map.60), channel_id=1, source_target_pairs={{0,16},{4,20},{8,24},{12,28},{16,0},{20,4},{24,8},{28,12},{1,17},{... | collective-permute-start | bytes 491528 | tf_op jit(solution)/shard_map/ppermute | solution.py:263
  32.6 10.3 %collective-permute-start.12 = (f32[20,16,128]{2,1,0:T(8,128)S(1)}, f32[20,16,128]{2,1,0:T(8,128)S(1)}, u32[]{:S(2)}, u32[]{:S(2)}) collective-permute-start(f32[20,16,128]{2,1,0:T(8,128)S(1)} %shard_map.61), channel_id=1, source_target_pairs={{0,8},{4,12},{8,0},{12,4},{16,24},{20,28},{24,16},{28,20},{1,9},{5... | collective-permute-start | bytes 491528 | tf_op jit(solution)/shard_map/ppermute | solution.py:263
  43.0 8.1 %collective-permute-start.13 = (f32[20,16,128]{2,1,0:T(8,128)S(1)}, f32[20,16,128]{2,1,0:T(8,128)S(1)}, u32[]{:S(2)}, u32[]{:S(2)}) collective-permute-start(f32[20,16,128]{2,1,0:T(8,128)S(1)} %shard_map.62.refs_0_), channel_id=1, source_target_pairs={{0,8},{4,12},{8,0},{12,4},{16,24},{20,28},{24,16},{28,20},{1,9},{5... | collective-permute-start | bytes 491528 | tf_op jit(solution)/shard_map/ppermute | solution.py:263
  43.0 9.7 %collective-permute-start.15 = (f32[20,16,128]{2,1,0:T(8,128)S(1)}, f32[20,16,128]{2,1,0:T(8,128)S(1)}, u32[]{:S(2)}, u32[]{:S(2)}) collective-permute-start(f32[20,16,128]{2,1,0:T(8,128)S(1)} %shard_map.62.refs_0_), channel_id=1, source_target_pairs={{0,16},{4,20},{8,24},{12,28},{16,0},{20,4},{24,8},{28,12},{1,17},{... | collective-permute-start | bytes 491528 | tf_op jit(solution)/shard_map/ppermute | solution.py:263
  46.2 10.1 %collective-permute-start.18 = (f32[20,16,128]{2,1,0:T(8,128)S(1)}, f32[20,16,128]{2,1,0:T(8,128)S(1)}, u32[]{:S(2)}, u32[]{:S(2)}) collective-permute-start(f32[20,16,128]{2,1,0:T(8,128)S(1)} %shard_map.62.refs_0_), channel_id=1, source_target_pairs={{0,4},{4,0},{8,12},{12,8},{16,20},{20,16},{24,28},{28,24},{1,5},{5... | collective-permute-start | bytes 491528 | tf_op jit(solution)/shard_map/ppermute | solution.py:263
  51.0 8.7 %collective-permute-start.14 = (f32[20,16,128]{2,1,0:T(8,128)S(1)}, f32[20,16,128]{2,1,0:T(8,128)S(1)}, u32[]{:S(2)}, u32[]{:S(2)}) collective-permute-start(f32[20,16,128]{2,1,0:T(8,128)S(1)} %collective-permute-done.13.refs_1_), channel_id=1, source_target_pairs={{0,4},{4,0},{8,12},{12,8},{16,20},{20,16},{24,28},{28,24},{1,5},{5... | collective-permute-start | bytes 491528 | tf_op jit(solution)/shard_map/ppermute | solution.py:263
  52.8 7.0 %collective-permute-start.16 = (f32[20,16,128]{2,1,0:T(8,128)S(1)}, f32[20,16,128]{2,1,0:T(8,128)S(1)}, u32[]{:S(2)}, u32[]{:S(2)}) collective-permute-start(f32[20,16,128]{2,1,0:T(8,128)S(1)} %collective-permute-done.15.refs_2_), channel_id=1, source_target_pairs={{0,4},{4,0},{8,12},{12,8},{16,20},{20,16},{24,28},{28,24},{1,5},{5... | collective-permute-start | bytes 491528 | tf_op jit(solution)/shard_map/ppermute | solution.py:263
  54.3 7.1 %collective-permute-start.17 = (f32[20,16,128]{2,1,0:T(8,128)S(1)}, f32[20,16,128]{2,1,0:T(8,128)S(1)}, u32[]{:S(2)}, u32[]{:S(2)}) collective-permute-start(f32[20,16,128]{2,1,0:T(8,128)S(1)} %shard_map.62.refs_0_), channel_id=1, source_target_pairs={{0,24},{4,28},{8,16},{12,20},{16,8},{20,12},{24,0},{28,4},{1,25},{... | collective-permute-start | bytes 491528 | tf_op jit(solution)/shard_map/ppermute | solution.py:263
  61.5 5.9 %collective-permute-start.19 = (f32[20,16,128]{2,1,0:T(8,128)S(1)}, f32[20,16,128]{2,1,0:T(8,128)S(1)}, u32[]{:S(2)}, u32[]{:S(2)}) collective-permute-start(f32[20,16,128]{2,1,0:T(8,128)S(1)} %collective-permute-done.17.refs_2_), channel_id=1, source_target_pairs={{0,4},{4,0},{8,12},{12,8},{16,20},{20,16},{24,28},{28,24},{1,5},{5... | collective-permute-start | bytes 491528 | tf_op jit(solution)/shard_map/ppermute | solution.py:263
  62.0 9.2 %collective-permute-start.27 = (f32[8,64,128]{2,1,0:T(8,128)S(1)}, f32[8,64,128]{2,1,0:T(8,128)S(1)}, u32[]{:S(2)}, u32[]{:S(2)}) collective-permute-start(f32[8,64,128]{2,1,0:T(8,128)S(1)} %maximum_add_fusion), channel_id=1, source_target_pairs={{0,2},{1,3},{2,0},{3,1},{4,6},{5,7},{6,4},{7,5},{8,10},{9,11},{10,... | collective-permute-start | bytes 786440 | tf_op jit(solution)/shard_map/ppermute | solution.py:263
  68.0 9.0 %collective-permute-start.31 = (f32[8,64,128]{2,1,0:T(8,128)S(1)}, f32[8,64,128]{2,1,0:T(8,128)S(1)}, u32[]{:S(2)}, u32[]{:S(2)}) collective-permute-start(f32[8,64,128]{2,1,0:T(8,128)S(1)} %get-tuple-element.88), channel_id=1, source_target_pairs={{0,1},{1,0},{2,3},{3,2},{4,5},{5,4},{6,7},{7,6},{8,9},{9,8},{10,11... | collective-permute-start | bytes 786440 | tf_op jit(solution)/shard_map/ppermute | solution.py:263
  68.1 10.3 %collective-permute-start.20 = (f32[8,48,128]{2,1,0:T(8,128)S(1)}, f32[8,48,128]{2,1,0:T(8,128)S(1)}, u32[]{:S(2)}, u32[]{:S(2)}) collective-permute-start(f32[8,48,128]{2,1,0:T(8,128)S(1)} %get-tuple-element.70), channel_id=1, source_target_pairs={{0,1},{1,0},{2,3},{3,2},{4,5},{5,4},{6,7},{7,6},{8,9},{9,8},{10,11... | collective-permute-start | bytes 589832 | tf_op jit(solution)/shard_map/ppermute | solution.py:263
  69.1 10.3 %collective-permute-start.22 = (f32[8,48,128]{2,1,0:T(8,128)S(1)}, f32[8,48,128]{2,1,0:T(8,128)S(1)}, u32[]{:S(2)}, u32[]{:S(2)}) collective-permute-start(f32[8,48,128]{2,1,0:T(8,128)S(1)} %add.37), channel_id=1, source_target_pairs={{0,2},{1,3},{2,0},{3,1},{4,6},{5,7},{6,4},{7,5},{8,10},{9,11},{10,... | collective-permute-start | bytes 589832 | tf_op jit(solution)/shard_map/ppermute | solution.py:263
  (9 other events, 34.7 us)
